TPU v7x, 32 devices: a whole 2x2x4 slice. The times are simulated.
32 devices in a mesh: dp: 16 (over z, y, core), fsdp: 2 (over x).
Axes of the slice: x: 2, y: 2, z: 4, core: 2. Of those that a mesh axis runs over, the one named last changes fastest.
Arguments:
- states: float32 [2, 4096, 1536], P('fsdp', 'dp'), may hold values from -50 to 50
- cotangent: float32 [2, 4096, 1536], P('fsdp', 'dp'), may hold values from -6 to 6
- segment_ids: int32 [2, 4096], P('fsdp'), may hold values from -1 to 1, as said below
- frame_ids: int32 [2, 4096], P('fsdp', 'dp'), may hold values from 0 to 15, as said below
- condition: float32 [2, 2, 1536], P('fsdp'), may hold values from -6 to 6
- context: bfloat16 [2, 512, 4096], P('fsdp', 'dp'), may hold values from -6 to 6
- w_modulate: bfloat16 [1536, 6144], P('fsdp'), may hold values from -0.15625 to 0.15625
- w_qkv: bfloat16 [1536, 4608], P('fsdp'), may hold values from -0.15625 to 0.15625
- w_text_kv: bfloat16 [4096, 3072], P('fsdp'), may hold values from -0.09375 to 0.09375
- w_out: bfloat16 [1536, 1536], P('fsdp'), may hold values from -0.15625 to 0.15625
- w_gate_up: bfloat16 [2, 1536, 4096], P(None, None, 'fsdp'), may hold values from -0.15625 to 0.15625
- w_down: bfloat16 [4096, 1536], P('fsdp'), may hold values from -0.09375 to 0.09375
- gain_attn_in: float32 [1536], replicated, may hold values from 0.1 to 1.9
- gain_attn_out: float32 [1536], replicated, may hold values from 0.1 to 1.9
- gain_ffn_in: float32 [1536], replicated, may hold values from 0.1 to 1.9
- gain_ffn_out: float32 [1536], replicated, may hold values from 0.1 to 1.9
- gain_query: float32 [64], replicated, may hold values from 0.1 to 1.9
- gain_key: float32 [64], replicated, may hold values from 0.1 to 1.9
- gain_text_key: float32 [64], replicated, may hold values from 0.1 to 1.9
- cross_gate: float32 [24], replicated, may hold values from -1.5 to 1.5
Outputs:
- output: float32 [2, 4096, 1536], P('fsdp', 'dp')
- grad_states: float32 [2, 4096, 1536], P('fsdp', 'dp')
- grad_w_modulate: float32 [1536, 6144], P('fsdp', 'dp')
- grad_w_qkv: float32 [1536, 4608], P('fsdp', 'dp')
- grad_w_text_kv: float32 [4096, 3072], P('fsdp', 'dp')
- grad_w_out: float32 [1536, 1536], P('fsdp', 'dp')
- grad_w_gate_up: float32 [2, 1536, 4096], P(None, 'dp', 'fsdp')
- grad_w_down: float32 [4096, 1536], P('fsdp', 'dp')
- grad_gain_attn_in: float32 [1536], replicated
- grad_gain_attn_out: float32 [1536], replicated
- grad_gain_ffn_in: float32 [1536], replicated
- grad_gain_ffn_out: float32 [1536], replicated
- grad_gain_query: float32 [64], replicated
- grad_gain_key: float32 [64], replicated
- grad_gain_text_key: float32 [64], replicated
- grad_cross_gate: float32 [24], replicated
Inputs may be any that keep to these rules, and one draw needn't show every extreme that they name: `segment_ids`: each stream has 2 clips; clip c covers between 4 and 16 whole frames of 128 tokens that start at multiples of 128, clip 0 exactly 16, with one of its frames first and one last in the stream; -1 marks padding frames. `frame_ids`: the frames of a clip carry the numbers 0 up to its frame count minus one, one frame each, in any order along the stream; padding carries 0.
All inputs are finite; a program needn't handle non-finite values.
Results may differ from a plain program's by a relative error of at most 0.025.
Values may be sent and summed in bfloat16 or wider, within the bound.
No kernel may reach another device: no remote copies, remote signals or barrier semaphores. Data moves between devices by JAX's collectives and lax.ppermute only.
A program may use at most 448 MiB of HBM per device.

v0:
```python
import jax
import jax.numpy as jnp
from jax import lax
from jax.sharding import PartitionSpec as P

HD = 64
CTX = 256
FRAME_TOK = 128
PW = 16


EPSILON = 1e-06
HIGHEST = lax.Precision.HIGHEST
NEG_LARGE = -1e30


def rms_norm(values, gain):
    return values * lax.rsqrt(jnp.mean(values * values, axis=-1, keepdims=True) + EPSILON) * gain


def frequencies(count):
    return 10000.0 ** (-jnp.arange(count, dtype=jnp.float32) / count)


def rope_tables(frames_row, first_row, row_count):
    place = first_row + jnp.arange(row_count)
    inner = place % FRAME_TOK
    row_pos = (inner // PW).astype(jnp.float32)
    col_pos = (inner % PW).astype(jnp.float32)
    frame_pos = frames_row.astype(jnp.float32)
    half_pairs = HD // 2
    frame_pairs = HD // 8
    row_pairs = (half_pairs - frame_pairs) // 2
    col_pairs = half_pairs - frame_pairs - row_pairs
    angles = jnp.concatenate(
        [
            frame_pos[:, None] * frequencies(frame_pairs)[None, :],
            row_pos[:, None] * frequencies(row_pairs)[None, :],
            col_pos[:, None] * frequencies(col_pairs)[None, :],
        ],
        axis=1,
    )
    return (jnp.cos(angles), jnp.sin(angles))


def rotate(values, cosine, sine):
    pairs = values.reshape(values.shape[0], values.shape[1], -1, 2)
    first_part = pairs[..., 0]
    second_part = pairs[..., 1]
    cos_heads = cosine[:, None, :]
    sin_heads = sine[:, None, :]
    turned = jnp.stack(
        [
            first_part * cos_heads - second_part * sin_heads,
            first_part * sin_heads + second_part * cos_heads,
        ],
        axis=-1,
    )
    return turned.reshape(values.shape)


def pre_norm(values, gain, shift_scale):
    return rms_norm(values, gain) * (1.0 + shift_scale)


def gated_norm(values, gain, gate_values):
    return jnp.tanh(gate_values) * rms_norm(values, gain)


def swiglu(gate_part, up_part):
    return jax.nn.silu(gate_part) * up_part


def full_weight(shard, shard_dim):
    return lax.all_gather(shard, "fsdp", axis=shard_dim, tiled=True)


def sum_rows(term, row_dim):
    return lax.psum_scatter(
        term.astype(jnp.bfloat16), "dp", scatter_dimension=row_dim, tiled=True
    ).astype(jnp.float32)


def reduce_grad(term, shard_dim, row_dim):
    return sum_rows(
        lax.psum_scatter(
            term.astype(jnp.bfloat16), "fsdp", scatter_dimension=shard_dim, tiled=True
        ).astype(jnp.float32),
        row_dim,
    )


def per_device(
    states,
    cotangent,
    segment_ids,
    frame_ids,
    condition,
    context,
    w_modulate,
    w_qkv,
    w_text_kv,
    w_out,
    w_gate_up,
    w_down,
    gain_attn_in,
    gain_attn_out,
    gain_ffn_in,
    gain_ffn_out,
    gain_query,
    gain_key,
    gain_text_key,
    cross_gate,
):
    rows_in = states[0]
    tokens, model_width = rows_in.shape
    head_count = cross_gate.shape[0]
    head_size = model_width // head_count
    score_scale = head_size ** (-0.5)
    segments = segment_ids[0]
    first_row = lax.axis_index("dp") * tokens
    own_seg = lax.dynamic_slice_in_dim(segments, first_row, tokens)
    clip_count = condition.shape[1]
    text_local = context[0]
    text_rows_dev = text_local.shape[0]
    onehot = (own_seg[:, None] == jnp.arange(clip_count)[None, :]).astype(jnp.float32)
    silu_cond = jax.nn.silu(condition[0]).astype(jnp.bfloat16)
    modulation = jnp.dot(silu_cond, full_weight(w_modulate, 0), preferred_element_type=jnp.float32)
    text_proj = jnp.dot(text_local, full_weight(w_text_kv, 0), preferred_element_type=jnp.float32)
    per_token = jnp.dot(onehot, modulation, precision=HIGHEST)
    scale_attn, gate_attn, scale_ffn, gate_ffn = jnp.split(per_token, 4, axis=1)
    normed = pre_norm(rows_in, gain_attn_in, scale_attn).astype(jnp.bfloat16)
    projected = jnp.dot(normed, full_weight(w_qkv, 0), preferred_element_type=jnp.float32)
    query_raw, key_raw, value_raw = jnp.split(projected, 3, axis=1)
    cosine, sine = rope_tables(frame_ids[0], first_row, tokens)

    def qk_piece(query_in, key_in, gain_q, gain_k):
        query_turned = rotate(
            rms_norm(query_in.reshape(tokens, head_count, head_size), gain_q), cosine, sine
        )
        key_turned = rotate(
            rms_norm(key_in.reshape(tokens, head_count, head_size), gain_k), cosine, sine
        )
        return (query_turned, key_turned)

    query_wide, key_wide = qk_piece(query_raw, key_raw, gain_query, gain_key)
    query = query_wide.astype(jnp.bfloat16)
    key_heads = key_wide.astype(jnp.bfloat16)
    key_flat = key_heads.reshape(tokens, model_width)
    value_flat = value_raw.astype(jnp.bfloat16)
    value_heads = value_flat.reshape(tokens, head_count, head_size)
    start_state = (
        jnp.full((head_count, tokens), NEG_LARGE, jnp.float32),
        jnp.zeros((head_count, tokens), jnp.float32),
        jnp.zeros((head_count, tokens, head_size), jnp.float32),
    )
    piece_keys = lax.all_gather(key_flat, "dp", axis=0, tiled=True)
    piece_values = lax.all_gather(value_flat, "dp", axis=0, tiled=True)
    piece_rows = piece_keys.shape[0]

    def attend_block(inner_state, block_index):
        row_best, row_total, accumulated = inner_state
        offset = block_index * tokens
        block_keys = lax.dynamic_slice_in_dim(piece_keys, offset, tokens).reshape(
            tokens, head_count, head_size
        )
        block_values = lax.dynamic_slice_in_dim(piece_values, offset, tokens).reshape(
            tokens, head_count, head_size
        )
        block_seg = lax.dynamic_slice_in_dim(segments, offset, tokens)
        allowed = (own_seg[:, None] == block_seg[None, :])[None]
        scores = (
            jnp.einsum("qhd,khd->hqk", query, block_keys, preferred_element_type=jnp.float32)
            * score_scale
        )
        scores = jnp.where(allowed, scores, NEG_LARGE)
        new_best = jnp.maximum(row_best, jnp.max(scores, axis=-1))
        weights = jnp.where(allowed, jnp.exp(scores - new_best[..., None]), 0.0)
        factor = jnp.exp(row_best - new_best)
        row_total = row_total * factor + jnp.sum(weights, axis=-1)
        accumulated = accumulated * factor[..., None] + jnp.einsum(
            "hqk,khd->hqd", weights, block_values.astype(jnp.float32)
        )
        return ((new_best, row_total, accumulated), None)

    state_out, _ = lax.scan(attend_block, start_state, jnp.arange(piece_rows // tokens))
    row_best, row_total, accumulated = state_out
    self_out = jnp.transpose(accumulated / row_total[..., None], (1, 0, 2))
    log_total = row_best + jnp.log(row_total)

    def text_norm(values, gain):
        return rms_norm(values.reshape(text_rows_dev, head_count, head_size), gain)

    text_key_own = text_norm(text_proj[:, :model_width], gain_text_key).astype(jnp.bfloat16)
    text_value_own = text_proj[:, model_width:].astype(jnp.bfloat16)
    text_keys, text_values = (
        lax.all_gather(text_key_own.reshape(text_rows_dev, model_width), "dp", axis=0, tiled=True),
        lax.all_gather(text_value_own, "dp", axis=0, tiled=True),
    )
    text_rows = text_keys.shape[0]
    text_keys = text_keys.reshape(text_rows, head_count, head_size)
    text_values = text_values.reshape(text_rows, head_count, head_size)
    text_allowed = (jnp.maximum(own_seg, 0)[:, None] == (jnp.arange(text_rows) // CTX)[None, :])[
        None
    ]
    text_scores = (
        jnp.einsum("qhd,khd->hqk", query, text_keys, preferred_element_type=jnp.float32)
        * score_scale
    )
    text_scores = jnp.where(text_allowed, text_scores, NEG_LARGE)
    text_weights = jax.nn.softmax(text_scores, axis=-1)
    text_out = jnp.einsum("hqk,khd->qhd", text_weights, text_values.astype(jnp.float32))
    tanh_gate = jnp.tanh(cross_gate)
    mixed = (self_out + tanh_gate[None, :, None] * text_out).reshape(tokens, model_width)
    mixed_low = mixed.astype(jnp.bfloat16)
    mixed_out = jnp.dot(mixed_low, full_weight(w_out, 0), preferred_element_type=jnp.float32)
    after_attn = rows_in + gated_norm(mixed_out, gain_attn_out, gate_attn)
    ffn_in = pre_norm(after_attn, gain_ffn_in, scale_ffn).astype(jnp.bfloat16)
    gate_up = jnp.einsum(
        "ld,cdf->clf", ffn_in, full_weight(w_gate_up, 2), preferred_element_type=jnp.float32
    )
    hidden = swiglu(gate_up[0], gate_up[1]).astype(jnp.bfloat16)
    ffn_out = jnp.dot(hidden, full_weight(w_down, 0), preferred_element_type=jnp.float32)
    output = after_attn + gated_norm(ffn_out, gain_ffn_out, gate_ffn)
    grad_output = cotangent[0]
    _, pullback = jax.vjp(gated_norm, ffn_out, gain_ffn_out, gate_ffn)
    grad_ffn_out, grad_gain_ffn_out, grad_gate_ffn = pullback(grad_output)
    grad_ffn_low = grad_ffn_out.astype(jnp.bfloat16)
    gate_up_full = full_weight(w_gate_up, 2)
    down_full = full_weight(w_down, 0)
    gate_up = jnp.einsum("ld,cdf->clf", ffn_in, gate_up_full, preferred_element_type=jnp.float32)
    activated, pullback = jax.vjp(swiglu, gate_up[0], gate_up[1])
    hidden = activated.astype(jnp.bfloat16)
    grad_hidden = jnp.einsum(
        "ld,fd->lf", grad_ffn_low, down_full, preferred_element_type=jnp.float32
    )
    grad_w_down = reduce_grad(
        jnp.einsum("lf,ld->fd", hidden, grad_ffn_low, preferred_element_type=jnp.float32), 0, 1
    )
    grad_gate, grad_up = pullback(grad_hidden)
    grad_gate_up = jnp.stack([grad_gate, grad_up]).astype(jnp.bfloat16)
    grad_w_gate_up = reduce_grad(
        jnp.einsum("ld,clf->cdf", ffn_in, grad_gate_up, preferred_element_type=jnp.float32), 2, 1
    )
    grad_ffn_in = jnp.einsum(
        "clf,cdf->ld", grad_gate_up, gate_up_full, preferred_element_type=jnp.float32
    )
    _, pullback = jax.vjp(pre_norm, after_attn, gain_ffn_in, scale_ffn)
    grad_after, grad_gain_ffn_in, grad_scale_ffn = pullback(grad_ffn_in)
    grad_after = grad_after + grad_output
    _, pullback = jax.vjp(gated_norm, mixed_out, gain_attn_out, gate_attn)
    grad_mixed_out, grad_gain_attn_out, grad_gate_attn = pullback(grad_after)
    grad_mixed_low = grad_mixed_out.astype(jnp.bfloat16)
    grad_mixed = jnp.einsum(
        "le,de->ld", grad_mixed_low, full_weight(w_out, 0), preferred_element_type=jnp.float32
    )
    grad_w_out = reduce_grad(
        jnp.einsum("ld,le->de", mixed_low, grad_mixed_low, preferred_element_type=jnp.float32), 0, 1
    )
    grad_heads = grad_mixed.reshape(tokens, head_count, head_size)
    grad_self = grad_heads.astype(jnp.bfloat16)
    grad_text = (grad_heads * tanh_gate[None, :, None]).astype(jnp.bfloat16)
    grad_gate_term = jnp.sum(grad_heads * text_out, axis=(0, 2)) * (1.0 - tanh_gate * tanh_gate)
    text_grad_weights = jnp.einsum(
        "qhd,khd->hqk", grad_text, text_values, preferred_element_type=jnp.float32
    )
    text_delta = jnp.transpose(jnp.sum(grad_text.astype(jnp.float32) * text_out, axis=-1))
    text_grad_scores = (text_weights * (text_grad_weights - text_delta[..., None])).astype(
        jnp.bfloat16
    )
    grad_query = (
        jnp.einsum("hqk,khd->qhd", text_grad_scores, text_keys, preferred_element_type=jnp.float32)
        * score_scale
    )
    grad_text_key = (
        jnp.einsum("hqk,qhd->khd", text_grad_scores, query, preferred_element_type=jnp.float32)
        * score_scale
    )
    grad_text_value = jnp.einsum("hqk,qhd->khd", text_weights, grad_text.astype(jnp.float32))
    own_text_key, own_text_value = (
        lax.psum_scatter(
            grad_text_key.reshape(text_rows, model_width).astype(jnp.bfloat16),
            "dp",
            scatter_dimension=0,
            tiled=True,
        ).astype(jnp.float32),
        lax.psum_scatter(
            grad_text_value.reshape(text_rows, model_width).astype(jnp.bfloat16),
            "dp",
            scatter_dimension=0,
            tiled=True,
        ).astype(jnp.float32),
    )
    _, pullback = jax.vjp(text_norm, text_proj[:, :model_width], gain_text_key)
    grad_text_raw, grad_gain_text_key = pullback(
        own_text_key.reshape(text_rows_dev, head_count, head_size)
    )
    grad_text_proj = jnp.concatenate([grad_text_raw, own_text_value], axis=1).astype(jnp.bfloat16)
    self_delta = jnp.transpose(jnp.sum(grad_self.astype(jnp.float32) * self_out, axis=-1))
    every_log_total, every_delta = (
        lax.all_gather(log_total, "dp", axis=1, tiled=True),
        lax.all_gather(self_delta, "dp", axis=1, tiled=True),
    )
    query_piece_keys = lax.all_gather(key_flat, "dp", axis=0, tiled=True)
    query_piece_values = lax.all_gather(value_flat, "dp", axis=0, tiled=True)
    piece_rows = query_piece_keys.shape[0]

    def query_grad_block(carried, block_index):
        offset = block_index * tokens
        block_keys = lax.dynamic_slice_in_dim(query_piece_keys, offset, tokens).reshape(
            tokens, head_count, head_size
        )
        block_values = lax.dynamic_slice_in_dim(query_piece_values, offset, tokens).reshape(
            tokens, head_count, head_size
        )
        block_seg = lax.dynamic_slice_in_dim(segments, offset, tokens)
        allowed = (own_seg[:, None] == block_seg[None, :])[None]
        scores = (
            jnp.einsum("qhd,khd->hqk", query, block_keys, preferred_element_type=jnp.float32)
            * score_scale
        )
        weights = jnp.where(
            allowed, jnp.exp(jnp.where(allowed, scores, NEG_LARGE) - log_total[..., None]), 0.0
        )
        grad_weights = jnp.einsum(
            "qhd,khd->hqk", grad_self, block_values, preferred_element_type=jnp.float32
        )
        grad_scores = (weights * (grad_weights - self_delta[..., None])).astype(jnp.bfloat16)
        carried = (
            carried
            + jnp.einsum(
                "hqk,khd->qhd", grad_scores, block_keys, preferred_element_type=jnp.float32
            )
            * score_scale
        )
        return (carried, None)

    grad_out, _ = lax.scan(
        query_grad_block,
        jnp.zeros((tokens, head_count, head_size), jnp.float32),
        jnp.arange(piece_rows // tokens),
    )
    grad_query = grad_query + grad_out
    zero_heads = jnp.zeros((tokens, head_count, head_size), jnp.float32)
    piece_queries = lax.all_gather(query.reshape(tokens, model_width), "dp", axis=0, tiled=True)
    piece_grads = lax.all_gather(grad_self.reshape(tokens, model_width), "dp", axis=0, tiled=True)
    piece_rows = piece_queries.shape[0]

    def key_grad_block(inner_state, block_index):
        grad_key_part, grad_value_part = inner_state
        offset = block_index * tokens
        block_queries = lax.dynamic_slice_in_dim(piece_queries, offset, tokens).reshape(
            tokens, head_count, head_size
        )
        block_grads = lax.dynamic_slice_in_dim(piece_grads, offset, tokens).reshape(
            tokens, head_count, head_size
        )
        block_seg = lax.dynamic_slice_in_dim(segments, offset, tokens)
        block_log = lax.dynamic_slice_in_dim(every_log_total, offset, tokens, axis=1)
        block_delta = lax.dynamic_slice_in_dim(every_delta, offset, tokens, axis=1)
        allowed = (block_seg[:, None] == own_seg[None, :])[None]
        scores = (
            jnp.einsum("qhd,khd->hqk", block_queries, key_heads, preferred_element_type=jnp.float32)
            * score_scale
        )
        weights = jnp.where(
            allowed, jnp.exp(jnp.where(allowed, scores, NEG_LARGE) - block_log[..., None]), 0.0
        )
        grad_value_part = grad_value_part + jnp.einsum(
            "hqk,qhd->khd", weights, block_grads.astype(jnp.float32)
        )
        grad_weights = jnp.einsum(
            "qhd,khd->hqk", block_grads, value_heads, preferred_element_type=jnp.float32
        )
        grad_scores = (weights * (grad_weights - block_delta[..., None])).astype(jnp.bfloat16)
        grad_key_part = (
            grad_key_part
            + jnp.einsum(
                "hqk,qhd->khd", grad_scores, block_queries, preferred_element_type=jnp.float32
            )
            * score_scale
        )
        return ((grad_key_part, grad_value_part), None)

    state_out, _ = lax.scan(
        key_grad_block, (zero_heads, zero_heads), jnp.arange(piece_rows // tokens)
    )
    grad_key, grad_value = state_out
    _, pullback = jax.vjp(qk_piece, query_raw, key_raw, gain_query, gain_key)
    grad_query_raw, grad_key_raw, grad_gain_query, grad_gain_key = pullback((grad_query, grad_key))
    grad_projected = jnp.concatenate(
        [grad_query_raw, grad_key_raw, grad_value.reshape(tokens, model_width)], axis=1
    ).astype(jnp.bfloat16)
    grad_normed = jnp.einsum(
        "le,de->ld", grad_projected, full_weight(w_qkv, 0), preferred_element_type=jnp.float32
    )
    grad_w_qkv = reduce_grad(
        jnp.einsum("ld,le->de", normed, grad_projected, preferred_element_type=jnp.float32), 0, 1
    )
    _, pullback = jax.vjp(pre_norm, rows_in, gain_attn_in, scale_attn)
    grad_rows_in, grad_gain_attn_in, grad_scale_attn = pullback(grad_normed)
    grad_input = grad_rows_in + grad_after
    grad_per_token = jnp.concatenate(
        [grad_scale_attn, grad_gate_attn, grad_scale_ffn, grad_gate_ffn], axis=1
    )
    grad_modulation = jnp.dot(jnp.transpose(onehot), grad_per_token, precision=HIGHEST)
    grad_w_text_kv = reduce_grad(
        jnp.einsum("rc,re->ce", text_local, grad_text_proj, preferred_element_type=jnp.float32),
        0,
        1,
    )
    grad_w_modulate = reduce_grad(
        jnp.dot(jnp.transpose(silu_cond.astype(jnp.float32)), grad_modulation, precision=HIGHEST),
        0,
        1,
    )
    small_sums = lax.psum(
        (
            grad_gain_attn_in,
            grad_gain_attn_out,
            grad_gain_ffn_in,
            grad_gain_ffn_out,
            grad_gain_query,
            grad_gain_key,
            grad_gain_text_key,
            grad_gate_term,
        ),
        ("dp", "fsdp"),
    )
    return (
        output[None],
        grad_input[None],
        grad_w_modulate,
        grad_w_qkv,
        grad_w_text_kv,
        grad_w_out,
        grad_w_gate_up,
        grad_w_down,
        small_sums[0],
        small_sums[1],
        small_sums[2],
        small_sums[3],
        small_sums[4],
        small_sums[5],
        small_sums[6],
        small_sums[7],
    )


def solution(mesh):
    return jax.shard_map(
        per_device,
        mesh=mesh,
        in_specs=(
            P("fsdp", "dp", None),
            P("fsdp", "dp", None),
            P("fsdp", None),
            P("fsdp", "dp"),
            P("fsdp", None, None),
            P("fsdp", "dp", None),
            P("fsdp", None),
            P("fsdp", None),
            P("fsdp", None),
            P("fsdp", None),
            P(None, None, "fsdp"),
            P("fsdp", None),
            P(),
            P(),
            P(),
            P(),
            P(),
            P(),
            P(),
            P(),
        ),
        out_specs=(
            P("fsdp", "dp", None),
            P("fsdp", "dp", None),
            P("fsdp", "dp"),
            P("fsdp", "dp"),
            P("fsdp", "dp"),
            P("fsdp", "dp"),
            P(None, "dp", "fsdp"),
            P("fsdp", "dp"),
            P(),
            P(),
            P(),
            P(),
            P(),
            P(),
            P(),
            P(),
        ),
        check_vma=False,
    )
```

profile of v0, /device:TPU:0, one launch (start us, length us, event | category | flops | bytes accessed | tf_op | source)
XLA Modules:
  0.0 3735.0 jit_solution(17778455118086896997)
XLA Ops:
  9.6 296.5 %all-gather.21.cloned.1.call-done = bf16[4096,3072]{1,0:T(8,128)(2,1)} async-done(((bf16[2048,3072]{1,0:T(8,128)(2,1)}), bf16[4096,3072]{1,0:T(8,128)(2,1)}) %all-gather.21.cloned.1.call-update) | async-done | bytes 25165840 | tf_op jit(solution)/shard_map/all_gather | solution.py:75
  320.6 211.4 %all-gather.13.cloned.1.call-done = bf16[1536,6144]{1,0:T(8,128)(2,1)} async-done(((bf16[768,6144]{1,0:T(8,128)(2,1)}), bf16[1536,6144]{1,0:T(8,128)(2,1)}) %all-gather.13.cloned.1.call-update) | async-done | bytes 18874384 | tf_op jit(solution)/shard_map/all_gather | solution.py:75
  547.7 155.6 %all-gather.15.cloned.1.call-done = bf16[1536,4608]{1,0:T(8,128)(2,1)} async-done(((bf16[768,4608]{1,0:T(8,128)(2,1)}), bf16[1536,4608]{1,0:T(8,128)(2,1)}) %all-gather.15.cloned.1.call-update) | async-done | bytes 14155792 | tf_op jit(solution)/shard_map/all_gather | solution.py:75
  767.3 19.2 all-gather.23.cloned.1.call-done
  789.1 99.2 %all-gather.19.cloned.1.call-done = bf16[4096,1536]{1,0:T(8,128)(2,1)} async-done(((bf16[256,1536]{1,0:T(8,128)(2,1)}), bf16[4096,1536]{1,0:T(8,128)(2,1)}) %all-gather.19.cloned.1.call-update) | async-done | bytes 12582928 | tf_op jit(solution)/shard_map/all_gather | solution.py:158
  888.3 15.9 copy.133
  904.2 89.0 %all-gather.17.cloned.1.call-done = bf16[4096,1536]{0,1:T(8,128)(2,1)} async-done(((bf16[256,1536]{0,1:T(8,128)(2,1)}), bf16[4096,1536]{0,1:T(8,128)(2,1)}) %all-gather.17.cloned.1.call-update) | async-done | bytes 12582928 | tf_op jit(solution)/shard_map/all_gather | solution.py:157
  993.7 277.6 %while.39 = (s32[]{:T(128)}, f32[24,256]{1,0:T(8,128)S(1)}, f32[24,256]{1,0:T(8,128)S(1)}, f32[24,256,64]{1,2,0:T(8,128)}, s32[256]{0:T(256)S(1)}, /*index=5*/s3...) while((s32[]{:T(128)}, f32[24,256]{1,0:T(8,128)S(1)}, ...), condition=%wide.region_6.7_spmd.clone, body=%wide.region_3.6_spmd.clone.sunk | while | flops 422803456 | bytes 53350644 | solution.py:186
  1289.5 61.4 %all-gather.29.cloned.1.call-done = bf16[2,1536,4096]{2,1,0:T(8,128)(2,1)} async-done(((bf16[2,1536,2048]{2,1,0:T(8,128)(2,1)}), bf16[2,1536,4096]{2,1,0:T(8,128)(2,1)}) %all-gather.29.cloned.1.call-update) | async-done | bytes 25165840 | tf_op jit(solution)/shard_map/all_gather | solution.py:75
  1350.9 12.2 convolution_bitcast_fusion
  1370.0 134.9 %all-gather.31.cloned.1.call-done = bf16[4096,1536]{1,0:T(8,128)(2,1)} async-done(((bf16[2048,1536]{1,0:T(8,128)(2,1)}), bf16[4096,1536]{1,0:T(8,128)(2,1)}) %all-gather.31.cloned.1.call-update) | async-done | bytes 12582928 | tf_op jit(solution)/shard_map/all_gather | solution.py:75
  1531.0 16.1 multiply_reduce_fusion.3
  1613.7 14.5 convert_bitcast_fusion
  1628.9 233.5 %while.40 = (s32[]{:T(128)}, f32[256,24,64]{0,2,1:T(8,128)}, s32[16]{0:T(128)S(1)}, bf16[4096,1536]{0,1:T(8,128)(2,1)}, s32[256]{0:T(256)S(1)}, /*index=5*/s32[4...) while((s32[]{:T(128)}, f32[256,24,64]{0,2,1:T(8,128)}, ...), condition=%wide.region_19.20_spmd.clone, body=%wide.region_18.19_spmd.clone.sunk | while | flops 616235008 | bytes 22991072 | solution.py:338
  1870.1 22.9 all_gather.59
  1893.0 18.9 all_gather.61
  1912.0 353.9 %while.41 = (s32[]{:T(128)}, f32[256,24,64]{0,2,1:T(8,128)}, f32[256,24,64]{0,2,1:T(8,128)}, s32[16]{0:T(128)S(1)}, bf16[4096,1536]{0,1:T(8,128)(2,1)}, /*index=...) while((s32[]{:T(128)}, f32[256,24,64]{0,2,1:T(8,128)}, ...), condition=%wide.region_22.23_spmd.clone, body=%wide.region_21.22_spmd.clone.sunk | while | flops 824639488 | bytes 41267552 | solution.py:385
  2319.8 13.0 convert_bitcast_fusion.1
  2334.2 12.4 multiply_reduce_fusion.5
  2351.0 18.0 convolution_convert_fusion
  2382.1 32.0 copy.154
  2414.1 76.3 %reduce-scatter.24.cloned.1.call-done = bf16[768,4608]{1,0:T(8,128)(2,1)} async-done(((bf16[1536,4608]{1,0:T(8,128)(2,1)}), bf16[768,4608]{1,0:T(8,128)(2,1)}) %reduce-scatter.24.cloned.1.call-update) | async-done | bytes 7077904 | tf_op jit(solution)/shard_map/reduce_scatter | solution.py:86
  2500.9 271.3 %reduce-scatter.30.cloned.1.call-done = bf16[2048,3072]{0,1:T(8,128)(2,1)} async-done(((bf16[4096,3072]{0,1:T(8,128)(2,1)}), bf16[2048,3072]{0,1:T(8,128)(2,1)}) %reduce-scatter.30.cloned.1.call-update) | async-done | bytes 12582928 | tf_op jit(solution)/shard_map/reduce_scatter | solution.py:86
  2772.3 213.9 %reduce-scatter.22.cloned.1.call-done = bf16[768,6144]{1,0:T(8,128)(2,1)} async-done(((bf16[1536,6144]{1,0:T(8,128)(2,1)}), bf16[768,6144]{1,0:T(8,128)(2,1)}) %reduce-scatter.22.cloned.1.call-update) | async-done | bytes 9437200 | tf_op jit(solution)/shard_map/reduce_scatter | solution.py:86
  2986.1 12.6 copy.162
  3000.8 52.6 %reduce-scatter.44.cloned.1.call-done = bf16[96,768]{1,0:T(8,128)(2,1)} async-done(((bf16[1536,768]{1,0:T(8,128)(2,1)}), bf16[96,768]{1,0:T(8,128)(2,1)}) %reduce-scatter.44.cloned.1.call-update) | async-done | bytes 147472
  3057.1 41.4 %all-reduce.5 = (f32[1536]{0:T(1024)}, f32[1536]{0:T(1024)}, f32[1536]{0:T(1024)}, f32[1536]{0:T(1024)}, f32[64]{0:T(128)}, /*index=5*/f32[64]{0:T(128)}, f32[64]{0:T(128)}, f32[24]{0:T(128)}) all-reduce(f32[1536]{0:T(1024)S(1)} %get-tuple-element.506, f32[1536]{0:T(1024)S(1)} %copy-done.83, ...), channel_id=1, replica_groups=mesh['dp'=16,'fsdp'=2] {'dp','fsdp'}, use_global_device_ids=true, to_apply=%region_41.42 | all-reduce | flops 6360 | bytes 50880 | tf_op jit(solution)/shard_map/psum | solution.py:417
  3102.0 40.1 %reduce-scatter.46.cloned.1.call-done = bf16[96,2048]{1,0:T(8,128)(2,1)} async-done(((bf16[1536,2048]{1,0:T(8,128)(2,1)}), bf16[96,2048]{1,0:T(8,128)(2,1)}) %reduce-scatter.46.cloned.1.call-update) | async-done | bytes 393232
  3144.5 233.8 %all-reduce.8.cloned.1.call-done = bf16[2,1536,2048]{2,0,1:T(2,128)(2,1)} async-done(((bf16[2,1536,2048]{2,0,1:T(2,128)(2,1)}), bf16[2,1536,2048]{2,0,1:T(2,128)(2,1)}) %all-reduce.8.cloned.1.call-update) | async-done | bytes 12582928
  3382.5 90.4 %reduce-scatter.42.cloned.1.call-done = bf16[288,768]{1,0:T(8,128)(2,1)} async-done(((bf16[4608,768]{1,0:T(8,128)(2,1)}), bf16[288,768]{1,0:T(8,128)(2,1)}) %reduce-scatter.42.cloned.1.call-update) | async-done | bytes 442384
  3475.4 135.7 %reduce-scatter.32.cloned.1.call-done = bf16[2048,192]{0,1:T(8,128)(2,1)} async-done(((bf16[2048,3072]{0,1:T(8,128)(2,1)}), bf16[2048,192]{0,1:T(8,128)(2,1)}) %reduce-scatter.32.cloned.1.call-update) | async-done | bytes 786448 | tf_op jit(solution)/shard_map/reduce_scatter | solution.py:79
  3613.5 112.0 %reduce-scatter.40.cloned.1.call-done = bf16[384,768]{1,0:T(8,128)(2,1)} async-done(((bf16[6144,768]{1,0:T(8,128)(2,1)}), bf16[384,768]{1,0:T(8,128)(2,1)}) %reduce-scatter.40.cloned.1.call-update) | async-done | bytes 589840
  (997 shorter events, 1162.1 us)
Async XLA Ops:
  7.2 298.8 %copy-start = (bf16[1,32,4096]{2,1,0:T(8,128)(2,1)S(1)}, bf16[1,32,4096]{2,1,0:T(8,128)(2,1)}, u32[]{:S(2)}) copy-start(bf16[1,32,4096]{2,1,0:T(8,128)(2,1)} %param.31) | copy-start | bytes 786436
  7.2 298.8 %all-gather.21.cloned.1.call-start = ((), (), s32[]{:S(2)}) async-start(), calls=%async_computation.17 | async-start | bytes 37748736 | tf_op jit(solution)/shard_map/all_gather | solution.py:75
  7.9 524.0 %all-gather.13.cloned.1.call-start = ((), (), s32[]{:S(2)}) async-start(), calls=%async_computation.13 | async-start | bytes 28311552 | tf_op jit(solution)/shard_map/all_gather | solution.py:75
  8.7 694.7 %all-gather.15.cloned.1.call-start = ((), (), s32[]{:S(2)}) async-start(), calls=%async_computation.14 | async-start | bytes 21233664 | tf_op jit(solution)/shard_map/all_gather | solution.py:75
  9.4 742.8 %all-gather.25.cloned.1.call-start = ((), (), s32[]{:S(2)}) async-start(), calls=%async_computation.19 | async-start | bytes 1671168 | tf_op jit(solution)/shard_map/all_gather | solution.py:197
  9.6 308.6 %copy-start.76 = (f32[1536]{0:T(1024)}, f32[1536]{0:T(1024)S(1)}, u32[]{:S(2)}) copy-start(f32[1536]{0:T(1024)S(1)} %mul.896) | copy-start | bytes 18436
  318.0 214.0 %copy-start.78 = (f32[1,2,1536]{2,1,0:T(2,128)S(1)}, f32[1,2,1536]{2,1,0:T(2,128)}, u32[]{:S(2)}) copy-start(f32[1,2,1536]{2,1,0:T(2,128)} %param.30) | copy-start | bytes 36868
  318.2 222.7 %copy-start.42 = (f32[32,1536]{1,0:T(8,128)}, f32[32,1536]{1,0:T(8,128)S(1)}, u32[]{:S(2)}) copy-start(f32[32,1536]{1,0:T(8,128)S(1)} %mul.893) | copy-start | bytes 589828
  318.9 467.6 %all-gather.23.cloned.1.call-start = ((), (), s32[]{:S(2)}) async-start(), calls=%async_computation.18 | async-start | bytes 1671168 | tf_op jit(solution)/shard_map/all_gather | solution.py:198
  319.8 221.1 %copy-start.91 = (f32[256]{0:T(256)}, f32[256]{0:T(256)S(1)}, u32[]{:S(2)}) copy-start(f32[256]{0:T(256)S(1)} %fusion.73) | copy-start | bytes 3076
  319.8 223.7 %copy-start.89 = (f32[256]{0:T(256)}, f32[256]{0:T(256)S(1)}, u32[]{:S(2)}) copy-start(f32[256]{0:T(256)S(1)} %fusion.110) | copy-start | bytes 3076
  320.5 567.8 %all-gather.19.cloned.1.call-start = ((), (), s32[]{:S(2)}) async-start(), calls=%async_computation.16 | async-start | bytes 13369344 | tf_op jit(solution)/shard_map/all_gather | solution.py:158
  713.7 279.5 %all-gather.17.cloned.1.call-start = ((), (), s32[]{:S(2)}) async-start(), calls=%async_computation.15 | async-start | bytes 13369344 | tf_op jit(solution)/shard_map/all_gather | solution.py:157
  744.3 535.5 %all-gather.27.cloned.1.call-start = ((), (), s32[]{:S(2)}) async-start(), calls=%async_computation.20 | async-start | bytes 7077888 | tf_op jit(solution)/shard_map/all_gather | solution.py:75
  745.1 605.8 %all-gather.29.cloned.1.call-start = ((), (), s32[]{:S(2)}) async-start(), calls=%async_computation.21 | async-start | bytes 37748736 | tf_op jit(solution)/shard_map/all_gather | solution.py:75
  745.8 759.0 %all-gather.31.cloned.1.call-start = ((), (), s32[]{:S(2)}) async-start(), calls=%async_computation.22 | async-start | bytes 18874368 | tf_op jit(solution)/shard_map/all_gather | solution.py:75
  746.4 1165.5 %all-gather.33.cloned.1.call-start = ((), (), s32[]{:S(2)}) async-start(), calls=%async_computation.23 | async-start | bytes 13369344 | tf_op jit(solution)/shard_map/all_gather | solution.py:345
  751.8 1160.2 %all-gather.35.cloned.1.call-start = ((), (), s32[]{:S(2)}) async-start(), calls=%async_computation.24 | async-start | bytes 13369344 | tf_op jit(solution)/shard_map/all_gather | solution.py:346
  1558.8 759.2 %reduce-scatter.26.cloned.1.call-start = ((), (), s32[]{:S(2)}) async-start(), calls=%async_computation.27 | async-start | bytes 1671168 | tf_op jit(solution)/shard_map/reduce_scatter | solution.py:281
  1578.5 741.3 %reduce-scatter.28.cloned.1.call-start = ((), (), s32[]{:S(2)}) async-start(), calls=%async_computation.28 | async-start | bytes 1671168 | tf_op jit(solution)/shard_map/reduce_scatter | solution.py:287
  1587.0 782.1 %reduce-scatter.34.cloned.1.call-start = ((), (), s32[]{:S(2)}) async-start(), calls=%async_computation.31 | async-start | bytes 7077888 | tf_op jit(solution)/shard_map/reduce_scatter | solution.py:86
  1591.7 781.8 %reduce-scatter.38.cloned.1.call-start = ((), (), s32[]{:S(2)}) async-start(), calls=%async_computation.33 | async-start | bytes 18874368 | tf_op jit(solution)/shard_map/reduce_scatter | solution.py:86
  1600.8 781.2 %reduce-scatter.36.cloned.1.call-start = ((), (), s32[]{:S(2)}) async-start(), calls=%async_computation.32 | async-start | bytes 37748736 | tf_op jit(solution)/shard_map/reduce_scatter | solution.py:86
  1628.2 862.3 %reduce-scatter.24.cloned.1.call-start = ((), (), s32[]{:S(2)}) async-start(), calls=%async_computation.26 | async-start | bytes 21233664 | tf_op jit(solution)/shard_map/reduce_scatter | solution.py:86
  2317.8 454.3 %reduce-scatter.30.cloned.1.call-start = ((), (), s32[]{:S(2)}) async-start(), calls=%async_computation.29 | async-start | bytes 37748736 | tf_op jit(solution)/shard_map/reduce_scatter | solution.py:86
  2332.8 653.3 %reduce-scatter.22.cloned.1.call-start = ((), (), s32[]{:S(2)}) async-start(), calls=%async_computation.25 | async-start | bytes 28311552 | tf_op jit(solution)/shard_map/reduce_scatter | solution.py:86
  2369.0 684.4 %reduce-scatter.44.cloned.1.call-start = ((), (), s32[]{:S(2)}) async-start(), calls=%async_computation.36 | async-start | bytes 2506752
  2373.4 768.8 %reduce-scatter.46.cloned.1.call-start = ((), (), s32[]{:S(2)}) async-start(), calls=%async_computation.37 | async-start | bytes 6684672
  2382.0 996.4 %all-reduce.8.cloned.1.call-start = ((), (), s32[]{:S(2)}) async-start(), calls=%async_computation.38 | async-start | bytes 25165824
  2414.1 1058.8 %reduce-scatter.42.cloned.1.call-start = ((), (), s32[]{:S(2)}) async-start(), calls=%async_computation.35 | async-start | bytes 7520256
  2500.8 1110.2 %reduce-scatter.32.cloned.1.call-start = ((), (), s32[]{:S(2)}) async-start(), calls=%async_computation.30 | async-start | bytes 13369344 | tf_op jit(solution)/shard_map/reduce_scatter | solution.py:79
  2772.2 953.3 %reduce-scatter.40.cloned.1.call-start = ((), (), s32[]{:S(2)}) async-start(), calls=%async_computation.34 | async-start | bytes 10027008
  (177 other events, 1682.0 us)
Sparse Core Ops, SparseCore 0:
  9.6 296.3 all-gather.20
  307.6 224.3 all-gather.12
  533.5 169.7 all-gather.14
  705.5 39.6 all-gather.24
  747.9 38.5 all-gather.22
  788.6 99.6 all-gather.18
  891.0 102.1 all-gather.16
  994.7 60.8 all-gather.26
  1057.2 293.7 all-gather.28
  1352.3 152.5 all-gather.30
  1507.6 103.9 all-gather.32
  1614.3 98.9 all-gather.34
  1717.0 57.6 reduce-scatter.25
  1778.6 58.5 reduce-scatter.27
  1839.3 59.0 reduce-scatter.33
  1900.7 144.4 reduce-scatter.37
  2047.4 279.2 reduce-scatter.35
  2329.0 161.4 reduce-scatter.23
  2492.9 279.2 reduce-scatter.29
  2774.4 211.6 reduce-scatter.21
  2990.4 62.9 reduce-scatter.43
  3057.3 84.8 reduce-scatter.45
  3146.5 231.8 all-reduce.7
  3382.8 90.0 reduce-scatter.41
  3476.9 134.0 reduce-scatter.31
  3615.0 110.4 reduce-scatter.39
where the time goes:
time: 3750 us; the launch traced here: 3730 us
  waiting for transfers between devices  2300 us (61%)
  matrix products  781 us (21%)
  local copies, waits for them, and re-layouts  360 us (10%)
  other arithmetic  161 us (4%)
  blocking collectives  83.2 us (2%)
    all_gather x6, waiting for transfers between devices, full_weight(): return lax.all_gather(shard, 'fsdp', axis=shard_dim, tiled=True)  860 us
    reduce_scatter x6, waiting for transfers between devices, reduce_grad(): lax.psum_scatter(term.astype(jnp.bfloat16), 'fsdp', scatter_dimension=sha...  562 us
    unnamed x31, waiting for transfers between devices  533 us
    reduce_scatter x1, waiting for transfers between devices, sum_rows(): lax.psum_scatter(term.astype(jnp.bfloat16), 'dp', scatter_dimension=row_d...  136 us
    dot_general x16, matrix products, key_grad_block(): jnp.einsum('hqk,qhd->khd', grad_scores, block_queries, preferred_element_...  125 us
    dot_general x16, matrix products, query_grad_block(): jnp.einsum('hqk,khd->qhd', grad_scores, block_keys, preferred_element_typ...  117 us
    all_gather x1, waiting for transfers between devices, per_device(): piece_values = lax.all_gather(value_flat, 'dp', axis=0, tiled=True)  99.2 us
    dot_general x16, matrix products, key_grad_block(): jnp.einsum('hqk,qhd->khd', weights, block_grads.astype(jnp.float32))  92.6 us
  transfers between devices with their start and end apart: 26, of which 17 were waited for; matrix products, arithmetic and copies ran while one was open for 34% of the time, Pallas kernels for 0%

commit v1 on v0

v1 whole, which is shorter than its diff:
```python
import functools
import math

import jax
import jax.numpy as jnp
import numpy as np
from jax import lax
from jax.experimental import pallas as pl
from jax.experimental.pallas import tpu as pltpu
from jax.sharding import PartitionSpec as P

HD = 64
CTX = 256
FRAME_TOK = 128
PW = 16
EPSILON = 1e-06
GROUP_HEADS = 3
GROUP_WIDTH = GROUP_HEADS * HD
STACK = GROUP_HEADS * FRAME_TOK
ONES_ROWS = 16
HIGHEST = lax.Precision.HIGHEST
BF16 = jnp.bfloat16
F32 = jnp.float32
SCALE = HD ** (-0.5)
EXP2_SCALE = SCALE * math.log2(math.e)
MIB = 1 << 20


def mxu(a, b, dims=((1,), (0,))):
    return lax.dot_general(a, b, (dims, ((), ())), preferred_element_type=F32)


class Moves:
    def __init__(self, axis, size):
        self.axis = axis
        self.size = size
        self.me = lax.axis_index(axis)

    def swap(self, value, mask):
        return lax.ppermute(value, self.axis, [(i, i ^ mask) for i in range(self.size)])

    def gather(self, value):
        return [value] + [self.swap(value, s) for s in range(1, self.size)]

    def scatter_sum(self, parts):
        total = parts[0].astype(F32)
        for s in range(1, self.size):
            total = total + self.swap(parts[s].astype(BF16), s).astype(F32)
        return total

    def reorder(self, value, axis):
        block = value.shape[axis] // self.size
        return jnp.concatenate(
            [
                lax.dynamic_slice_in_dim(value, (self.me ^ s) * block, block, axis)
                for s in range(self.size)
            ],
            axis,
        )

    def own_block(self, value, axis, s=0):
        block = value.shape[axis] // self.size
        return lax.dynamic_slice_in_dim(value, (self.me ^ s) * block, block, axis)


def lane_tiles(width):
    return -(-width // 128) * 128


def turn(values, cosine, sine):
    lane = lax.broadcasted_iota(jnp.int32, values.shape, 1)
    other = jnp.where(lane % 2 == 0, pltpu.roll(values, 127, 1), pltpu.roll(values, 1, 1))
    return values * cosine + other * sine


def head_sums(values, ones):
    return lax.dot_general(
        values, ones, (((1,), (0,)), ((), ())), precision=HIGHEST, preferred_element_type=F32
    )


def norm_fwd_kernel(raw_ref, cos_ref, sin_ref, gain_ref, ones_ref, out_ref, *, kinds, wide, groups):
    for part, (normed, turned) in enumerate(kinds):
        pieces = []
        for t in range(wide // 128):
            x = raw_ref[:, part * wide + 128 * t : part * wide + 128 * (t + 1)]
            if normed:
                mean = head_sums(x * x, ones_ref[...]) * (1.0 / HD)
                x = x * lax.rsqrt(mean + EPSILON) * gain_ref[part : part + 1, :]
            if turned:
                x = turn(x, cos_ref[...], sin_ref[...])
            pieces.append(x)
        full = jnp.concatenate(pieces, axis=1) if len(pieces) > 1 else pieces[0]
        for g in range(groups):
            out_ref[part, g] = full[:, GROUP_WIDTH * g : GROUP_WIDTH * (g + 1)].astype(BF16)


def norm_bwd_kernel(
    raw_ref, grad_ref, cos_ref, sin_ref, gain_ref, ones_ref, out_ref, dgain_ref, *, kinds, wide, groups
):
    @pl.when(pl.program_id(0) == 0)
    def _():
        dgain_ref[...] = jnp.zeros_like(dgain_ref)

    rows = raw_ref.shape[0]
    for part, (normed, turned) in enumerate(kinds):
        pieces = [grad_ref[part, g].astype(F32) for g in range(groups)]
        if wide > groups * GROUP_WIDTH:
            pieces.append(jnp.zeros((rows, wide - groups * GROUP_WIDTH), F32))
        full = jnp.concatenate(pieces, axis=1) if len(pieces) > 1 else pieces[0]
        total = jnp.zeros((1, 128), F32)
        for t in range(wide // 128):
            dy = full[:, 128 * t : 128 * (t + 1)]
            if turned:
                dy = turn(dy, cos_ref[...], -sin_ref[...])
            if normed:
                x = raw_ref[:, part * wide + 128 * t : part * wide + 128 * (t + 1)]
                mean = head_sums(x * x, ones_ref[...]) * (1.0 / HD)
                inv = lax.rsqrt(mean + EPSILON)
                unit = x * inv
                total = total + jnp.sum(dy * unit, axis=0, keepdims=True)
                dn = dy * gain_ref[part : part + 1, :]
                dy = inv * (dn - unit * (head_sums(dn * unit, ones_ref[...]) * (1.0 / HD)))
            out_ref[:, part * wide + 128 * t : part * wide + 128 * (t + 1)] = dy.astype(BF16)
        if normed:
            dgain_ref[part : part + 1, :] += total


def head_ones():
    lane = np.arange(128) // HD
    return jnp.asarray((lane[:, None] == lane[None, :]).astype(np.float32))


def norm_fwd(raw, cosine, sine, gains, kinds, groups):
    rows = raw.shape[0]
    wide = raw.shape[1] // len(kinds)
    block = min(rows, 128)
    return pl.pallas_call(
        functools.partial(norm_fwd_kernel, kinds=kinds, wide=wide, groups=groups),
        grid=(rows // block,),
        in_specs=[
            pl.BlockSpec((block, raw.shape[1]), lambda i: (i, 0)),
            pl.BlockSpec((block, 128), lambda i: (i, 0)),
            pl.BlockSpec((block, 128), lambda i: (i, 0)),
            pl.BlockSpec((8, 128), lambda i: (0, 0)),
            pl.BlockSpec((128, 128), lambda i: (0, 0)),
        ],
        out_specs=pl.BlockSpec((len(kinds), groups, block, GROUP_WIDTH), lambda i: (0, 0, i, 0)),
        out_shape=jax.ShapeDtypeStruct((len(kinds), groups, rows, GROUP_WIDTH), BF16),
        compiler_params=pltpu.CompilerParams(vmem_limit_bytes=32 * MIB),
        name="head_norm",
    )(raw, cosine, sine, gains, head_ones())


def norm_bwd(raw, grad, cosine, sine, gains, kinds, groups):
    rows = raw.shape[0]
    wide = raw.shape[1] // len(kinds)
    block = min(rows, 128)
    return pl.pallas_call(
        functools.partial(norm_bwd_kernel, kinds=kinds, wide=wide, groups=groups),
        grid=(rows // block,),
        in_specs=[
            pl.BlockSpec((block, raw.shape[1]), lambda i: (i, 0)),
            pl.BlockSpec((len(kinds), groups, block, GROUP_WIDTH), lambda i: (0, 0, i, 0)),
            pl.BlockSpec((block, 128), lambda i: (i, 0)),
            pl.BlockSpec((block, 128), lambda i: (i, 0)),
            pl.BlockSpec((8, 128), lambda i: (0, 0)),
            pl.BlockSpec((128, 128), lambda i: (0, 0)),
        ],
        out_specs=[
            pl.BlockSpec((block, raw.shape[1]), lambda i: (i, 0)),
            pl.BlockSpec((8, 128), lambda i: (0, 0)),
        ],
        out_shape=[
            jax.ShapeDtypeStruct(raw.shape, BF16),
            jax.ShapeDtypeStruct((8, 128), F32),
        ],
        compiler_params=pltpu.CompilerParams(vmem_limit_bytes=32 * MIB),
        name="head_norm_back",
    )(raw, grad, cosine, sine, gains, head_ones())


BIG = 4


def over_tiles(start, count, body):
    big = count // BIG

    def big_step(t, carry):
        body(pl.multiple_of((start + t * BIG) * FRAME_TOK, FRAME_TOK), BIG * FRAME_TOK)
        return carry

    def small_step(t, carry):
        body(pl.multiple_of((start + big * BIG + t) * FRAME_TOK, FRAME_TOK), FRAME_TOK)
        return carry

    lax.fori_loop(0, big, big_step, 0)
    lax.fori_loop(0, count - big * BIG, small_step, 0)


def stacked(values, mask):
    return jnp.concatenate([values] * GROUP_HEADS, axis=0) * mask


def diagonal(values):
    own = [
        values[HD * h : HD * (h + 1), FRAME_TOK * h : FRAME_TOK * (h + 1)]
        for h in range(GROUP_HEADS)
    ]
    return jnp.transpose(jnp.concatenate(own, axis=0))


def head_row(values):
    flipped = jnp.transpose(values)
    return jnp.concatenate(
        [
            jnp.sum(flipped[HD * h : HD * (h + 1), :], axis=0, keepdims=True)
            for h in range(GROUP_HEADS)
        ],
        axis=1,
    )


def attn_fwd_kernel(
    rank_ref,
    start_ref,
    count_ref,
    clip_ref,
    place_ref,
    kv_ref,
    q_ref,
    gate_ref,
    mask_ref,
    mixed_ref,
    self_ref,
    text_ref,
    lse_ref,
    keys,
    values,
    rows_text,
    acc,
    *,
    chunks,
    frames,
    chunk_text,
):
    s = pl.program_id(0)
    j = pl.program_id(1)
    self_rows = chunks * frames * FRAME_TOK
    tokens = frames * FRAME_TOK

    @pl.when(j == 0)
    def _():
        values[GROUP_WIDTH:, :] = jnp.ones((ONES_ROWS, values.shape[1]), BF16)

        def chunk(i, carry):
            for f in range(frames):
                at = pl.multiple_of(rank_ref[s, i * frames + f] * FRAME_TOK, FRAME_TOK)
                rows = slice(f * FRAME_TOK, (f + 1) * FRAME_TOK)
                keys[pl.ds(at, FRAME_TOK), :] = kv_ref[i, 0, rows, :]
                values[:GROUP_WIDTH, pl.ds(at, FRAME_TOK)] = jnp.transpose(kv_ref[i, 1, rows, :])
            at = pl.multiple_of(place_ref[i] * chunk_text, chunk_text)
            rows = slice(tokens, tokens + chunk_text)
            keys[pl.ds(self_rows + at, chunk_text), :] = kv_ref[i, 0, rows, :]
            rows_text[pl.ds(at, chunk_text), :] = kv_ref[i, 1, rows, :]
            return carry

        lax.fori_loop(0, chunks, chunk, 0)
        for b in range(chunks * chunk_text // 128):
            values[:GROUP_WIDTH, self_rows + 128 * b : self_rows + 128 * (b + 1)] = jnp.transpose(
                rows_text[128 * b : 128 * (b + 1), :]
            )

    query = stacked(q_ref[0, 0, 0], mask_ref[...])

    def tile(base, size):
        scores = mxu(keys[pl.ds(base, size), :], query, ((1,), (1,)))
        weights = jnp.exp2(scores * EXP2_SCALE).astype(BF16)
        acc[...] += mxu(values[:, pl.ds(base, size)], weights)

    def finish(row):
        total = acc[GROUP_WIDTH : GROUP_WIDTH + 1, :]
        lse_ref[0, 0, row : row + 1, :] = jnp.log(total) * math.log2(math.e)
        return diagonal(acc[:GROUP_WIDTH, :] * (1.0 / total))

    acc[...] = jnp.zeros_like(acc)
    over_tiles(start_ref[s, j], count_ref[s, j], tile)
    self_out = finish(0)
    acc[...] = jnp.zeros_like(acc)
    tile(pl.multiple_of(self_rows + clip_ref[s, j] * CTX, 128), CTX)
    text_out = finish(1)
    self_ref[0, 0, 0] = self_out
    text_ref[0, 0, 0] = text_out
    mixed_ref[0, 0, 0] = (self_out + gate_ref[...] * text_out).astype(BF16)


def attn_bwd_kernel(
    rank_ref,
    start_ref,
    count_ref,
    clip_ref,
    place_ref,
    kv_ref,
    q_ref,
    grad_ref,
    self_ref,
    text_ref,
    lse_ref,
    gate_ref,
    mask_ref,
    dq_ref,
    dkv_ref,
    dgate_ref,
    keys,
    keys_flip,
    values,
    dkeys,
    dvalues,
    dquery,
    rows_text,
    *,
    chunks,
    frames,
    chunk_text,
):
    s = pl.program_id(0)
    j = pl.program_id(1)
    self_rows = chunks * frames * FRAME_TOK
    tokens = frames * FRAME_TOK

    @pl.when(jnp.logical_and(s == 0, j == 0))
    def _():
        dgate_ref[...] = jnp.zeros_like(dgate_ref)

    @pl.when(j == 0)
    def _():
        dkeys[...] = jnp.zeros_like(dkeys)
        dvalues[...] = jnp.zeros_like(dvalues)

        def chunk(i, carry):
            for f in range(frames):
                at = pl.multiple_of(rank_ref[s, i * frames + f] * FRAME_TOK, FRAME_TOK)
                rows = slice(f * FRAME_TOK, (f + 1) * FRAME_TOK)
                keys[pl.ds(at, FRAME_TOK), :] = kv_ref[i, 0, rows, :]
                keys_flip[:, pl.ds(at, FRAME_TOK)] = jnp.transpose(kv_ref[i, 0, rows, :])
                values[pl.ds(at, FRAME_TOK), :] = kv_ref[i, 1, rows, :]
            at = pl.multiple_of(place_ref[i] * chunk_text, chunk_text)
            rows = slice(tokens, tokens + chunk_text)
            keys[pl.ds(self_rows + at, chunk_text), :] = kv_ref[i, 0, rows, :]
            values[pl.ds(self_rows + at, chunk_text), :] = kv_ref[i, 1, rows, :]
            return carry

        lax.fori_loop(0, chunks, chunk, 0)
        for b in range(chunks * chunk_text // 128):
            rows = slice(self_rows + 128 * b, self_rows + 128 * (b + 1))
            keys_flip[:, rows] = jnp.transpose(keys[rows, :])

    mask = mask_ref[...]
    query = stacked(q_ref[0, 0, 0], mask)
    grad_low = grad_ref[0, 0, 0]
    grad_wide = grad_low.astype(F32)
    grad_text = (grad_wide * gate_ref[...]).astype(BF16)
    text_out = text_ref[0, 0, 0]
    dgate_ref[...] += jnp.sum(grad_wide * text_out, axis=0, keepdims=True)
    dquery[...] = jnp.zeros_like(dquery)

    def over(grad, out, lse):
        grad_stack = stacked(grad, mask)
        delta = head_row(grad.astype(F32) * out)

        def tile(base, size):
            rows = pl.ds(base, size)
            scores = mxu(keys[rows, :], query, ((1,), (1,)))
            weights = jnp.exp2(scores * EXP2_SCALE - lse)
            dweights = mxu(values[rows, :], grad_stack, ((1,), (1,)))
            dscores = (weights * (dweights - delta)).astype(BF16)
            dvalues[rows, :] += mxu(weights.astype(BF16), grad_stack)
            dkeys[rows, :] += mxu(dscores, query)
            dquery[...] += mxu(keys_flip[:, rows], dscores)

        return tile

    over_tiles(start_ref[s, j], count_ref[s, j], over(grad_low, self_ref[0, 0, 0], lse_ref[0, 0, 0:1, :]))
    over(grad_text, text_out, lse_ref[0, 0, 1:2, :])(
        pl.multiple_of(self_rows + clip_ref[s, j] * CTX, 128), CTX
    )
    dq_ref[0, 0, 0] = (diagonal(dquery[...]) * SCALE).astype(BF16)

    @pl.when(j == pl.num_programs(1) - 1)
    def _():
        def chunk(i, carry):
            for f in range(frames):
                at = pl.multiple_of(rank_ref[s, i * frames + f] * FRAME_TOK, FRAME_TOK)
                rows = slice(f * FRAME_TOK, (f + 1) * FRAME_TOK)
                dkv_ref[i, 0, rows, :] = (dkeys[pl.ds(at, FRAME_TOK), :] * SCALE).astype(BF16)
                dkv_ref[i, 1, rows, :] = dvalues[pl.ds(at, FRAME_TOK), :].astype(BF16)
            at = pl.multiple_of(self_rows + place_ref[i] * chunk_text, chunk_text)
            rows = slice(tokens, tokens + chunk_text)
            dkv_ref[i, 0, rows, :] = (dkeys[pl.ds(at, chunk_text), :] * SCALE).astype(BF16)
            dkv_ref[i, 1, rows, :] = dvalues[pl.ds(at, chunk_text), :].astype(BF16)
            return carry

        lax.fori_loop(0, chunks, chunk, 0)


def attention_specs(kv, query):
    chunks, _, streams, chunk_rows, _ = kv.shape
    groups, _, frames = query.shape[:3]
    chunk_text = chunk_rows - frames * FRAME_TOK
    sizes = dict(chunks=chunks, frames=frames, chunk_text=chunk_text)
    grid = (streams, groups * frames)
    kv_spec = pl.BlockSpec(
        (chunks, 2, None, chunk_rows, GROUP_WIDTH),
        lambda s, j, *_: (0, 0, s, 0, 0),
        pipeline_mode=pl.Buffered(1),
    )
    tok_spec = pl.BlockSpec(
        (1, 1, 1, FRAME_TOK, GROUP_WIDTH), lambda s, j, *_: (j // frames, s, j % frames, 0, 0)
    )
    lse_spec = pl.BlockSpec((1, 1, 2, STACK), lambda s, j, *_: (s, j, 0, 0))
    gate_spec = pl.BlockSpec((1, GROUP_WIDTH), lambda s, j, *_: (0, 0))
    mask_spec = pl.BlockSpec((STACK, GROUP_WIDTH), lambda s, j, *_: (0, 0))
    return sizes, grid, kv_spec, tok_spec, lse_spec, gate_spec, mask_spec


def stack_mask():
    head_of_row = np.arange(STACK) // FRAME_TOK
    head_of_lane = np.arange(GROUP_WIDTH) // HD
    return jnp.asarray((head_of_row[:, None] == head_of_lane[None, :]).astype(np.float32), BF16)


def attn_fwd(tables, kv, query, gate):
    sizes, grid, kv_spec, tok_spec, lse_spec, gate_spec, mask_spec = attention_specs(kv, query)
    total = kv.shape[0] * kv.shape[3]
    text_rows = sizes["chunks"] * sizes["chunk_text"]
    wide = jax.ShapeDtypeStruct(query.shape, F32)
    return pl.pallas_call(
        functools.partial(attn_fwd_kernel, **sizes),
        grid_spec=pltpu.PrefetchScalarGridSpec(
            num_scalar_prefetch=5,
            grid=grid,
            in_specs=[kv_spec, tok_spec, gate_spec, mask_spec],
            out_specs=[tok_spec, tok_spec, tok_spec, lse_spec],
            scratch_shapes=[
                pltpu.VMEM((total, GROUP_WIDTH), BF16),
                pltpu.VMEM((GROUP_WIDTH + ONES_ROWS, total), BF16),
                pltpu.VMEM((text_rows, GROUP_WIDTH), BF16),
                pltpu.VMEM((GROUP_WIDTH + ONES_ROWS, STACK), F32),
            ],
        ),
        out_shape=[
            jax.ShapeDtypeStruct(query.shape, BF16),
            wide,
            wide,
            jax.ShapeDtypeStruct((grid[0], grid[1], 2, STACK), F32),
        ],
        compiler_params=pltpu.CompilerParams(
            dimension_semantics=("arbitrary", "arbitrary"),
            vmem_limit_bytes=min(60 * MIB, total * 2600 + 16 * MIB),
        ),
        cost_estimate=pl.CostEstimate(
            flops=grid[0] * grid[1] * STACK * 2304 * GROUP_WIDTH * 4,
            bytes_accessed=kv.size * 2 + query.size * 12,
            transcendentals=grid[0] * grid[1] * STACK * 2304,
        ),
        name="attention",
    )(*tables, kv, query, gate, stack_mask())


def attn_bwd(tables, kv, query, grad, self_out, text_out, lse, gate):
    sizes, grid, kv_spec, tok_spec, lse_spec, gate_spec, mask_spec = attention_specs(kv, query)
    total = kv.shape[0] * kv.shape[3]
    text_rows = sizes["chunks"] * sizes["chunk_text"]
    return pl.pallas_call(
        functools.partial(attn_bwd_kernel, **sizes),
        grid_spec=pltpu.PrefetchScalarGridSpec(
            num_scalar_prefetch=5,
            grid=grid,
            in_specs=[
                kv_spec,
                tok_spec,
                tok_spec,
                tok_spec,
                tok_spec,
                lse_spec,
                gate_spec,
                mask_spec,
            ],
            out_specs=[tok_spec, kv_spec, gate_spec],
            scratch_shapes=[
                pltpu.VMEM((total, GROUP_WIDTH), BF16),
                pltpu.VMEM((GROUP_WIDTH, total), BF16),
                pltpu.VMEM((total, GROUP_WIDTH), BF16),
                pltpu.VMEM((total, GROUP_WIDTH), F32),
                pltpu.VMEM((total, GROUP_WIDTH), F32),
                pltpu.VMEM((GROUP_WIDTH, STACK), F32),
                pltpu.VMEM((text_rows, GROUP_WIDTH), BF16),
            ],
        ),
        out_shape=[
            jax.ShapeDtypeStruct(query.shape, BF16),
            jax.ShapeDtypeStruct(kv.shape, BF16),
            jax.ShapeDtypeStruct((1, GROUP_WIDTH), F32),
        ],
        compiler_params=pltpu.CompilerParams(
            dimension_semantics=("arbitrary", "arbitrary"),
            vmem_limit_bytes=min(62 * MIB, total * 5800 + 16 * MIB),
        ),
        cost_estimate=pl.CostEstimate(
            flops=grid[0] * grid[1] * STACK * 2304 * GROUP_WIDTH * 10,
            bytes_accessed=kv.size * 4 + query.size * 14,
            transcendentals=grid[0] * grid[1] * STACK * 2304,
        ),
        name="attention_back",
    )(*tables, kv, query, grad, self_out, text_out, lse, gate, stack_mask())


def unit_rms(values):
    inv = lax.rsqrt(jnp.mean(values * values, axis=-1, keepdims=True) + EPSILON)
    return values * inv, inv


def unit_back(grad_unit, unit, inv):
    return inv * (grad_unit - unit * jnp.mean(grad_unit * unit, axis=-1, keepdims=True))


def rope_lanes(frames):
    half = HD // 2
    frame_pairs = HD // 8
    row_pairs = (half - frame_pairs) // 2
    col_pairs = half - frame_pairs - row_pairs
    pair = (np.arange(128) % HD) // 2

    def lanes(first, count):
        freq = 10000.0 ** (-(np.arange(count, dtype=np.float32)) / np.float32(count))
        out = np.zeros((128,), np.float32)
        inside = (pair >= first) & (pair < first + count)
        out[inside] = freq.astype(np.float32)[pair[inside] - first]
        return jnp.asarray(out)[None, :]

    rows = frames.shape[0]
    inner = jnp.arange(rows) % FRAME_TOK
    row_pos = (inner // PW).astype(F32)
    col_pos = (inner % PW).astype(F32)
    angle = (
        frames[:, None] * lanes(0, frame_pairs)
        + row_pos[:, None] * lanes(frame_pairs, row_pairs)
        + col_pos[:, None] * lanes(frame_pairs + row_pairs, col_pairs)
    )
    sign = jnp.asarray(np.where(np.arange(128) % 2 == 0, -1.0, 1.0).astype(np.float32))[None, :]
    return jnp.cos(angle), jnp.sin(angle) * sign


def gain_rows(*gains):
    rows = [jnp.concatenate([g, g]) for g in gains]
    rows += [jnp.zeros((128,), F32)] * (8 - len(rows))
    return jnp.stack(rows)


def pad_parts(values, parts):
    width = values.shape[1] // parts
    wide = lane_tiles(width)
    if wide == width:
        return values
    cut = values.reshape(values.shape[0], parts, width)
    cut = jnp.pad(cut, ((0, 0), (0, 0), (0, wide - width)))
    return cut.reshape(values.shape[0], parts * wide)


def cut_parts(values, parts, width):
    wide = values.shape[1] // parts
    if wide == width:
        return values
    return values.reshape(values.shape[0], parts, wide)[:, :, :width].reshape(
        values.shape[0], parts * width
    )


def bit_reverse(index, bits):
    return sum(((index >> b) & 1) << (bits - 1 - b) for b in range(bits))


def per_device(
    fsdp,
    dps,
    states,
    cotangent,
    segment_ids,
    frame_ids,
    condition,
    context,
    w_modulate,
    w_qkv,
    w_text_kv,
    w_out,
    w_gate_up,
    w_down,
    gain_attn_in,
    gain_attn_out,
    gain_ffn_in,
    gain_ffn_out,
    gain_query,
    gain_key,
    gain_text_key,
    cross_gate,
):
    xs = Moves("fsdp", fsdp)
    ds = Moves("dp", dps)
    rows_in = states[0]
    tokens, width = rows_in.shape
    frames = tokens // FRAME_TOK
    heads = cross_gate.shape[0]
    own_heads = heads // fsdp
    own_width = own_heads * HD
    groups = own_heads // GROUP_HEADS
    ranks = dps // groups
    clips = condition.shape[1]
    text_local = context[0]
    text_own = text_local.shape[0]
    all_tokens = fsdp * tokens
    group_me = ds.me // ranks
    rank_me = ds.me % ranks

    def frame_view(values):
        return values.reshape(frames, FRAME_TOK, values.shape[-1])

    def group_exchange(blocks):
        pick = lambda s: lax.dynamic_index_in_dim(blocks, group_me ^ s, 0, keepdims=False)
        return [pick(0)] + [ds.swap(pick(s), s * ranks) for s in range(1, groups)]

    def group_return(blocks):
        got = jnp.stack([blocks[0]] + [ds.swap(blocks[s], s * ranks) for s in range(1, groups)])
        return [
            lax.dynamic_index_in_dim(got, group_me ^ g, 0, keepdims=False) for g in range(groups)
        ]

    rank_bits = ranks.bit_length() - 1

    def rank_gather(value):
        for b in reversed(range(rank_bits)):
            value = jnp.stack([value, ds.swap(value, 1 << b)])
        return value.reshape((ranks,) + value.shape[rank_bits:])

    def rank_scatter(value):
        value = value.reshape((2,) * rank_bits + value.shape[1:])
        for b in range(rank_bits):
            got = ds.swap(value[1], 1 << b)
            value = (value[0].astype(F32) + got.astype(F32)).astype(BF16)
        return value

    own_frames = segment_ids[0][::FRAME_TOK].astype(F32)
    stream_seg = jnp.stack(xs.gather(own_frames)).astype(jnp.int32)
    rel_of_place = [bit_reverse(p, rank_bits) for p in range(ranks)]
    place_dev = jnp.stack(
        [
            (group_me ^ g) * ranks + (rank_me ^ rel_of_place[p])
            for p in range(ranks)
            for g in range(groups)
        ]
    )
    kv_frame = (place_dev[:, None] * frames + jnp.arange(frames)[None, :]).reshape(-1)
    q_dev = jnp.stack([(group_me ^ g) * ranks + rank_me for g in range(groups)])
    q_frame = (q_dev[:, None] * frames + jnp.arange(frames)[None, :]).reshape(-1)
    kv_seg = jnp.take(stream_seg, kv_frame, axis=1)
    q_seg = jnp.take(stream_seg, q_frame, axis=1)
    order = jnp.arange(kv_seg.shape[1])
    less = kv_seg[:, None, :] < kv_seg[:, :, None]
    tie = (kv_seg[:, None, :] == kv_seg[:, :, None]) & (order[None, None, :] < order[None, :, None])
    kv_rank = jnp.sum((less | tie).astype(jnp.int32), axis=2)
    q_start = jnp.sum((kv_seg[:, None, :] < q_seg[:, :, None]).astype(jnp.int32), axis=2)
    q_count = jnp.sum((kv_seg[:, None, :] == q_seg[:, :, None]).astype(jnp.int32), axis=2)
    tables = (
        kv_rank,
        q_start,
        q_count,
        jnp.maximum(q_seg, 0),
        place_dev.astype(jnp.int32),
    )

    silu_cond = jax.nn.silu(condition[0]).astype(BF16)
    cond_rel = jnp.concatenate(xs.gather(silu_cond))
    cond_own = xs.own_block(cond_rel, 1)
    mod_part = mxu(cond_own, w_modulate).reshape(fsdp, clips, -1)
    modulation = mod_part[0]
    for s in range(1, fsdp):
        modulation = modulation + xs.swap(mod_part[s], s)
    own_seg = lax.dynamic_slice_in_dim(stream_seg[0], ds.me * frames, frames)
    onehot = (own_seg[:, None] == jnp.arange(clips)[None, :]).astype(F32)
    per_frame = jnp.dot(onehot, modulation, precision=HIGHEST)[:, None, :]
    scale_attn, gate_attn, scale_ffn, gate_ffn = jnp.split(per_frame, 4, axis=2)

    def own_columns(weight, parts):
        rows = weight.shape[0]
        cut = weight.reshape(rows, parts, fsdp, own_width)
        pick = lambda s: lax.dynamic_index_in_dim(cut, xs.me ^ s, 2, keepdims=False)
        blocks = [pick(0)]
        core = ds.me % 2
        for s in range(1, fsdp):
            half = lax.dynamic_slice_in_dim(pick(s), core * (rows // 2), rows // 2)
            got = xs.swap(half, s)
            other = ds.swap(got, 1)
            blocks.append(
                jnp.where(
                    core == 0,
                    jnp.concatenate([got, other]),
                    jnp.concatenate([other, got]),
                )
            )
        return jnp.concatenate(blocks).reshape(fsdp * rows, parts * own_width)

    w_cols = own_columns(w_qkv, 3)
    states_f = frame_view(rows_in)
    unit_in, inv_in = unit_rms(states_f)
    normed = (unit_in * gain_attn_in * (1.0 + scale_attn)).astype(BF16).reshape(tokens, width)
    normed_all = xs.reorder(jnp.concatenate(xs.gather(normed)), 1)
    projected = pad_parts(mxu(normed_all, w_cols), 3)
    frames_all = jnp.concatenate(xs.gather(frame_ids[0].astype(F32)))
    cosine, sine = rope_lanes(frames_all)
    qk_kinds = ((True, True), (True, True), (False, False))
    qk_gains = gain_rows(gain_query, gain_key)
    heads_qkv = norm_fwd(projected, cosine, sine, qk_gains, qk_kinds, groups)

    text_rel = jnp.concatenate(
        [xs.own_block(text_local, 1)]
        + [xs.swap(xs.own_block(text_local, 1, s), s) for s in range(1, fsdp)]
    )
    text_part = mxu(text_rel, w_text_kv).reshape(fsdp, text_own, 2, fsdp, own_width)
    text_raw = lax.dynamic_index_in_dim(text_part, xs.me, 3, keepdims=False)
    for s in range(1, fsdp):
        piece = lax.dynamic_index_in_dim(text_part, xs.me ^ s, 3, keepdims=False)
        piece = jnp.stack([piece[s ^ k] for k in range(fsdp)])
        text_raw = text_raw + xs.swap(piece.astype(BF16), s).astype(F32)
    text_raw = pad_parts(text_raw.reshape(fsdp * text_own, 2 * own_width), 2)
    text_kinds = ((True, False), (False, False))
    text_gains = gain_rows(gain_text_key)
    text_flat = jnp.ones((fsdp * text_own, 128), F32)
    heads_text = norm_fwd(text_raw, text_flat, text_flat, text_gains, text_kinds, groups)

    def joined(parts, text):
        return jnp.concatenate(
            [
                parts.reshape(parts.shape[:2] + (fsdp, tokens, GROUP_WIDTH)),
                text.reshape(text.shape[:2] + (fsdp, text_own, GROUP_WIDTH)),
            ],
            axis=3,
        )

    kv_blocks = jnp.swapaxes(joined(heads_qkv[1:], heads_text), 0, 1)
    kv = rank_gather(jnp.stack(group_exchange(kv_blocks)))
    kv = kv.reshape((ranks * groups,) + kv.shape[2:])
    query = jnp.stack(group_exchange(heads_qkv[0]))
    query = query.reshape(groups, fsdp, frames, FRAME_TOK, GROUP_WIDTH)
    tanh_gate = jnp.tanh(cross_gate)
    first_head = xs.me * own_heads + group_me * GROUP_HEADS
    gate_row = jnp.repeat(lax.dynamic_slice_in_dim(tanh_gate, first_head, GROUP_HEADS), HD)[None, :]
    mixed_group, self_out, text_out, lse = attn_fwd(tables, kv, query, gate_row)
    mixed_low = jnp.concatenate(
        group_return(mixed_group.reshape(groups, all_tokens, GROUP_WIDTH)), axis=1
    )

    def by_stream(values):
        return values.reshape(fsdp, tokens, values.shape[-1])

    mixed_out = frame_view(xs.scatter_sum(by_stream(mxu(mixed_low, w_out))))
    unit_mix, inv_mix = unit_rms(mixed_out)
    tanh_attn = jnp.tanh(gate_attn)
    after = states_f + tanh_attn * unit_mix * gain_attn_out
    unit_ffn, inv_ffn = unit_rms(after)
    ffn_low = (unit_ffn * gain_ffn_in * (1.0 + scale_ffn)).astype(BF16).reshape(tokens, width)
    ffn_all = jnp.concatenate(xs.gather(ffn_low))
    gate_part = mxu(ffn_all, w_gate_up[0])
    up_part = mxu(ffn_all, w_gate_up[1])
    sig = jax.nn.sigmoid(gate_part)
    silu = gate_part * sig
    hidden = (silu * up_part).astype(BF16)
    ffn_out = frame_view(xs.scatter_sum(by_stream(mxu(hidden, w_down))))
    unit_out, inv_out = unit_rms(ffn_out)
    tanh_ffn = jnp.tanh(gate_ffn)
    output = after + tanh_ffn * unit_out * gain_ffn_out

    def frame_sum(values):
        return jnp.sum(values, axis=1)

    def gain_sum(values):
        return jnp.sum(values, axis=(0, 1))

    cot = frame_view(cotangent[0])
    cot_unit = cot * unit_out
    grad_gate_ffn = frame_sum(cot_unit) * gain_ffn_out * (1.0 - tanh_ffn[:, 0] ** 2)
    grad_gain_ffn_out = jnp.sum(frame_sum(cot_unit) * tanh_ffn[:, 0], axis=0)
    grad_ffn_low = (
        unit_back(cot * (tanh_ffn * gain_ffn_out), unit_out, inv_out)
        .astype(BF16)
        .reshape(tokens, width)
    )
    grad_ffn_all = jnp.concatenate(xs.gather(grad_ffn_low))
    grad_hidden = mxu(grad_ffn_all, w_down, ((1,), (1,)))
    grad_gate = grad_hidden * up_part * (sig * (1.0 + gate_part * (1.0 - sig)))
    grad_up = grad_hidden * silu
    grad_gate_low = grad_gate.astype(BF16)
    grad_up_low = grad_up.astype(BF16)

    def reduce_rows(term):
        return lax.psum_scatter(
            term.astype(BF16), "dp", scatter_dimension=0, tiled=True
        ).astype(F32)

    rows_first = ((0,), (0,))
    grad_w_down = jnp.transpose(reduce_rows(mxu(grad_ffn_all, hidden, rows_first)))
    grad_w_gate_up = jnp.stack(
        [
            reduce_rows(mxu(ffn_all, grad_gate_low, rows_first)),
            reduce_rows(mxu(ffn_all, grad_up_low, rows_first)),
        ]
    )
    grad_ffn_in = frame_view(
        xs.scatter_sum(
            by_stream(
                mxu(grad_gate_low, w_gate_up[0], ((1,), (1,)))
                + mxu(grad_up_low, w_gate_up[1], ((1,), (1,)))
            )
        )
    )
    grad_unit = grad_ffn_in * unit_ffn
    grad_scale_ffn = frame_sum(grad_unit) * gain_ffn_in
    grad_gain_ffn_in = jnp.sum(frame_sum(grad_unit) * (1.0 + scale_ffn[:, 0]), axis=0)
    grad_after = cot + unit_back(
        grad_ffn_in * (gain_ffn_in * (1.0 + scale_ffn)), unit_ffn, inv_ffn
    )
    after_unit = grad_after * unit_mix
    grad_gate_attn = frame_sum(after_unit) * gain_attn_out * (1.0 - tanh_attn[:, 0] ** 2)
    grad_gain_attn_out = jnp.sum(frame_sum(after_unit) * tanh_attn[:, 0], axis=0)
    grad_mix_low = (
        unit_back(grad_after * (tanh_attn * gain_attn_out), unit_mix, inv_mix)
        .astype(BF16)
        .reshape(tokens, width)
    )
    grad_mix_all = jnp.concatenate(xs.gather(grad_mix_low))
    grad_mixed = mxu(grad_mix_all, w_out, ((1,), (1,))).astype(BF16)
    grad_w_out = jnp.transpose(reduce_rows(mxu(grad_mix_all, mixed_low, rows_first)))

    grad_blocks = jnp.stack(
        [grad_mixed[:, GROUP_WIDTH * g : GROUP_WIDTH * (g + 1)] for g in range(groups)]
    )
    grad_group = jnp.stack(group_exchange(grad_blocks)).reshape(query.shape)
    dquery, dkv, dgate = attn_bwd(tables, kv, query, grad_group, self_out, text_out, lse, gate_row)
    dkv = rank_scatter(dkv.reshape((ranks, groups) + dkv.shape[1:]))
    dq_back = jnp.stack(group_return(dquery.reshape(groups, all_tokens, GROUP_WIDTH)))
    dkv_back = jnp.stack(group_return(dkv))
    dkv_tok = dkv_back[:, :, :, :tokens].reshape(groups, 2, all_tokens, GROUP_WIDTH)
    dkv_text = dkv_back[:, :, :, tokens:].reshape(groups, 2, fsdp * text_own, GROUP_WIDTH)
    grad_heads = jnp.concatenate([dq_back[None], jnp.swapaxes(dkv_tok, 0, 1)])
    grad_proj, gain_qk = norm_bwd(projected, grad_heads, cosine, sine, qk_gains, qk_kinds, groups)
    grad_proj = cut_parts(grad_proj, 3, own_width)
    grad_text, gain_text = norm_bwd(
        text_raw,
        jnp.swapaxes(dkv_text, 0, 1),
        text_flat,
        text_flat,
        text_gains,
        text_kinds,
        groups,
    )
    grad_text = cut_parts(grad_text, 2, own_width)

    grad_normed_rel = mxu(grad_proj, w_cols, ((1,), (1,)))
    grad_normed = frame_view(xs.scatter_sum(by_stream(xs.reorder(grad_normed_rel, 1))))
    in_unit = grad_normed * unit_in
    grad_scale_attn = frame_sum(in_unit) * gain_attn_in
    grad_gain_attn_in = jnp.sum(frame_sum(in_unit) * (1.0 + scale_attn[:, 0]), axis=0)
    grad_input = grad_after + unit_back(
        grad_normed * (gain_attn_in * (1.0 + scale_attn)), unit_in, inv_in
    )

    def gather_columns(values, rows, parts):
        cut = values.reshape(fsdp, rows, parts, own_width)
        got = [cut]
        for s in range(1, fsdp):
            other = xs.swap(cut, s)
            got.append(jnp.stack([other[s ^ k] for k in range(fsdp)]))
        got = jnp.stack(got)
        whole = jnp.stack(
            [lax.dynamic_index_in_dim(got, xs.me ^ k, 0, keepdims=False) for k in range(fsdp)],
            axis=3,
        )
        return whole.reshape(fsdp * rows, parts * fsdp * own_width)

    grad_proj_all = gather_columns(grad_proj, tokens, 3)
    normed_own = normed_all[:, : width // fsdp]
    grad_w_qkv = jnp.transpose(reduce_rows(mxu(grad_proj_all, normed_own, rows_first)))

    grad_text_all = gather_columns(grad_text, text_own, 2)
    text_cols = grad_text_all.shape[1] // dps
    grad_text_cols = jnp.swapaxes(
        grad_text_all.reshape(fsdp * text_own, dps, text_cols), 0, 1
    )
    grad_text_cols = lax.all_to_all(grad_text_cols, "dp", 0, 0, tiled=True)
    text_every = lax.all_gather(text_rel, "dp", axis=0, tiled=True)
    grad_w_text_kv = mxu(text_every, grad_text_cols.reshape(-1, text_cols), rows_first)

    frame_grads = jnp.concatenate(
        [grad_scale_attn, grad_gate_attn, grad_scale_ffn, grad_gate_ffn], axis=1
    )
    clip_grads = jnp.dot(jnp.transpose(onehot), frame_grads, precision=HIGHEST)
    mod_cols = clip_grads.shape[1] // dps
    clip_grads = jnp.swapaxes(clip_grads.reshape(clips, dps, mod_cols), 0, 1)
    clip_grads = jnp.sum(lax.all_to_all(clip_grads, "dp", 0, 0, tiled=True), axis=0)
    clip_rel = jnp.concatenate(xs.gather(clip_grads))
    grad_w_modulate = jnp.dot(
        jnp.transpose(cond_own.astype(F32)), clip_rel, precision=HIGHEST
    )
    head_term = jnp.sum(dgate.reshape(GROUP_HEADS, HD), axis=1)
    gate_term = lax.dynamic_update_slice_in_dim(
        jnp.zeros((heads,), F32), head_term, first_head, 0
    )
    gate_term = gate_term * (1.0 - tanh_gate * tanh_gate)
    fold = lambda row: row[:HD] + row[HD:]
    small = [
        grad_gain_attn_in,
        grad_gain_attn_out,
        grad_gain_ffn_in,
        grad_gain_ffn_out,
        fold(gain_qk[0]),
        fold(gain_qk[1]),
        fold(gain_text[0]),
        gate_term,
    ]
    sizes = [v.shape[0] for v in small]
    packed = jnp.concatenate(small)
    packed = jnp.pad(packed, (0, -packed.shape[0] % 1024)).reshape(-1, 128)
    for moves in (ds, xs):
        for b in range(moves.size.bit_length() - 1):
            packed = packed + moves.swap(packed, 1 << b)
    packed = packed.reshape(-1)
    sums = []
    at = 0
    for size in sizes:
        sums.append(packed[at : at + size])
        at += size
    return (
        output.reshape(1, tokens, width),
        grad_input.reshape(1, tokens, width),
        grad_w_modulate,
        grad_w_qkv,
        grad_w_text_kv,
        grad_w_out,
        grad_w_gate_up,
        grad_w_down,
        *sums,
    )


def solution(mesh):
    rows = P("fsdp", "dp", None)
    first = P("fsdp", None)
    split = P("fsdp", "dp")
    return jax.shard_map(
        functools.partial(per_device, mesh.shape["fsdp"], mesh.shape["dp"]),
        mesh=mesh,
        in_specs=(
            rows,
            rows,
            first,
            split,
            P("fsdp", None, None),
            rows,
            first,
            first,
            first,
            first,
            P(None, None, "fsdp"),
            first,
        )
        + (P(),) * 8,
        out_specs=(
            rows,
            rows,
            split,
            split,
            split,
            split,
            P(None, "dp", "fsdp"),
            split,
        )
        + (P(),) * 8,
        check_vma=False,
    )
```

time: 3750 us -> 1050 us (0.28)
  waiting for transfers between devices: 2300 us -> 504 us
  matrix products: 781 us -> 111 us
  local copies, waits for them, and re-layouts: 360 us -> 119 us
  Pallas kernels: 0 us -> 128 us
  blocking collectives: 83.2 us -> 0 us
  other arithmetic: 161 us -> 88.8 us
  starting transfers between devices: 1.85 us -> 72.3 us
    all_gather x12 -> x1, waiting for transfers between devices: 1070 us -> 0.01 us  [per_device(): text_every = lax.all_gather(text_rel, 'dp', axis=0, tiled=True)]
    dot_general x136 -> x21, matrix products: 781 us -> 111 us  [the longest x18 108 us: mxu(): return lax.dot_general(a, b, (dims, ((), ())), preferred_element_type=F32)]
    reduce_scatter x9 -> x5, waiting for transfers between devices: 697 us -> 31.3 us  [reduce_rows(): lax.psum_scatter(term.astype(BF16), 'dp', scatter_dimension=0, tiled=True)]
    unnamed x31 -> x6, waiting for transfers between devices: 533 us -> 0.1 us
    ppermute x0 -> x46, waiting for transfers between devices: none -> 459 us  [swap(): lax.ppermute(value, self.axis, [(i, i ^ mask) for i in range(self.size)])]
    dynamic_slice x193 -> x15, local copies, waits for them, and re-layouts: 168 us -> 27.2 us  [the longest x2 11.6 us: gather_columns(): lax.dynamic_index_in_dim(got, xs.me ^ k, 0, keepdims=False)]
    pallas_call x0 -> x6, Pallas kernels: none -> 128 us  [the longest x1 70.8 us: attn_bwd(): pl.pallas_call(functools.partial(attn_bwd_kernel, **sizes), grid_spec=plt...]
    reduce_sum x32 -> x14, other arithmetic: 104 us -> 10.4 us  [the longest x4 4.49 us: unit_back(): jnp.mean(grad_unit * unit, axis=-1, keepdims=True)]
  transfers between devices with their start and end apart: 26 -> 54, of which waited for: 17 -> 26; matrix products, arithmetic and copies ran while one was open for 34% -> 21% of each run, Pallas kernels for 0% -> 8%
where the time goes in v1:
time: 1050 us; the launch traced here: 1040 us
  waiting for transfers between devices  504 us (48%)
  Pallas kernels  128 us (12%)
  local copies, waits for them, and re-layouts  119 us (11%)
  matrix products  111 us (11%)
  other arithmetic  88.8 us (8%)
  starting transfers between devices  72.3 us (7%)
  between operations  16.5 us (2%)
    ppermute x46, waiting for transfers between devices, swap(): lax.ppermute(value, self.axis, [(i, i ^ mask) for i in range(self.size)])  459 us
    dot_general x18, matrix products, mxu(): return lax.dot_general(a, b, (dims, ((), ())), preferred_element_type=F32)  108 us
    pallas_call x1, Pallas kernels, attn_bwd(): pl.pallas_call(functools.partial(attn_bwd_kernel, **sizes), grid_spec=plt...  70.8 us
    ppermute x46, starting transfers between devices, swap(): lax.ppermute(value, self.axis, [(i, i ^ mask) for i in range(self.size)])  64.4 us
    pallas_call x1, Pallas kernels, attn_fwd(): pl.pallas_call(functools.partial(attn_fwd_kernel, **sizes), grid_spec=plt...  43.4 us
    reduce_scatter x5, waiting for transfers between devices, reduce_rows(): lax.psum_scatter(term.astype(BF16), 'dp', scatter_dimension=0, tiled=True)  31.3 us
    unnamed x229, local copies, waits for them, and re-layouts  28.4 us
  transfers between devices with their start and end apart: 54, of which 26 were waited for; matrix products, arithmetic and copies ran while one was open for 21% of the time, Pallas kernels for 8%

profile of v1, /device:TPU:0, one launch (start us, length us, event | category | flops | bytes accessed | tf_op | source)
XLA Modules:
  0.0 1038.8 jit_solution(5131263933236694576)
XLA Ops:
  15.9 10.3 copy.123
  48.8 25.6 %collective-permute-done.2 = f32[2,6144]{1,0:T(2,128)S(1)} collective-permute-done((f32[2,6144]{1,0:T(2,128)S(1)}, f32[2,6144]{1,0:T(2,128)S(1)}, u32[]{:S(2)}, u32[]{:S(2)}) %collective-permute-start.2) | collective-permute-done | bytes 49184 | tf_op jit(solution)/shard_map/ppermute | solution.py:40
  130.6 20.1 %collective-permute-done.9 = bf16[2,2,288,192]{3,2,1,0:T(8,128)(2,1)S(1)} collective-permute-done((bf16[2,2,288,192]{3,2,1,0:T(8,128)(2,1)S(1)}, bf16[2,2,288,192]{3,2,1,0:T(8,128)(2,1)S(1)}, u32[]{:S(2)}, u32[]{:S(2)}) %collective-permute-start.9) | collective-permute-done | bytes 442400 | tf_op jit(solution)/shard_map/ppermute | solution.py:40
  150.7 19.5 %collective-permute-done.10 = bf16[2,2,288,192]{3,2,1,0:T(8,128)(2,1)S(1)} collective-permute-done((bf16[2,2,288,192]{3,2,1,0:T(8,128)(2,1)S(1)}, bf16[2,2,288,192]{3,2,1,0:T(8,128)(2,1)S(1)}, u32[]{:S(2)}, u32[]{:S(2)}) %collective-permute-start.10) | collective-permute-done | bytes 442400 | tf_op jit(solution)/shard_map/ppermute | solution.py:40
  172.4 45.8 %collective-permute-done.12 = bf16[4,2,2,288,192]{4,3,2,1,0:T(8,128)(2,1)S(1)} collective-permute-done((bf16[4,2,2,288,192]{4,3,2,1,0:T(8,128)(2,1)S(1)}, bf16[4,2,2,288,192]{4,3,2,1,0:T(8,128)(2,1)S(1)}, u32[]{:S(2)}, u32[]{:S(2)}) %collective-permute-start.12) | collective-permute-done | bytes 1769504 | tf_op jit(solution)/shard_map/ppermute | solution.py:40
  226.6 13.3 %collective-permute-start.15 = (bf16[512,192]{1,0:T(8,128)(2,1)S(1)}, bf16[512,192]{1,0:T(8,128)(2,1)S(1)}, u32[]{:S(2)}, u32[]{:S(2)}) collective-permute-start(bf16[512,192]{1,0:T(8,128)(2,1)S(1)} %get-tuple-element.107), channel_id=1, source_target_pairs={{0,16},{2,18},{4,20},{6,22},{8,24},{10,26},{12,28},{14,30},{16,0},... | collective-permute-start | bytes 589832 | tf_op jit(solution)/shard_map/ppermute | solution.py:40
  240.4 17.4 %collective-permute-done.15 = bf16[512,192]{1,0:T(8,128)(2,1)S(1)} collective-permute-done((bf16[512,192]{1,0:T(8,128)(2,1)S(1)}, bf16[512,192]{1,0:T(8,128)(2,1)S(1)}, u32[]{:S(2)}, u32[]{:S(2)}) %collective-permute-start.15) | collective-permute-done | bytes 196640 | tf_op jit(solution)/shard_map/ppermute | solution.py:40
  258.1 9.2 pad_maximum_fusion
  271.9 43.4 %attention.1 = (bf16[4,2,2,128,192]{4,3,2,1,0:T(8,128)(2,1)S(1)}, f32[4,2,2,128,192]{4,3,2,1,0:T(8,128)S(1)}, f32[4,2,2,128,192]{4,3,2,1,0:T(8,128)S(1)}, f32[2,8,2,384]{3,2,1,0:T(2,128)S(1)}) custom-call(s32[2,32]{1,0:T(2,128)S(1)} %convert_reduce_fusion.rank_ref, s32[2,8]{1,0:T(2,128)S(1)} %get-tuple-element.47.start_ref, ...), custom_call_target="tpu_custom_call" | custom-call | flops 10871635968 | bytes 11796480 | tf_op jit(solution)/shard_map/attention/pallas_call | solution.py:437
  326.5 13.2 %collective-permute-done.18 = bf16[512,192]{1,0:T(8,128)(2,1)S(1)} collective-permute-done((bf16[512,192]{1,0:T(8,128)(2,1)S(1)}, bf16[512,192]{1,0:T(8,128)(2,1)S(1)}, u32[]{:S(2)}, u32[]{:S(2)}) %collective-permute-start.18) | collective-permute-done | bytes 196640 | tf_op jit(solution)/shard_map/ppermute | solution.py:40
  341.8 18.8 %collective-permute-done.20 = bf16[256,1536]{1,0:T(8,128)(2,1)S(1)} collective-permute-done((bf16[256,1536]{1,0:T(8,128)(2,1)S(1)}, bf16[256,1536]{1,0:T(8,128)(2,1)S(1)}, u32[]{:S(2)}, u32[]{:S(2)}) %collective-permute-start.20) | collective-permute-done | bytes 786464 | tf_op jit(solution)/shard_map/ppermute | solution.py:40
  363.4 17.6 %collective-permute-done.21 = bf16[256,1536]{1,0:T(8,128)(2,1)S(1)} collective-permute-done((bf16[256,1536]{1,0:T(8,128)(2,1)S(1)}, bf16[256,1536]{1,0:T(8,128)(2,1)S(1)}, u32[]{:S(2)}, u32[]{:S(2)}) %collective-permute-start.21) | collective-permute-done | bytes 786464 | tf_op jit(solution)/shard_map/ppermute | solution.py:40
  384.5 10.0 multiply_convert_fusion.2
  401.6 16.4 %collective-permute-done.22 = bf16[256,1536]{1,0:T(8,128)(2,1)S(1)} collective-permute-done((bf16[256,1536]{1,0:T(8,128)(2,1)S(1)}, bf16[256,1536]{1,0:T(8,128)(2,1)S(1)}, u32[]{:S(2)}, u32[]{:S(2)}) %collective-permute-start.22) | collective-permute-done | bytes 786464 | tf_op jit(solution)/shard_map/ppermute | solution.py:40
  422.0 15.1 %collective-permute-done.23 = bf16[256,1536]{1,0:T(8,128)(2,1)S(1)} collective-permute-done((bf16[256,1536]{1,0:T(8,128)(2,1)S(1)}, bf16[256,1536]{1,0:T(8,128)(2,1)S(1)}, u32[]{:S(2)}, u32[]{:S(2)}) %collective-permute-start.23) | collective-permute-done | bytes 786464 | tf_op jit(solution)/shard_map/ppermute | solution.py:40
  437.1 10.2 multiply_convert_fusion.1
  461.1 13.9 %collective-permute-done.24 = bf16[256,1536]{1,0:T(8,128)(2,1)S(1)} collective-permute-done((bf16[256,1536]{1,0:T(8,128)(2,1)S(1)}, bf16[256,1536]{1,0:T(8,128)(2,1)S(1)}, u32[]{:S(2)}, u32[]{:S(2)}) %collective-permute-start.24) | collective-permute-done | bytes 786464 | tf_op jit(solution)/shard_map/ppermute | solution.py:40
  480.0 12.7 %collective-permute-done.25 = bf16[256,1536]{1,0:T(8,128)(2,1)S(1)} collective-permute-done((bf16[256,1536]{1,0:T(8,128)(2,1)S(1)}, bf16[256,1536]{1,0:T(8,128)(2,1)S(1)}, u32[]{:S(2)}, u32[]{:S(2)}) %collective-permute-start.25) | collective-permute-done | bytes 786464 | tf_op jit(solution)/shard_map/ppermute | solution.py:40
  506.9 8.3 convolution_convert_fusion.2
  531.8 14.7 %collective-permute-done.27 = bf16[512,192]{1,0:T(8,128)(2,1)S(1)} collective-permute-done((bf16[512,192]{1,0:T(8,128)(2,1)S(1)}, bf16[512,192]{1,0:T(8,128)(2,1)S(1)}, u32[]{:S(2)}, u32[]{:S(2)}) %collective-permute-start.27) | collective-permute-done | bytes 196640 | tf_op jit(solution)/shard_map/ppermute | solution.py:40
  546.8 70.8 %attention_back.1 = (bf16[4,2,2,128,192]{4,3,2,1,0:T(8,128)(2,1)S(1)}, bf16[16,2,2,288,192]{4,3,2,1,0:T(8,128)(2,1)}, f32[1,192]{1,0:T(1,128)S(1)}) custom-call(s32[2,32]{1,0:T(2,128)S(1)} %convert_reduce_fusion.rank_ref, s32[2,8]{1,0:T(2,128)S(1)} %get-tuple-element.47.start_ref, s32[2,8]{1,0:T(2,128)S(1)} %get-tuple-element.46.count_ref, ...), custom_call_target="tpu_custom_call" | custom-call | flops 27179089920 | bytes 19660800 | tf_op jit(solution)/shard_map/attention_back/pallas_call | solution.py:474
  625.5 9.1 collective-permute-done.32
  652.3 60.7 %collective-permute-done.33 = bf16[4,2,2,288,192]{4,3,2,1,0:T(8,128)(2,1)} collective-permute-done((bf16[4,2,2,288,192]{4,3,2,1,0:T(8,128)(2,1)}, bf16[4,2,2,288,192]{4,3,2,1,0:T(8,128)(2,1)}, u32[]{:S(2)}, u32[]{:S(2)}) %collective-permute-start.33) | collective-permute-done | bytes 1769504 | tf_op jit(solution)/shard_map/ppermute | solution.py:40
  721.4 15.2 %collective-permute-done.36 = bf16[2,2,288,192]{3,2,1,0:T(8,128)(2,1)S(1)} collective-permute-done((bf16[2,2,288,192]{3,2,1,0:T(8,128)(2,1)S(1)}, bf16[2,2,288,192]{3,2,1,0:T(8,128)(2,1)S(1)}, u32[]{:S(2)}, u32[]{:S(2)}) %collective-permute-start.36) | collective-permute-done | bytes 442400 | tf_op jit(solution)/shard_map/ppermute | solution.py:40
  736.7 36.0 %collective-permute-done.35 = bf16[2,2,288,192]{3,2,1,0:T(8,128)(2,1)S(1)} collective-permute-done((bf16[2,2,288,192]{3,2,1,0:T(8,128)(2,1)S(1)}, bf16[2,2,288,192]{3,2,1,0:T(8,128)(2,1)S(1)}, u32[]{:S(2)}, u32[]{:S(2)}) %collective-permute-start.35) | collective-permute-done | bytes 442400 | tf_op jit(solution)/shard_map/ppermute | solution.py:40
  801.5 45.4 %collective-permute-done.39 = bf16[2,256,3,768]{1,0,3,2:T(2,128)(2,1)S(1)} collective-permute-done((bf16[2,256,3,768]{1,0,3,2:T(2,128)(2,1)}, bf16[2,256,3,768]{1,0,3,2:T(2,128)(2,1)S(1)}, u32[]{:S(2)}, u32[]{:S(2)}) %collective-permute-start.39) | collective-permute-done | bytes 2359328 | tf_op jit(solution)/shard_map/ppermute | solution.py:40
  855.7 13.0 %fusion.21 = (bf16[1,2,256,3,768]{2,1,4,3,0:T(2,128)(2,1)}, bf16[1,2,256,3,768]{2,1,4,3,0:T(2,128)(2,1)}) fusion(s32[]{:T(128)S(6)} %select_n.198, bf16[1,2,256,3,768]{2,1,4,3,0:T(2,128)(2,1)S(1)} %copy-done.44, bf16[1,2,256,3,768]{2,1,4,3,0:T(2,128)(2,1)S(1)} %maximum_bitcast_fusion, s32[]{:T(128)S(6)} %select_n.203), kind=kLoop, calls=%fused_computation.49 | loop fusion | flops 2359296 | bytes 9437192 | tf_op jit(solution)/shard_map/stack | solution.py:881
  885.1 9.3 copy.136
  902.4 8.4 convolution_convert_fusion
  927.0 17.7 %collective-permute-done.37 = bf16[256,1536]{1,0:T(8,128)(2,1)S(1)} collective-permute-done((bf16[256,1536]{1,0:T(8,128)(2,1)S(1)}, bf16[256,1536]{1,0:T(8,128)(2,1)S(1)}, u32[]{:S(2)}, u32[]{:S(2)}) %collective-permute-start.37) | collective-permute-done | bytes 786464 | tf_op jit(solution)/shard_map/ppermute | solution.py:40
  976.4 13.0 %all-to-all-done.1 = bf16[16,64,192]{2,1,0:T(8,128)(2,1)S(1)} async-done(((bf16[16,64,192]{2,1,0:T(8,128)(2,1)}), bf16[16,64,192]{2,1,0:T(8,128)(2,1)S(1)}, u32[]{:S(2)}, u32[]{:S(2)}) %all-to-all-start.1) | async-done | bytes 393248 | tf_op jit(solution)/shard_map/all_to_all | solution.py:897
  998.2 31.3 %reduce-scatter.6.cloned.1.call-done = bf16[288,768]{1,0:T(8,128)(2,1)} async-done(((bf16[4608,768]{1,0:T(8,128)(2,1)}), bf16[288,768]{1,0:T(8,128)(2,1)}) %reduce-scatter.6.cloned.1.call-update) | async-done | bytes 442384 | tf_op jit(solution)/shard_map/reduce_scatter | solution.py:804
  (514 shorter events, 336.9 us)
Async XLA Ops:
  7.2 905.6 %reduce-scatter.8.cloned.1.call-start = ((), (), s32[]{:S(2)}) async-start(), calls=%async_computation.9 | async-start | bytes 2506752 | tf_op jit(solution)/shard_map/reduce_scatter | solution.py:804
  8.2 34.3 %collective-permute-start = (f32[32]{0:T(128)S(1)}, f32[32]{0:T(128)S(1)}, u32[]{:S(2)}, u32[]{:S(2)}) collective-permute-start(f32[32]{0:T(128)S(1)} %get-tuple-element.157), channel_id=1, source_target_pairs={{0,1},{1,0},{2,3},{3,2},{4,5},{5,4},{6,7},{7,6},{8,9},{9,8},{10,11... | collective-permute-start | bytes 392 | tf_op jit(solution)/shard_map/ppermute | solution.py:40
  11.9 36.9 %collective-permute-start.6 = (f32[256]{0:T(256)S(1)}, f32[256]{0:T(256)S(1)}, u32[]{:S(2)}, u32[]{:S(2)}) collective-permute-start(f32[256]{0:T(256)S(1)} %bitcast.475), channel_id=1, source_target_pairs={{0,1},{1,0},{2,3},{3,2},{4,5},{5,4},{6,7},{7,6},{8,9},{9,8},{10,11... | collective-permute-start | bytes 3080 | tf_op jit(solution)/shard_map/ppermute | solution.py:40
  12.7 30.8 %collective-permute-start.1 = (bf16[2,1536]{1,0:T(2,128)(2,1)S(1)}, bf16[2,1536]{1,0:T(2,128)(2,1)S(1)}, u32[]{:S(2)}, u32[]{:S(2)}) collective-permute-start(bf16[2,1536]{1,0:T(2,128)(2,1)S(1)} %fusion.64), channel_id=1, source_target_pairs={{0,1},{1,0},{2,3},{3,2},{4,5},{5,4},{6,7},{7,6},{8,9},{9,8},{10,11... | collective-permute-start | bytes 18440 | tf_op jit(solution)/shard_map/ppermute | solution.py:40
  15.8 63.1 %collective-permute-start.7 = (bf16[32,2048]{1,0:T(8,128)(2,1)S(1)}, bf16[32,2048]{1,0:T(8,128)(2,1)S(1)}, u32[]{:S(2)}, u32[]{:S(2)}) collective-permute-start(bf16[32,2048]{1,0:T(8,128)(2,1)S(1)} %get-tuple-element.116), channel_id=1, source_target_pairs={{0,1},{1,0},{2,3},{3,2},{4,5},{5,4},{6,7},{7,6},{8,9},{9,8},{10,11... | collective-permute-start | bytes 393224 | tf_op jit(solution)/shard_map/ppermute | solution.py:40
  33.9 45.0 %collective-permute-start.4 = (bf16[384,3,768]{2,0,1:T(8,128)(2,1)}, bf16[384,3,768]{2,0,1:T(8,128)(2,1)}, u32[]{:S(2)}, u32[]{:S(2)}) collective-permute-start(bf16[384,3,768]{2,0,1:T(8,128)(2,1)} %bitcast.440), channel_id=1, source_target_pairs={{0,1},{1,0},{2,3},{3,2},{4,5},{5,4},{6,7},{7,6},{8,9},{9,8},{10,11... | collective-permute-start | bytes 5308424 | tf_op jit(solution)/shard_map/ppermute | solution.py:40
  48.7 25.8 %collective-permute-start.2 = (f32[2,6144]{1,0:T(2,128)S(1)}, f32[2,6144]{1,0:T(2,128)S(1)}, u32[]{:S(2)}, u32[]{:S(2)}) collective-permute-start(f32[2,6144]{1,0:T(2,128)S(1)} %slice.311), channel_id=1, source_target_pairs={{0,1},{1,0},{2,3},{3,2},{4,5},{5,4},{6,7},{7,6},{8,9},{9,8},{10,11... | collective-permute-start | bytes 147464 | tf_op jit(solution)/shard_map/ppermute | solution.py:40
  77.2 23.5 %collective-permute-start.3 = (bf16[256,1536]{1,0:T(8,128)(2,1)}, bf16[256,1536]{1,0:T(8,128)(2,1)}, u32[]{:S(2)}, u32[]{:S(2)}) collective-permute-start(bf16[256,1536]{1,0:T(8,128)(2,1)} %fusion.42), channel_id=1, source_target_pairs={{0,1},{1,0},{2,3},{3,2},{4,5},{5,4},{6,7},{7,6},{8,9},{9,8},{10,11... | collective-permute-start | bytes 2359304 | tf_op jit(solution)/shard_map/ppermute | solution.py:40
  78.9 28.3 %collective-permute-start.5 = (bf16[384,3,768]{2,0,1:T(8,128)(2,1)}, bf16[384,3,768]{2,0,1:T(8,128)(2,1)}, u32[]{:S(2)}, u32[]{:S(2)}) collective-permute-start(bf16[384,3,768]{2,0,1:T(8,128)(2,1)} %collective-permute-done.4), channel_id=1, source_target_pairs={{0,2},{2,0},{4,6},{6,4},{8,10},{10,8},{12,14},{14,12},{16,18},{18,... | collective-permute-start | bytes 5308424 | tf_op jit(solution)/shard_map/ppermute | solution.py:40
  126.2 24.6 %collective-permute-start.9 = (bf16[2,2,288,192]{3,2,1,0:T(8,128)(2,1)S(1)}, bf16[2,2,288,192]{3,2,1,0:T(8,128)(2,1)S(1)}, u32[]{:S(2)}, u32[]{:S(2)}) collective-permute-start(bf16[2,2,288,192]{3,2,1,0:T(8,128)(2,1)S(1)} %get-tuple-element.78), channel_id=1, source_target_pairs={{0,8},{2,10},{4,12},{6,14},{8,0},{10,2},{12,4},{14,6},{16,24},{18,... | collective-permute-start | bytes 1327112 | tf_op jit(solution)/shard_map/ppermute | solution.py:40
  127.7 42.4 %collective-permute-start.10 = (bf16[2,2,288,192]{3,2,1,0:T(8,128)(2,1)S(1)}, bf16[2,2,288,192]{3,2,1,0:T(8,128)(2,1)S(1)}, u32[]{:S(2)}, u32[]{:S(2)}) collective-permute-start(bf16[2,2,288,192]{3,2,1,0:T(8,128)(2,1)S(1)} %get-tuple-element.79), channel_id=1, source_target_pairs={{0,16},{2,18},{4,20},{6,22},{8,24},{10,26},{12,28},{14,30},{16,0},... | collective-permute-start | bytes 1327112 | tf_op jit(solution)/shard_map/ppermute | solution.py:40
  130.3 39.9 %collective-permute-start.11 = (bf16[2,2,288,192]{3,2,1,0:T(8,128)(2,1)S(1)}, bf16[2,2,288,192]{3,2,1,0:T(8,128)(2,1)S(1)}, u32[]{:S(2)}, u32[]{:S(2)}) collective-permute-start(bf16[2,2,288,192]{3,2,1,0:T(8,128)(2,1)S(1)} %get-tuple-element.80), channel_id=1, source_target_pairs={{0,24},{2,26},{4,28},{6,30},{8,16},{10,18},{12,20},{14,22},{16,8},... | collective-permute-start | bytes 1327112 | tf_op jit(solution)/shard_map/ppermute | solution.py:40
  170.8 47.3 %collective-permute-start.12 = (bf16[4,2,2,288,192]{4,3,2,1,0:T(8,128)(2,1)S(1)}, bf16[4,2,2,288,192]{4,3,2,1,0:T(8,128)(2,1)S(1)}, u32[]{:S(2)}, u32[]{:S(2)}) collective-permute-start(bf16[4,2,2,288,192]{4,3,2,1,0:T(8,128)(2,1)S(1)} %get-tuple-element.76), channel_id=1, source_target_pairs={{0,4},{2,6},{4,0},{6,2},{8,12},{10,14},{12,8},{14,10},{16,20},{18,... | collective-permute-start | bytes 5308424 | tf_op jit(solution)/shard_map/ppermute | solution.py:40
  222.7 35.4 %collective-permute-start.13 = (bf16[2,4,2,2,288,192]{5,4,3,2,1,0:T(8,128)(2,1)}, bf16[2,4,2,2,288,192]{5,4,3,2,1,0:T(8,128)(2,1)}, u32[]{:S(2)}, u32[]{:S(2)}) collective-permute-start(bf16[2,4,2,2,288,192]{5,4,3,2,1,0:T(8,128)(2,1)} %get-tuple-element.62), channel_id=1, source_target_pairs={{0,2},{2,0},{4,6},{6,4},{8,10},{10,8},{12,14},{14,12},{16,18},{18,... | collective-permute-start | bytes 10616840 | tf_op jit(solution)/shard_map/ppermute | solution.py:40
  226.6 31.2 %collective-permute-start.15 = (bf16[512,192]{1,0:T(8,128)(2,1)S(1)}, bf16[512,192]{1,0:T(8,128)(2,1)S(1)}, u32[]{:S(2)}, u32[]{:S(2)}) collective-permute-start(bf16[512,192]{1,0:T(8,128)(2,1)S(1)} %get-tuple-element.107), channel_id=1, source_target_pairs={{0,16},{2,18},{4,20},{6,22},{8,24},{10,26},{12,28},{14,30},{16,0},... | collective-permute-start | bytes 589832 | tf_op jit(solution)/shard_map/ppermute | solution.py:40
  317.9 21.8 %collective-permute-start.18 = (bf16[512,192]{1,0:T(8,128)(2,1)S(1)}, bf16[512,192]{1,0:T(8,128)(2,1)S(1)}, u32[]{:S(2)}, u32[]{:S(2)}) collective-permute-start(bf16[512,192]{1,0:T(8,128)(2,1)S(1)} %bitcast.466), channel_id=1, source_target_pairs={{0,16},{2,18},{4,20},{6,22},{8,24},{10,26},{12,28},{14,30},{16,0},... | collective-permute-start | bytes 589832 | tf_op jit(solution)/shard_map/ppermute | solution.py:40
  317.9 21.8 %collective-permute-start.17 = (bf16[512,192]{1,0:T(8,128)(2,1)S(1)}, bf16[512,192]{1,0:T(8,128)(2,1)S(1)}, u32[]{:S(2)}, u32[]{:S(2)}) collective-permute-start(bf16[512,192]{1,0:T(8,128)(2,1)S(1)} %bitcast.463), channel_id=1, source_target_pairs={{0,8},{2,10},{4,12},{6,14},{8,0},{10,2},{12,4},{14,6},{16,24},{18,... | collective-permute-start | bytes 589832 | tf_op jit(solution)/shard_map/ppermute | solution.py:40
  496.6 479.8 %all-gather.2.cloned.1.call-start = ((), (), s32[]{:S(2)}) async-start(), calls=%async_computation.8 | async-start | bytes 4456448 | tf_op jit(solution)/shard_map/all_gather | solution.py:898
  498.3 495.4 %reduce-scatter.10.cloned.1.call-start = ((), (), s32[]{:S(2)}) async-start(), calls=%async_computation.10 | async-start | bytes 6684672 | tf_op jit(solution)/shard_map/reduce_scatter | solution.py:804
  506.9 486.9 %reduce-scatter.12.cloned.1.call-start = ((), (), s32[]{:S(2)}) async-start(), calls=%async_computation.11 | async-start | bytes 6684672 | tf_op jit(solution)/shard_map/reduce_scatter | solution.py:804
  515.3 481.0 %reduce-scatter.14.cloned.1.call-start = ((), (), s32[]{:S(2)}) async-start(), calls=%async_computation.12 | async-start | bytes 6684672 | tf_op jit(solution)/shard_map/reduce_scatter | solution.py:804
  520.4 26.1 %collective-permute-start.27 = (bf16[512,192]{1,0:T(8,128)(2,1)S(1)}, bf16[512,192]{1,0:T(8,128)(2,1)S(1)}, u32[]{:S(2)}, u32[]{:S(2)}) collective-permute-start(bf16[512,192]{1,0:T(8,128)(2,1)S(1)} %get-tuple-element.95), channel_id=1, source_target_pairs={{0,16},{2,18},{4,20},{6,22},{8,24},{10,26},{12,28},{14,30},{16,0},... | collective-permute-start | bytes 589832 | tf_op jit(solution)/shard_map/ppermute | solution.py:40
  520.4 26.1 %collective-permute-start.26 = (bf16[512,192]{1,0:T(8,128)(2,1)S(1)}, bf16[512,192]{1,0:T(8,128)(2,1)S(1)}, u32[]{:S(2)}, u32[]{:S(2)}) collective-permute-start(bf16[512,192]{1,0:T(8,128)(2,1)S(1)} %get-tuple-element.96), channel_id=1, source_target_pairs={{0,8},{2,10},{4,12},{6,14},{8,0},{10,2},{12,4},{14,6},{16,24},{18,... | collective-permute-start | bytes 589832 | tf_op jit(solution)/shard_map/ppermute | solution.py:40
  640.1 73.0 %collective-permute-start.33 = (bf16[4,2,2,288,192]{4,3,2,1,0:T(8,128)(2,1)}, bf16[4,2,2,288,192]{4,3,2,1,0:T(8,128)(2,1)}, u32[]{:S(2)}, u32[]{:S(2)}) collective-permute-start(bf16[4,2,2,288,192]{4,3,2,1,0:T(8,128)(2,1)} %slice_bitcast_fusion), channel_id=1, source_target_pairs={{0,4},{2,6},{4,0},{6,2},{8,12},{10,14},{12,8},{14,10},{16,20},{18,... | collective-permute-start | bytes 5308424 | tf_op jit(solution)/shard_map/ppermute | solution.py:40
  646.6 383.0 %reduce-scatter.6.cloned.1.call-start = ((), (), s32[]{:S(2)}) async-start(), calls=%async_computation.7 | async-start | bytes 7520256 | tf_op jit(solution)/shard_map/reduce_scatter | solution.py:804
  647.9 68.7 %collective-permute-start.31 = (bf16[512,192]{1,0:T(8,128)(2,1)S(1)}, bf16[512,192]{1,0:T(8,128)(2,1)S(1)}, u32[]{:S(2)}, u32[]{:S(2)}) collective-permute-start(bf16[512,192]{1,0:T(8,128)(2,1)S(1)} %bitcast.459), channel_id=1, source_target_pairs={{0,24},{2,26},{4,28},{6,30},{8,16},{10,18},{12,20},{14,22},{16,8},... | collective-permute-start | bytes 589832 | tf_op jit(solution)/shard_map/ppermute | solution.py:40
  649.4 71.4 %collective-permute-start.30 = (bf16[512,192]{1,0:T(8,128)(2,1)S(1)}, bf16[512,192]{1,0:T(8,128)(2,1)S(1)}, u32[]{:S(2)}, u32[]{:S(2)}) collective-permute-start(bf16[512,192]{1,0:T(8,128)(2,1)S(1)} %bitcast.456), channel_id=1, source_target_pairs={{0,16},{2,18},{4,20},{6,22},{8,24},{10,26},{12,28},{14,30},{16,0},... | collective-permute-start | bytes 589832 | tf_op jit(solution)/shard_map/ppermute | solution.py:40
  649.4 71.4 %collective-permute-start.29 = (bf16[512,192]{1,0:T(8,128)(2,1)S(1)}, bf16[512,192]{1,0:T(8,128)(2,1)S(1)}, u32[]{:S(2)}, u32[]{:S(2)}) collective-permute-start(bf16[512,192]{1,0:T(8,128)(2,1)S(1)} %bitcast.454), channel_id=1, source_target_pairs={{0,8},{2,10},{4,12},{6,14},{8,0},{10,2},{12,4},{14,6},{16,24},{18,... | collective-permute-start | bytes 589832 | tf_op jit(solution)/shard_map/ppermute | solution.py:40
  716.4 56.2 %collective-permute-start.35 = (bf16[2,2,288,192]{3,2,1,0:T(8,128)(2,1)S(1)}, bf16[2,2,288,192]{3,2,1,0:T(8,128)(2,1)S(1)}, u32[]{:S(2)}, u32[]{:S(2)}) collective-permute-start(bf16[2,2,288,192]{3,2,1,0:T(8,128)(2,1)S(1)} %get-tuple-element.73), channel_id=1, source_target_pairs={{0,16},{2,18},{4,20},{6,22},{8,24},{10,26},{12,28},{14,30},{16,0},... | collective-permute-start | bytes 1327112 | tf_op jit(solution)/shard_map/ppermute | solution.py:40
  716.5 56.1 %collective-permute-start.34 = (bf16[2,2,288,192]{3,2,1,0:T(8,128)(2,1)S(1)}, bf16[2,2,288,192]{3,2,1,0:T(8,128)(2,1)S(1)}, u32[]{:S(2)}, u32[]{:S(2)}) collective-permute-start(bf16[2,2,288,192]{3,2,1,0:T(8,128)(2,1)S(1)} %get-tuple-element.74), channel_id=1, source_target_pairs={{0,8},{2,10},{4,12},{6,14},{8,0},{10,2},{12,4},{14,6},{16,24},{18,... | collective-permute-start | bytes 1327112 | tf_op jit(solution)/shard_map/ppermute | solution.py:40
  793.7 53.2 %collective-permute-start.39 = (bf16[2,256,3,768]{1,0,3,2:T(2,128)(2,1)}, bf16[2,256,3,768]{1,0,3,2:T(2,128)(2,1)S(1)}, u32[]{:S(2)}, u32[]{:S(2)}) collective-permute-start(bf16[2,256,3,768]{1,0,3,2:T(2,128)(2,1)} %reshape.842), channel_id=1, source_target_pairs={{0,1},{1,0},{2,3},{3,2},{4,5},{5,4},{6,7},{7,6},{8,9},{9,8},{10,11... | collective-permute-start | bytes 7077896 | tf_op jit(solution)/shard_map/ppermute | solution.py:40
  962.8 26.6 %all-to-all-start.1 = ((bf16[16,64,192]{2,1,0:T(8,128)(2,1)}), bf16[16,64,192]{2,1,0:T(8,128)(2,1)S(1)}, u32[]{:S(2)}, u32[]{:S(2)}) async-start(bf16[16,64,192]{2,1,0:T(8,128)(2,1)} %copy.140), calls=%async_computation.2 | async-start | bytes 1048576 | tf_op jit(solution)/shard_map/all_to_all | solution.py:897
  (136 other events, 2140.2 us)
Sparse Core Ops, SparseCore 0:
  496.7 64.9 reduce-scatter.7
  564.1 49.7 all-gather.1
  618.3 134.5 reduce-scatter.9
  756.7 83.9 reduce-scatter.11
  845.1 84.3 reduce-scatter.13
  933.3 96.2 reduce-scatter.5

commit v2 on v1

v2 whole, which is shorter than its diff:
```python
import functools
import math

import jax
import jax.numpy as jnp
import numpy as np
from jax import lax
from jax.experimental import pallas as pl
from jax.experimental.pallas import tpu as pltpu
from jax.sharding import PartitionSpec as P

HD = 64
CTX = 256
FRAME_TOK = 128
PW = 16
EPSILON = 1e-06
GROUP_HEADS = 3
GROUP_WIDTH = GROUP_HEADS * HD
STACK = GROUP_HEADS * FRAME_TOK
ONES_ROWS = 16
HIGHEST = lax.Precision.HIGHEST
BF16 = jnp.bfloat16
F32 = jnp.float32
SCALE = HD ** (-0.5)
EXP2_SCALE = SCALE * math.log2(math.e)
MIB = 1 << 20
COST_CUT = 100


def mxu(a, b, dims=((1,), (0,))):
    return lax.dot_general(a, b, (dims, ((), ())), preferred_element_type=F32)


class Moves:
    def __init__(self, axis, size):
        self.axis = axis
        self.size = size
        self.me = lax.axis_index(axis)

    def swap(self, value, mask):
        return lax.ppermute(value, self.axis, [(i, i ^ mask) for i in range(self.size)])

    def gather(self, value):
        return [value] + [self.swap(value, s) for s in range(1, self.size)]

    def scatter_sum(self, parts):
        total = parts[0].astype(F32)
        for s in range(1, self.size):
            total = total + self.swap(parts[s].astype(BF16), s).astype(F32)
        return total

    def reorder(self, value, axis):
        block = value.shape[axis] // self.size
        return jnp.concatenate(
            [
                lax.dynamic_slice_in_dim(value, (self.me ^ s) * block, block, axis)
                for s in range(self.size)
            ],
            axis,
        )

    def own_block(self, value, axis, s=0):
        block = value.shape[axis] // self.size
        return lax.dynamic_slice_in_dim(value, (self.me ^ s) * block, block, axis)


def lane_tiles(width):
    return -(-width // 128) * 128


def turn(values, cosine, sine):
    lane = lax.broadcasted_iota(jnp.int32, values.shape, 1)
    other = jnp.where(lane % 2 == 0, pltpu.roll(values, 127, 1), pltpu.roll(values, 1, 1))
    return values * cosine + other * sine


def head_means(values, ones):
    total = lax.dot_general(
        values, ones, (((1,), (0,)), ((), ())), precision=HIGHEST, preferred_element_type=F32
    )
    return total * (1.0 / HD)


def joined(pieces, axis):
    return jnp.concatenate(pieces, axis=axis) if len(pieces) > 1 else pieces[0]


def widened(values):
    missing = lane_tiles(values.shape[1]) - values.shape[1]
    if not missing:
        return values
    return jnp.concatenate([values, jnp.zeros((values.shape[0], missing), values.dtype)], axis=1)


def tiles_of(values):
    return [values[:, 128 * t : 128 * (t + 1)] for t in range(values.shape[1] // 128)]


def normed_heads(raw, ones, gain):
    return [x * lax.rsqrt(head_means(x * x, ones) + EPSILON) * gain for x in tiles_of(raw)]


def head_ones():
    lane = np.arange(128) // HD
    return jnp.asarray((lane[:, None] == lane[None, :]).astype(np.float32))


def group_cut(values, g):
    return values[:, GROUP_WIDTH * g : GROUP_WIDTH * (g + 1)]


def packed_frames(values, frames):
    return joined([values[FRAME_TOK * f : FRAME_TOK * (f + 1)] for f in range(frames)], 1)


def call(kernel, name, grid, prefetch, in_specs, out_specs, out_shape, scratch, vmem, flops, moved, args):
    return pl.pallas_call(
        kernel,
        grid_spec=pltpu.PrefetchScalarGridSpec(
            num_scalar_prefetch=prefetch,
            grid=grid,
            in_specs=in_specs,
            out_specs=out_specs,
            scratch_shapes=scratch,
        ),
        out_shape=out_shape,
        compiler_params=pltpu.CompilerParams(
            dimension_semantics=("arbitrary",) * len(grid), vmem_limit_bytes=vmem
        ),
        cost_estimate=pl.CostEstimate(
            flops=int(flops) // COST_CUT, bytes_accessed=int(moved) // COST_CUT, transcendentals=0
        ),
        name=name,
    )(*args)


def whole_spec(shape):
    zeros = (0,) * len(shape)
    return pl.BlockSpec(shape, lambda *_: zeros)


def heads_kernel(
    core_ref,
    x_ref,
    w_ref,
    text_ref,
    cos_ref,
    sin_ref,
    gain_ref,
    ones_ref,
    send_q,
    send_kv,
    keep_q,
    keep_kv,
    *,
    half,
    groups,
    frames,
    own_width,
):
    step = pl.program_id(0)
    tokens = frames * FRAME_TOK
    ones = ones_ref[...]
    parts = []
    for p in range(3):
        raw = widened(mxu(x_ref[0], w_ref[:, own_width * p : own_width * (p + 1)]))
        if p < 2:
            raw = joined(
                [
                    turn(x, cos_ref[0], sin_ref[0])
                    for x in normed_heads(raw, ones, gain_ref[p : p + 1, :])
                ],
                1,
            )
        parts.append(raw.astype(BF16))
    wide = text_ref.shape[2] // 2
    text_key = joined(normed_heads(text_ref[0, :, :wide], ones, gain_ref[2:3, :]), 1).astype(BF16)
    text_value = text_ref[0, :, wide:].astype(BF16)

    def put(q_ref, kv_ref):
        for g in range(groups):
            q_ref[0, g] = packed_frames(group_cut(parts[0], g), frames)
            kv_ref[0, g, :tokens] = joined([group_cut(parts[1], g), group_cut(parts[2], g)], 1)
            kv_ref[0, g, tokens:] = joined([group_cut(text_key, g), group_cut(text_value, g)], 1)

    @pl.when(step < half)
    def _():
        put(send_q, send_kv)

    @pl.when(step >= half)
    def _():
        put(keep_q, keep_kv)


def set_stream(step, core, half):
    other = jnp.where(step < half, 1 - core, core)
    return other * half + step % half


def make_heads(core, x, w_cols, text_raw, cosine, sine, gains, groups):
    streams, tokens, width = x.shape
    half = streams // 2
    frames = tokens // FRAME_TOK
    own_width = w_cols.shape[1] // 3
    text_own = text_raw.shape[1]
    by_stream = lambda i, core: (set_stream(i, core[0], half), 0, 0)
    q_block = (1, groups, FRAME_TOK, frames * GROUP_WIDTH)
    kv_block = (1, groups, tokens + text_own, 2 * GROUP_WIDTH)
    first = lambda i, core: (jnp.minimum(i, half - 1), 0, 0, 0)
    second = lambda i, core: (jnp.maximum(i - half, 0), 0, 0, 0)
    return call(
        functools.partial(
            heads_kernel, half=half, groups=groups, frames=frames, own_width=own_width
        ),
        "make_heads",
        (streams,),
        1,
        [
            pl.BlockSpec((1, tokens, width), by_stream),
            whole_spec(w_cols.shape),
            pl.BlockSpec((1,) + text_raw.shape[1:], by_stream),
            pl.BlockSpec((1, tokens, 128), by_stream),
            pl.BlockSpec((1, tokens, 128), by_stream),
            whole_spec((8, 128)),
            whole_spec((128, 128)),
        ],
        [
            pl.BlockSpec(q_block, first),
            pl.BlockSpec(kv_block, first),
            pl.BlockSpec(q_block, second),
            pl.BlockSpec(kv_block, second),
        ],
        [
            jax.ShapeDtypeStruct((half,) + q_block[1:], BF16),
            jax.ShapeDtypeStruct((half,) + kv_block[1:], BF16),
        ]
        * 2,
        [],
        48 * MIB,
        2 * x.size * w_cols.shape[1],
        x.size * 2 + w_cols.size * 2 + x.size * 3,
        (core, x, w_cols, text_raw, cosine, sine, gains, head_ones()),
    )


BIG = 4


def over_tiles(start, count, body):
    big = count // BIG

    def big_step(t, carry):
        body(pl.multiple_of((start + t * BIG) * FRAME_TOK, FRAME_TOK), BIG * FRAME_TOK)
        return carry

    def small_step(t, carry):
        body(pl.multiple_of((start + big * BIG + t) * FRAME_TOK, FRAME_TOK), FRAME_TOK)
        return carry

    lax.fori_loop(0, big, big_step, 0)
    lax.fori_loop(0, count - big * BIG, small_step, 0)


def stacked(values, mask):
    return jnp.concatenate([values] * GROUP_HEADS, axis=0) * mask


def diagonal(values):
    own = [
        values[HD * h : HD * (h + 1), FRAME_TOK * h : FRAME_TOK * (h + 1)]
        for h in range(GROUP_HEADS)
    ]
    return jnp.transpose(jnp.concatenate(own, axis=0))


def head_row(values):
    flipped = jnp.transpose(values)
    return jnp.concatenate(
        [
            jnp.sum(flipped[HD * h : HD * (h + 1), :], axis=0, keepdims=True)
            for h in range(GROUP_HEADS)
        ],
        axis=1,
    )


def each_chunk(kv_refs, rank_ref, place_ref, s, frames, chunk_text, self_rows, frame_body, text_body):
    tokens = frames * FRAME_TOK
    for i, ref in enumerate(kv_refs):

        def one(c, carry, i=i, ref=ref):
            chunk = 2 * i + c
            for f in range(frames):
                at = pl.multiple_of(rank_ref[s, chunk * frames + f] * FRAME_TOK, FRAME_TOK)
                frame_body(ref, c, slice(f * FRAME_TOK, (f + 1) * FRAME_TOK), at)
            at = pl.multiple_of(self_rows + place_ref[chunk] * chunk_text, chunk_text)
            text_body(ref, c, slice(tokens, tokens + chunk_text), at)
            return carry

        lax.fori_loop(0, 2, one, 0)


def unpack_frames(refs, scratch, frames):
    for i, ref in enumerate(refs):
        for c in range(2):
            for f in range(frames):
                scratch[(2 * i + c) * frames + f] = ref[
                    c, :, GROUP_WIDTH * f : GROUP_WIDTH * (f + 1)
                ]


def attn_fwd_kernel(*refs, pieces, groups, frames, chunk_text):
    rank_ref, start_ref, count_ref, clip_ref, place_ref = refs[:5]
    refs = refs[5:]
    kv_refs, refs = refs[:pieces], refs[pieces:]
    q_refs, refs = refs[:groups], refs[groups:]
    gate_ref, mask_ref = refs[:2]
    mixed_refs, refs = refs[2 : 2 + groups], refs[2 + groups :]
    self_ref, text_ref, lse_ref, keys, values, rows_text, queries, mixes, acc = refs
    s = pl.program_id(0)
    j = pl.program_id(1)
    self_rows = pieces * 2 * frames * FRAME_TOK
    text_rows = rows_text.shape[0]
    K = slice(0, GROUP_WIDTH)
    V = slice(GROUP_WIDTH, 2 * GROUP_WIDTH)

    @pl.when(j == 0)
    def _():
        values[GROUP_WIDTH:, :] = jnp.ones((ONES_ROWS, values.shape[1]), BF16)

        def frame_body(ref, c, rows, at):
            keys[pl.ds(at, FRAME_TOK), :] = ref[c, rows, K]
            values[:GROUP_WIDTH, pl.ds(at, FRAME_TOK)] = jnp.transpose(ref[c, rows, V])

        def text_body(ref, c, rows, at):
            keys[pl.ds(at, chunk_text), :] = ref[c, rows, K]
            rows_text[pl.ds(at - self_rows, chunk_text), :] = ref[c, rows, V]

        each_chunk(
            kv_refs, rank_ref, place_ref, s, frames, chunk_text, self_rows, frame_body, text_body
        )
        for b in range(text_rows // 128):
            values[:GROUP_WIDTH, self_rows + 128 * b : self_rows + 128 * (b + 1)] = jnp.transpose(
                rows_text[128 * b : 128 * (b + 1), :]
            )
        unpack_frames(q_refs, queries, frames)

    query = stacked(queries[j], mask_ref[...])

    def tile(base, size):
        scores = mxu(keys[pl.ds(base, size), :], query, ((1,), (1,)))
        weights = jnp.exp2(scores * EXP2_SCALE).astype(BF16)
        acc[...] += mxu(values[:, pl.ds(base, size)], weights)

    def finish(row):
        total = acc[GROUP_WIDTH : GROUP_WIDTH + 1, :]
        lse_ref[0, 0, row : row + 1, :] = jnp.log(total) * math.log2(math.e)
        return diagonal(acc[:GROUP_WIDTH, :] * (1.0 / total))

    acc[...] = jnp.zeros_like(acc)
    over_tiles(start_ref[s, j], count_ref[s, j], tile)
    self_out = finish(0)
    acc[...] = jnp.zeros_like(acc)
    tile(pl.multiple_of(self_rows + clip_ref[s, j] * CTX, 128), CTX)
    text_out = finish(1)
    self_ref[0, 0] = self_out
    text_ref[0, 0] = text_out
    mixes[j] = (self_out + gate_ref[...] * text_out).astype(BF16)

    @pl.when(j == pl.num_programs(1) - 1)
    def _():
        for g, ref in enumerate(mixed_refs):
            for c in range(2):
                at = (2 * g + c) * frames
                ref[c] = joined([mixes[at + f] for f in range(frames)], 1)


def attn_bwd_kernel(*refs, pieces, groups, frames, chunk_text):
    rank_ref, start_ref, count_ref, clip_ref, place_ref = refs[:5]
    refs = refs[5:]
    kv_refs, refs = refs[:pieces], refs[pieces:]
    q_refs, refs = refs[:groups], refs[groups:]
    grad_refs, refs = refs[:groups], refs[groups:]
    self_ref, text_ref, lse_ref, gate_ref, mask_ref, dq_ref = refs[:6]
    dkv_refs, refs = refs[6 : 6 + pieces], refs[6 + pieces :]
    dgate_ref, keys, keys_flip, values, dkeys, dvalues, dquery, queries, grads = refs
    s = pl.program_id(0)
    j = pl.program_id(1)
    self_rows = pieces * 2 * frames * FRAME_TOK
    text_rows = pieces * 2 * chunk_text
    K = slice(0, GROUP_WIDTH)
    V = slice(GROUP_WIDTH, 2 * GROUP_WIDTH)

    @pl.when(jnp.logical_and(s == 0, j == 0))
    def _():
        dgate_ref[...] = jnp.zeros_like(dgate_ref)

    @pl.when(j == 0)
    def _():
        dkeys[...] = jnp.zeros_like(dkeys)
        dvalues[...] = jnp.zeros_like(dvalues)

        def frame_body(ref, c, rows, at):
            keys[pl.ds(at, FRAME_TOK), :] = ref[c, rows, K]
            keys_flip[:, pl.ds(at, FRAME_TOK)] = jnp.transpose(ref[c, rows, K])
            values[pl.ds(at, FRAME_TOK), :] = ref[c, rows, V]

        def text_body(ref, c, rows, at):
            keys[pl.ds(at, chunk_text), :] = ref[c, rows, K]
            values[pl.ds(at, chunk_text), :] = ref[c, rows, V]

        each_chunk(
            kv_refs, rank_ref, place_ref, s, frames, chunk_text, self_rows, frame_body, text_body
        )
        for b in range(text_rows // 128):
            rows = slice(self_rows + 128 * b, self_rows + 128 * (b + 1))
            keys_flip[:, rows] = jnp.transpose(keys[rows, :])
        unpack_frames(q_refs, queries, frames)
        unpack_frames(grad_refs, grads, frames)

    mask = mask_ref[...]
    query = stacked(queries[j], mask)
    grad_low = grads[j]
    grad_wide = grad_low.astype(F32)
    grad_text = (grad_wide * gate_ref[...]).astype(BF16)
    text_out = text_ref[0, 0]
    dgate_ref[...] += jnp.sum(grad_wide * text_out, axis=0, keepdims=True)
    dquery[...] = jnp.zeros_like(dquery)

    def over(grad, out, lse):
        grad_stack = stacked(grad, mask)
        delta = head_row(grad.astype(F32) * out)

        def tile(base, size):
            rows = pl.ds(base, size)
            scores = mxu(keys[rows, :], query, ((1,), (1,)))
            weights = jnp.exp2(scores * EXP2_SCALE - lse)
            dweights = mxu(values[rows, :], grad_stack, ((1,), (1,)))
            dscores = (weights * (dweights - delta)).astype(BF16)
            dvalues[rows, :] += mxu(weights.astype(BF16), grad_stack)
            dkeys[rows, :] += mxu(dscores, query)
            dquery[...] += mxu(keys_flip[:, rows], dscores)

        return tile

    over_tiles(start_ref[s, j], count_ref[s, j], over(grad_low, self_ref[0, 0], lse_ref[0, 0, 0:1, :]))
    over(grad_text, text_out, lse_ref[0, 0, 1:2, :])(
        pl.multiple_of(self_rows + clip_ref[s, j] * CTX, 128), CTX
    )
    dq_ref[0, 0] = (diagonal(dquery[...]) * SCALE).astype(BF16)

    @pl.when(j == pl.num_programs(1) - 1)
    def _():
        def frame_body(ref, c, rows, at):
            taken = pl.ds(at, FRAME_TOK)
            ref[c, rows, :] = jnp.concatenate(
                [dkeys[taken, :] * SCALE, dvalues[taken, :]], axis=1
            ).astype(BF16)

        def text_body(ref, c, rows, at):
            taken = pl.ds(at, chunk_text)
            ref[c, rows, :] = jnp.concatenate(
                [dkeys[taken, :] * SCALE, dvalues[taken, :]], axis=1
            ).astype(BF16)

        each_chunk(
            dkv_refs, rank_ref, place_ref, s, frames, chunk_text, self_rows, frame_body, text_body
        )


def attention_specs(kv, query):
    _, streams, chunk_rows, _ = kv[0].shape
    frames = query[0].shape[3] // GROUP_WIDTH
    chunk_text = chunk_rows - frames * FRAME_TOK
    sizes = dict(pieces=len(kv), groups=len(query), frames=frames, chunk_text=chunk_text)
    count = len(query) * 2 * frames
    grid = (streams, count)
    piece = lambda shape: pl.BlockSpec(
        (2, None) + shape, lambda s, j, *_: (0, s, 0, 0), pipeline_mode=pl.Buffered(1)
    )
    kv_spec = piece((chunk_rows, 2 * GROUP_WIDTH))
    q_spec = piece((FRAME_TOK, frames * GROUP_WIDTH))
    tok_spec = pl.BlockSpec((1, 1, FRAME_TOK, GROUP_WIDTH), lambda s, j, *_: (s, j, 0, 0))
    lse_spec = pl.BlockSpec((1, 1, 2, STACK), lambda s, j, *_: (s, j, 0, 0))
    const_specs = [whole_spec((1, GROUP_WIDTH)), whole_spec((STACK, GROUP_WIDTH))]
    return sizes, grid, kv_spec, q_spec, tok_spec, lse_spec, const_specs


def stack_mask():
    head_of_row = np.arange(STACK) // FRAME_TOK
    head_of_lane = np.arange(GROUP_WIDTH) // HD
    return jnp.asarray((head_of_row[:, None] == head_of_lane[None, :]).astype(np.float32), BF16)


def attn_fwd(tables, kv, query, gate):
    sizes, grid, kv_spec, q_spec, tok_spec, lse_spec, const_specs = attention_specs(kv, query)
    total = len(kv) * 2 * kv[0].shape[2]
    text_rows = len(kv) * 2 * sizes["chunk_text"]
    wide = jax.ShapeDtypeStruct(grid + (FRAME_TOK, GROUP_WIDTH), F32)
    got = call(
        functools.partial(attn_fwd_kernel, **sizes),
        "attention",
        grid,
        5,
        [kv_spec] * len(kv) + [q_spec] * len(query) + const_specs,
        [q_spec] * len(query) + [tok_spec, tok_spec, lse_spec],
        [jax.ShapeDtypeStruct(q.shape, BF16) for q in query]
        + [wide, wide, jax.ShapeDtypeStruct(grid + (2, STACK), F32)],
        [
            pltpu.VMEM((total, GROUP_WIDTH), BF16),
            pltpu.VMEM((GROUP_WIDTH + ONES_ROWS, total), BF16),
            pltpu.VMEM((text_rows, GROUP_WIDTH), BF16),
            pltpu.VMEM((grid[1], FRAME_TOK, GROUP_WIDTH), BF16),
            pltpu.VMEM((grid[1], FRAME_TOK, GROUP_WIDTH), BF16),
            pltpu.VMEM((GROUP_WIDTH + ONES_ROWS, STACK), F32),
        ],
        min(60 * MIB, total * 2600 + 16 * MIB),
        grid[0] * grid[1] * STACK * 2304 * GROUP_WIDTH * 8,
        grid[0] * grid[1] * 300000,
        (*tables, *kv, *query, gate, stack_mask()),
    )
    return got[: len(query)], got[len(query) :]


def attn_bwd(tables, kv, query, grad, kept, gate):
    sizes, grid, kv_spec, q_spec, tok_spec, lse_spec, const_specs = attention_specs(kv, query)
    total = len(kv) * 2 * kv[0].shape[2]
    got = call(
        functools.partial(attn_bwd_kernel, **sizes),
        "attention_back",
        grid,
        5,
        [kv_spec] * len(kv)
        + [q_spec] * (2 * len(query))
        + [tok_spec, tok_spec, lse_spec]
        + const_specs,
        [tok_spec] + [kv_spec] * len(kv) + [whole_spec((1, GROUP_WIDTH))],
        [jax.ShapeDtypeStruct(grid + (FRAME_TOK, GROUP_WIDTH), BF16)]
        + [jax.ShapeDtypeStruct(v.shape, BF16) for v in kv]
        + [jax.ShapeDtypeStruct((1, GROUP_WIDTH), F32)],
        [
            pltpu.VMEM((total, GROUP_WIDTH), BF16),
            pltpu.VMEM((GROUP_WIDTH, total), BF16),
            pltpu.VMEM((total, GROUP_WIDTH), BF16),
            pltpu.VMEM((total, GROUP_WIDTH), F32),
            pltpu.VMEM((total, GROUP_WIDTH), F32),
            pltpu.VMEM((GROUP_WIDTH, STACK), F32),
            pltpu.VMEM((grid[1], FRAME_TOK, GROUP_WIDTH), BF16),
            pltpu.VMEM((grid[1], FRAME_TOK, GROUP_WIDTH), BF16),
        ],
        min(62 * MIB, total * 5800 + 16 * MIB),
        grid[0] * grid[1] * STACK * 2304 * GROUP_WIDTH * 20,
        grid[0] * grid[1] * 500000,
        (*tables, *kv, *query, *grad, *kept, gate, stack_mask()),
    )
    return got[0], got[1 : 1 + len(kv)], got[-1]


def for_group(group, groups, body):
    for v in range(groups):

        @pl.when(group == v)
        def _(v=v):
            body(v)


def out_kernel(info_ref, *refs, half, groups, frames):
    own_refs, refs = refs[:groups], refs[groups:]
    other_ref, w_ref, mixed_ref, first_ref, rest_ref = refs
    k = pl.program_id(0)
    here = (k // half) == info_ref[0]

    def fill(v, take):
        for s in range(groups):
            piece = take(s)
            for f in range(frames):
                mixed_ref[0, FRAME_TOK * f : FRAME_TOK * (f + 1), GROUP_WIDTH * (v ^ s) : GROUP_WIDTH * ((v ^ s) + 1)] = piece[
                    :, GROUP_WIDTH * f : GROUP_WIDTH * (f + 1)
                ]

    @pl.when(here)
    def _():
        for_group(info_ref[1], groups, lambda v: fill(v, lambda s: own_refs[s][0, 0]))

    @pl.when(jnp.logical_not(here))
    def _():
        for_group(info_ref[1], groups, lambda v: fill(v, lambda s: other_ref[s, 0]))

    part = mxu(mixed_ref[0], w_ref[...])

    @pl.when(k == 0)
    def _():
        first_ref[...] = part

    @pl.when(k > 0)
    def _():
        rest_ref[0] = part.astype(BF16)


def out_project(info, own, other, w_out, streams, tokens):
    groups = len(own)
    half = streams // 2
    frames = tokens // FRAME_TOK
    own_width, width = w_out.shape
    lanes = frames * GROUP_WIDTH
    return call(
        functools.partial(out_kernel, half=half, groups=groups, frames=frames),
        "out_project",
        (streams,),
        1,
        [pl.BlockSpec((1, 1, FRAME_TOK, lanes), lambda k, _: (0, k % half, 0, 0))] * groups
        + [
            pl.BlockSpec((groups, 1, FRAME_TOK, lanes), lambda k, _: (0, k % half, 0, 0)),
            whole_spec(w_out.shape),
        ],
        [
            pl.BlockSpec((1, tokens, own_width), lambda k, _: (k, 0, 0)),
            whole_spec((tokens, width)),
            pl.BlockSpec((1, tokens, width), lambda k, _: (jnp.maximum(k - 1, 0), 0, 0)),
        ],
        [
            jax.ShapeDtypeStruct((streams, tokens, own_width), BF16),
            jax.ShapeDtypeStruct((tokens, width), F32),
            jax.ShapeDtypeStruct((streams - 1, tokens, width), BF16),
        ],
        [],
        32 * MIB,
        2 * streams * tokens * own_width * width,
        streams * tokens * width * 6 + w_out.size * 2,
        (info, *own, other, w_out),
    )


def out_back_kernel(core_ref, grad_ref, w_ref, send_ref, keep_ref, *, half, groups, frames):
    step = pl.program_id(0)
    grad = mxu(grad_ref[0], w_ref[...], ((1,), (1,))).astype(BF16)

    def put(ref):
        for g in range(groups):
            ref[0, g] = packed_frames(group_cut(grad, g), frames)

    @pl.when(step < half)
    def _():
        put(send_ref)

    @pl.when(step >= half)
    def _():
        put(keep_ref)


def out_back(core, grad, w_out, groups):
    streams, tokens, width = grad.shape
    half = streams // 2
    frames = tokens // FRAME_TOK
    block = (1, groups, FRAME_TOK, frames * GROUP_WIDTH)
    return call(
        functools.partial(out_back_kernel, half=half, groups=groups, frames=frames),
        "out_back",
        (streams,),
        1,
        [
            pl.BlockSpec((1, tokens, width), lambda i, core: (set_stream(i, core[0], half), 0, 0)),
            whole_spec(w_out.shape),
        ],
        [
            pl.BlockSpec(block, lambda i, core: (jnp.minimum(i, half - 1), 0, 0, 0)),
            pl.BlockSpec(block, lambda i, core: (jnp.maximum(i - half, 0), 0, 0, 0)),
        ],
        [jax.ShapeDtypeStruct((half,) + block[1:], BF16)] * 2,
        [],
        32 * MIB,
        2 * streams * tokens * w_out.size,
        streams * tokens * width * 3 + w_out.size * 2,
        (core, grad, w_out),
    )


def proj_back_kernel(*refs, groups, frames, half, chunk_text):
    group_ref, x_ref, w_ref, dq_ref = refs[:4]
    dkv_refs, refs = refs[4 : 4 + groups], refs[4 + groups :]
    cos_ref, sin_ref, gain_ref, ones_ref = refs[:4]
    out_refs, refs = refs[4 : 4 + groups], refs[4 + groups :]
    dw_ref, dgain_ref, dkv, total = refs
    i = pl.program_id(0)
    tokens = frames * FRAME_TOK

    @pl.when(i == 0)
    def _():
        total[...] = jnp.zeros_like(total)
        dgain_ref[...] = jnp.zeros_like(dgain_ref)

    for g, ref in enumerate(dkv_refs):

        @pl.when(i // half == g)
        def _(ref=ref):
            dkv[...] = ref[...]

    ones = ones_ref[...]
    x = jnp.concatenate([x_ref[0, c, 0] for c in range(2)], axis=0)
    raw = mxu(x, w_ref[...])
    key_grad = jnp.concatenate([dkv[c, :tokens, :GROUP_WIDTH] for c in range(2)], axis=0)
    value_grad = jnp.concatenate([dkv[c, :tokens, GROUP_WIDTH:] for c in range(2)], axis=0)
    query_grad = jnp.concatenate([dq_ref[0, n] for n in range(2 * frames)], axis=0)
    turned = jnp.concatenate([query_grad, key_grad], axis=1).astype(F32)
    done = []
    for t, (x_t, dy) in enumerate(zip(tiles_of(raw), tiles_of(turned))):
        dy = turn(dy, cos_ref[0, 0], -sin_ref[0, 0])
        inv = lax.rsqrt(head_means(x_t * x_t, ones) + EPSILON)
        unit = x_t * inv
        lanes = slice(128 * t, 128 * (t + 1))
        dgain_ref[0:1, lanes] += jnp.sum(dy * unit, axis=0, keepdims=True)
        dn = dy * gain_ref[0:1, lanes]
        done.append((inv * (dn - unit * head_means(dn * unit, ones))).astype(BF16))
    grads = jnp.concatenate(done + [value_grad], axis=1)
    total[...] += mxu(grads, x, ((0,), (0,)))

    def put(ref):
        for c in range(2):
            ref[c, :FRAME_TOK, :] = packed_frames(grads[tokens * c : tokens * (c + 1)], frames)
            rows = slice(tokens, tokens + chunk_text)
            text = dkv[c, rows, :]
            lower = chunk_text // 2
            ref[c, FRAME_TOK:, : 4 * GROUP_WIDTH] = jnp.concatenate(
                [text[:lower], text[lower:]], axis=1
            )
            ref[c, FRAME_TOK:, 4 * GROUP_WIDTH :] = jnp.zeros(
                (lower, ref.shape[2] - 4 * GROUP_WIDTH), BF16
            )

    for g, ref in enumerate(out_refs):

        @pl.when(i // half == g)
        def _(ref=ref):
            put(ref)

    @pl.when(i == pl.num_programs(0) - 1)
    def _():
        for b in range(total.shape[1] // 256):
            lanes = slice(256 * b, 256 * (b + 1))
            dw_ref[lanes, :] = jnp.transpose(total[:, lanes]).astype(BF16)


def proj_back(group, x, w_tri, dq, dkv, cosine, sine, gains):
    groups = len(dkv)
    half = x.shape[2]
    tokens, width = x.shape[3:]
    frames = tokens // FRAME_TOK
    chunk_text = dkv[0].shape[2] - tokens
    lanes = frames * 3 * GROUP_WIDTH
    rows = FRAME_TOK + chunk_text // 2
    got = call(
        functools.partial(
            proj_back_kernel, groups=groups, frames=frames, half=half, chunk_text=chunk_text
        ),
        "proj_back",
        (groups * half,),
        1,
        [
            pl.BlockSpec(
                (1, 2, 1, tokens, width), lambda i, g: (g[0] ^ (i // half), 0, i % half, 0, 0)
            ),
            whole_spec(w_tri.shape),
            pl.BlockSpec(
                (1, 2 * frames, FRAME_TOK, GROUP_WIDTH), lambda i, g: (i % half, i // half, 0, 0)
            ),
        ]
        + [
            pl.BlockSpec((2, None) + dkv[0].shape[2:], lambda i, g: (0, i % half, 0, 0))
        ]
        * groups
        + [
            pl.BlockSpec((1, 1, 2 * tokens, 128), lambda i, g: (i // half, i % half, 0, 0)),
            pl.BlockSpec((1, 1, 2 * tokens, 128), lambda i, g: (i // half, i % half, 0, 0)),
            whole_spec(gains.shape),
            whole_spec((128, 128)),
        ],
        [
            pl.BlockSpec(
                (2, None, rows, lanes),
                lambda i, g, n=n: (0, jnp.clip(i - n * half, 0, half - 1), 0, 0),
            )
            for n in range(groups)
        ]
        + [whole_spec((width, 3 * GROUP_WIDTH)), whole_spec((8, 2 * GROUP_WIDTH))],
        [jax.ShapeDtypeStruct((2, half, rows, lanes), BF16)] * groups
        + [
            jax.ShapeDtypeStruct((width, 3 * GROUP_WIDTH), BF16),
            jax.ShapeDtypeStruct((8, 2 * GROUP_WIDTH), F32),
        ],
        [
            pltpu.VMEM(dkv[0].shape[:1] + dkv[0].shape[2:], BF16),
            pltpu.VMEM((3 * GROUP_WIDTH, width), F32),
        ],
        48 * MIB,
        2 * x.size * GROUP_WIDTH * 5,
        x.size * 4 + w_tri.size * 2,
        (group, x, w_tri, dq, *dkv, cosine, sine, gains, head_ones()),
    )
    return got[:groups], got[groups], got[groups + 1]


def in_back_kernel(info_ref, *refs, half, groups, frames, own_width, chunk_text):
    own_refs, refs = refs[:groups], refs[groups:]
    other_ref, w_ref, raw_ref, gain_ref, ones_ref = refs[:5]
    first_ref, rest_ref, text_ref, dgain_ref, grads, texts = refs[5:]
    k = pl.program_id(0)
    here = (k // half) == info_ref[0]
    wide = lane_tiles(own_width)
    lower = chunk_text // 2

    @pl.when(k == 0)
    def _():
        dgain_ref[...] = jnp.zeros_like(dgain_ref)
        texts[...] = jnp.zeros_like(texts)

    def fill(v, take):
        for s in range(groups):
            piece = take(s)
            at = GROUP_WIDTH * (v ^ s)
            for f in range(frames):
                for p in range(3):
                    from_lane = GROUP_WIDTH * (3 * f + p)
                    grads[
                        FRAME_TOK * f : FRAME_TOK * (f + 1),
                        own_width * p + at : own_width * p + at + GROUP_WIDTH,
                    ] = piece[:FRAME_TOK, from_lane : from_lane + GROUP_WIDTH]
            for f in range(2):
                for p in range(2):
                    from_lane = GROUP_WIDTH * (2 * f + p)
                    texts[lower * f : lower * (f + 1), wide * p + at : wide * p + at + GROUP_WIDTH] = piece[
                        FRAME_TOK:, from_lane : from_lane + GROUP_WIDTH
                    ].astype(F32)

    @pl.when(here)
    def _():
        for_group(info_ref[1], groups, lambda v: fill(v, lambda s: own_refs[s][0, 0]))

    @pl.when(jnp.logical_not(here))
    def _():
        for_group(info_ref[1], groups, lambda v: fill(v, lambda s: other_ref[s, 0]))

    part = mxu(grads[...], w_ref[...], ((1,), (1,)))

    @pl.when(k == 0)
    def _():
        first_ref[...] = part

    @pl.when(k > 0)
    def _():
        rest_ref[0] = part.astype(BF16)

    ones = ones_ref[...]
    for t in range(wide // 128):
        lanes = slice(128 * t, 128 * (t + 1))
        x = raw_ref[0, :, lanes]
        dy = texts[:, lanes]
        inv = lax.rsqrt(head_means(x * x, ones) + EPSILON)
        unit = x * inv
        dgain_ref[0:1, :] += jnp.sum(dy * unit, axis=0, keepdims=True)
        dn = dy * gain_ref[2:3, :]
        text_ref[0, :, lanes] = (inv * (dn - unit * head_means(dn * unit, ones))).astype(BF16)
    text_ref[0, :, wide:] = texts[:, wide:].astype(BF16)


def in_back(info, own, other, w_cols, text_raw, gains, tokens):
    streams, chunk_text, text_lanes = text_raw.shape
    groups = len(own)
    half = streams // 2
    frames = tokens // FRAME_TOK
    width = w_cols.shape[0]
    own_width = w_cols.shape[1] // 3
    rows, lanes = own[0].shape[2:]
    return call(
        functools.partial(
            in_back_kernel,
            half=half,
            groups=groups,
            frames=frames,
            own_width=own_width,
            chunk_text=chunk_text,
        ),
        "in_back",
        (streams,),
        1,
        [pl.BlockSpec((1, 1, rows, lanes), lambda k, _: (0, k % half, 0, 0))] * groups
        + [
            pl.BlockSpec((groups, 1, rows, lanes), lambda k, _: (0, k % half, 0, 0)),
            whole_spec(w_cols.shape),
            pl.BlockSpec((1, chunk_text, text_lanes), lambda k, _: (k, 0, 0)),
            whole_spec((8, 128)),
            whole_spec((128, 128)),
        ],
        [
            whole_spec((tokens, width)),
            pl.BlockSpec((1, tokens, width), lambda k, _: (jnp.maximum(k - 1, 0), 0, 0)),
            pl.BlockSpec((1, chunk_text, text_lanes), lambda k, _: (k, 0, 0)),
            whole_spec((8, 128)),
        ],
        [
            jax.ShapeDtypeStruct((tokens, width), F32),
            jax.ShapeDtypeStruct((streams - 1, tokens, width), BF16),
            jax.ShapeDtypeStruct(text_raw.shape, BF16),
            jax.ShapeDtypeStruct((8, 128), F32),
        ],
        [
            pltpu.VMEM((tokens, 3 * own_width), BF16),
            pltpu.VMEM((chunk_text, text_lanes), F32),
        ],
        48 * MIB,
        2 * streams * tokens * w_cols.size,
        streams * tokens * width * 6 + w_cols.size * 2,
        (info, *own, other, w_cols, text_raw, gains, head_ones()),
    )


def weights_kernel(*refs, tiles, streams):
    cut = [refs[streams * n : streams * (n + 1)] for n in range(5)]
    x_refs, g_refs, gate_refs, up_refs, hidden_refs = cut
    out_ref, x_flip, g_flip = refs[5 * streams :]
    i = pl.program_id(0)
    rows = x_refs[0].shape[0]

    @pl.when(i == 0)
    def _():
        for k in range(streams):
            x_flip[:, rows * k : rows * (k + 1)] = jnp.transpose(x_refs[k][...])
            g_flip[:, rows * k : rows * (k + 1)] = jnp.transpose(g_refs[k][...])

    def total(flip, refs):
        right = joined([ref[...] for ref in refs], 0)
        out_ref[...] = mxu(flip[...], right).astype(BF16)

    @pl.when(i < tiles)
    def _():
        total(x_flip, gate_refs)

    @pl.when(jnp.logical_and(i >= tiles, i < 2 * tiles))
    def _():
        total(x_flip, up_refs)

    @pl.when(i >= 2 * tiles)
    def _():
        total(g_flip, hidden_refs)


def ffn_weights(x, g, gate, up, hidden):
    streams = len(x)
    rows, width = x[0].shape
    inner = hidden[0].shape[1]
    tile = min(512, inner)
    tiles = inner // tile
    at = lambda first: pl.BlockSpec(
        (rows, tile), lambda i: (0, jnp.clip(i - first * tiles, 0, tiles - 1))
    )
    return call(
        functools.partial(weights_kernel, tiles=tiles, streams=streams),
        "ffn_weights",
        (3 * tiles,),
        0,
        [whole_spec((rows, width))] * (2 * streams)
        + [at(0)] * streams
        + [at(1)] * streams
        + [at(2)] * streams,
        pl.BlockSpec((width, tile), lambda i: (0, i)),
        jax.ShapeDtypeStruct((width, 3 * inner), BF16),
        [pltpu.VMEM((width, streams * rows), BF16)] * 2,
        56 * MIB,
        6 * streams * rows * width * inner,
        6 * width * inner + 10 * streams * rows * width,
        (*x, *g, *gate, *up, *hidden),
    )


def unit_rms(values):
    inv = lax.rsqrt(jnp.mean(values * values, axis=-1, keepdims=True) + EPSILON)
    return values * inv, inv


def unit_back(grad_unit, unit, inv):
    return inv * (grad_unit - unit * jnp.mean(grad_unit * unit, axis=-1, keepdims=True))


def rope_lanes(frames):
    half = HD // 2
    frame_pairs = HD // 8
    row_pairs = (half - frame_pairs) // 2
    col_pairs = half - frame_pairs - row_pairs
    pair = (np.arange(128) % HD) // 2

    def lanes(first, count):
        freq = 10000.0 ** (-(np.arange(count, dtype=np.float32)) / np.float32(count))
        out = np.zeros((128,), np.float32)
        inside = (pair >= first) & (pair < first + count)
        out[inside] = freq.astype(np.float32)[pair[inside] - first]
        return jnp.asarray(out)[None, :]

    rows = frames.shape[0]
    inner = jnp.arange(rows) % FRAME_TOK
    row_pos = (inner // PW).astype(F32)
    col_pos = (inner % PW).astype(F32)
    angle = (
        frames[:, None] * lanes(0, frame_pairs)
        + row_pos[:, None] * lanes(frame_pairs, row_pairs)
        + col_pos[:, None] * lanes(frame_pairs + row_pairs, col_pairs)
    )
    sign = jnp.asarray(np.where(np.arange(128) % 2 == 0, -1.0, 1.0).astype(np.float32))[None, :]
    return jnp.cos(angle), jnp.sin(angle) * sign


def gain_rows(*gains):
    rows = [jnp.concatenate([g, g]) for g in gains]
    rows += [jnp.zeros((128,), F32)] * (8 - len(rows))
    return jnp.stack(rows)


def pad_parts(values, parts):
    width = values.shape[-1] // parts
    wide = lane_tiles(width)
    if wide == width:
        return values
    cut = values.reshape(values.shape[:-1] + (parts, width))
    cut = jnp.pad(cut, [(0, 0)] * (cut.ndim - 1) + [(0, wide - width)])
    return cut.reshape(values.shape[:-1] + (parts * wide,))


def pick(values, index, axis=0):
    return lax.dynamic_index_in_dim(values, index, axis, keepdims=False)


def beside(value, *others):
    return lax.optimization_barrier((value,) + others)


def held(value, *others):
    return lax.optimization_barrier((value,) + others)[0]


def per_device(
    fsdp,
    dps,
    states,
    cotangent,
    segment_ids,
    frame_ids,
    condition,
    context,
    w_modulate,
    w_qkv,
    w_text_kv,
    w_out,
    w_gate_up,
    w_down,
    gain_attn_in,
    gain_attn_out,
    gain_ffn_in,
    gain_ffn_out,
    gain_query,
    gain_key,
    gain_text_key,
    cross_gate,
):
    xs = Moves("fsdp", fsdp)
    ds = Moves("dp", dps)
    rows_in = states[0]
    tokens, width = rows_in.shape
    frames = tokens // FRAME_TOK
    heads = cross_gate.shape[0]
    own_heads = heads // fsdp
    own_width = own_heads * HD
    groups = own_heads // GROUP_HEADS
    ranks = dps // groups
    rank_bits = ranks.bit_length() - 1
    clips = condition.shape[1]
    text_local = context[0]
    text_own = text_local.shape[0]
    half = fsdp // 2
    group_me = ds.me // ranks
    rank_me = ds.me % ranks
    core = ds.me % 2

    def frame_view(values):
        return values.reshape(frames, FRAME_TOK, values.shape[-1])

    def group_swap(pieces):
        return [pieces[0]] + [ds.swap(pieces[s], s * ranks) for s in range(1, groups)]

    def group_exchange(keep, send, *first):
        other = ds.swap(send, 1)
        pieces = [
            jnp.stack([pick(keep, group_me ^ s, 1), pick(other, group_me ^ s, 1)])
            for s in range(groups)
        ]
        return group_swap([held(piece, *first) for piece in pieces])

    def group_return(pieces):
        own = group_swap(pieces)
        return own, ds.swap(jnp.stack([piece[1] for piece in own]), 1)

    own_frames = segment_ids[0][::FRAME_TOK].astype(F32)
    own_frame_ids = frame_ids[0].reshape(frames, FRAME_TOK)[:, 0].astype(F32)
    met = jnp.stack(xs.gather(jnp.concatenate([own_frames, own_frame_ids])))
    core_info = core.astype(jnp.int32)[None]
    group_info = group_me.astype(jnp.int32)[None]
    both_info = jnp.concatenate([core_info, group_info])

    silu_cond = jax.nn.silu(condition[0]).astype(BF16)
    cond_rel = jnp.concatenate(xs.gather(silu_cond))
    rows = w_qkv.shape[0]
    quarter = rows // 4

    def columns_of(weight, first, count, s):
        return jnp.concatenate(
            [
                lax.dynamic_slice(
                    weight, (first, p * width + (xs.me ^ s) * own_width), (count, own_width)
                )
                for p in range(3)
            ],
            axis=1,
        )

    fetched = []
    for s in range(1, fsdp):
        wanted = columns_of(w_qkv, (ds.me % 4) * quarter, quarter, s)
        wanted, cond_rel = beside(wanted, cond_rel)
        quarters = [(0, xs.swap(wanted, s))]
        for mask in (2, 1):
            quarters += [(m ^ mask, ds.swap(v, mask)) for m, v in quarters]
        fetched += [(s, m, v) for m, v in quarters]
    cond_own = xs.own_block(cond_rel, 1)
    mod_part = mxu(cond_own, w_modulate).reshape(fsdp, clips, -1)
    modulation = mod_part[0]
    for s in range(1, fsdp):
        modulation = modulation + xs.swap(mod_part[s], s)

    own_seg = lax.dynamic_slice_in_dim(own_frames, ds.me * frames, frames)
    onehot = (own_seg[:, None] == jnp.arange(clips, dtype=F32)[None, :]).astype(F32)
    per_frame = jnp.dot(onehot, modulation, precision=HIGHEST)[:, None, :]
    scale_attn, gate_attn, scale_ffn, gate_ffn = jnp.split(per_frame, 4, axis=2)

    states_f = frame_view(rows_in)
    unit_in, inv_in = unit_rms(states_f)
    normed = (unit_in * gain_attn_in * (1.0 + scale_attn)).astype(BF16).reshape(tokens, width)
    normed, met, w_there = beside(normed, met, w_qkv)
    normed_all = jnp.stack(xs.gather(normed))
    w_cols = lax.dynamic_update_slice_in_dim(
        jnp.zeros((width, 3 * own_width), BF16), columns_of(w_there, 0, rows, 0), xs.me * rows, 0
    )
    for s, m, v in fetched:
        at = (xs.me ^ s) * rows + ((ds.me % 4) ^ m) * quarter
        w_cols = lax.dynamic_update_slice_in_dim(w_cols, v, at, 0)

    stream_seg = met[:, : own_frames.shape[0]].astype(jnp.int32)
    rel_frame_ids = met[:, own_frames.shape[0] :]
    core_seg = lax.dynamic_slice_in_dim(stream_seg, core * half, half, 0)
    masks = [s * ranks for s in range(groups)]
    for b in reversed(range(1, rank_bits)):
        masks = masks + [m ^ (1 << b) for m in masks]
    place_dev = jnp.stack([ds.me ^ (m ^ c) for m in masks for c in range(2)])
    q_dev = jnp.stack([ds.me ^ (s * ranks ^ c) for s in range(groups) for c in range(2)])
    in_frames = lambda dev: (dev[:, None] * frames + jnp.arange(frames)[None, :]).reshape(-1)
    kv_seg = jnp.take(core_seg, in_frames(place_dev), axis=1)
    q_seg = jnp.take(core_seg, in_frames(q_dev), axis=1)
    order = jnp.arange(kv_seg.shape[1])
    less = kv_seg[:, None, :] < kv_seg[:, :, None]
    tie = (kv_seg[:, None, :] == kv_seg[:, :, None]) & (order[None, None, :] < order[None, :, None])
    kv_rank = jnp.sum((less | tie).astype(jnp.int32), axis=2)
    q_start = jnp.sum((kv_seg[:, None, :] < q_seg[:, :, None]).astype(jnp.int32), axis=2)
    q_count = jnp.sum((kv_seg[:, None, :] == q_seg[:, :, None]).astype(jnp.int32), axis=2)
    tables = (kv_rank, q_start, q_count, jnp.maximum(q_seg, 0), place_dev.astype(jnp.int32))
    cosine, sine = rope_lanes(jnp.repeat(rel_frame_ids, FRAME_TOK, axis=1).reshape(-1))
    cosine = cosine.reshape(fsdp, tokens, 128)
    sine = sine.reshape(fsdp, tokens, 128)

    text_rel = jnp.concatenate(
        [xs.own_block(text_local, 1)]
        + [xs.swap(xs.own_block(text_local, 1, s), s) for s in range(1, fsdp)]
    )
    text_part = mxu(text_rel, w_text_kv).reshape(fsdp, text_own, 2, fsdp, own_width)
    text_raw = pick(text_part, xs.me, 3)
    for s in range(1, fsdp):
        piece = pick(text_part, xs.me ^ s, 3)
        piece = jnp.stack([piece[s ^ k] for k in range(fsdp)])
        text_raw = text_raw + xs.swap(piece.astype(BF16), s).astype(F32)
    text_raw = pad_parts(text_raw.reshape(fsdp, text_own, 2 * own_width), 2)

    gains = gain_rows(gain_query, gain_key, gain_text_key)
    send_q, send_kv, keep_q, keep_kv = make_heads(
        core_info, normed_all, w_cols, text_raw, cosine, sine, gains, groups
    )

    kv = group_exchange(keep_kv, send_kv)
    kv_first = kv[1:]
    for b in reversed(range(1, rank_bits)):
        kv = kv + [ds.swap(v, 1 << b) for v in kv]
    query = group_exchange(keep_q, send_q, *kv_first)
    tanh_gate = jnp.tanh(cross_gate)
    first_head = xs.me * own_heads + group_me * GROUP_HEADS
    gate_row = jnp.repeat(lax.dynamic_slice_in_dim(tanh_gate, first_head, GROUP_HEADS), HD)[None, :]

    mixed, kept = attn_fwd(tables, kv, query, gate_row)
    mixed_own, mixed_other = group_return(mixed)
    mixed_low, mix_first, mix_rest = out_project(
        both_info, mixed_own, mixed_other, w_out, fsdp, tokens
    )

    def swapped_sum(first, rest):
        for s in range(1, fsdp):
            first = first + xs.swap(rest[s - 1], s).astype(F32)
        return first

    late_ids = held(rel_frame_ids, mix_first)
    set_of = lambda values, which: lax.dynamic_slice_in_dim(values, which * half, half, 0)
    near_ids = jnp.stack(
        [set_of(late_ids, core), ds.swap(set_of(late_ids, 1 - core), 1)], axis=1
    )
    far_ids = jnp.stack([near_ids] + [ds.swap(near_ids, s * ranks) for s in range(1, groups)])
    normed_two = jnp.stack(
        [set_of(normed_all, core), ds.swap(set_of(normed_all, 1 - core), 1)]
    )
    late_normed = held(normed_two, *mixed_own)
    text_every = lax.all_gather(held(text_rel, *mixed_own), "dp", axis=0, tiled=True)
    if groups > 1:
        members = [[g * ranks + r for g in range(groups)] for r in range(ranks)]
        normed_group = lax.all_gather(late_normed, "dp", axis_index_groups=members)
    else:
        normed_group = late_normed[None]
    far_cos, far_sin = rope_lanes(jnp.repeat(far_ids.reshape(-1), FRAME_TOK))
    far_shape = (groups, half, 2 * tokens, 128)
    far_cos = far_cos.reshape(far_shape)
    far_sin = far_sin.reshape(far_shape)
    mix_got = [xs.swap(mix_rest[s - 1], s) for s in range(1, fsdp)]
    mix_got = [held(v, far_cos, far_sin) for v in mix_got]
    for v in mix_got:
        mix_first = mix_first + v.astype(F32)
    mixed_out = frame_view(mix_first)
    unit_mix, inv_mix = unit_rms(mixed_out)
    tanh_attn = jnp.tanh(gate_attn)
    after = states_f + tanh_attn * unit_mix * gain_attn_out
    unit_ffn, inv_ffn = unit_rms(after)
    ffn_low = (unit_ffn * gain_ffn_in * (1.0 + scale_ffn)).astype(BF16).reshape(tokens, width)
    ffn_all = xs.gather(ffn_low)
    gate_part = [mxu(x, w_gate_up[0]) for x in ffn_all]
    up_part = [mxu(x, w_gate_up[1]) for x in ffn_all]
    hidden = [(jax.nn.silu(g) * u).astype(BF16) for g, u in zip(gate_part, up_part)]
    ffn_out = swapped_sum(
        mxu(hidden[0], w_down), [mxu(h, w_down).astype(BF16) for h in hidden[1:]]
    )
    ffn_out = frame_view(ffn_out)
    unit_out, inv_out = unit_rms(ffn_out)
    tanh_ffn = jnp.tanh(gate_ffn)
    output = after + tanh_ffn * unit_out * gain_ffn_out

    def frame_sum(values):
        return jnp.sum(values, axis=1)

    cot = frame_view(cotangent[0])
    cot_unit = frame_sum(cot * unit_out)
    grad_gate_ffn = cot_unit * gain_ffn_out * (1.0 - tanh_ffn[:, 0] ** 2)
    grad_gain_ffn_out = jnp.sum(cot_unit * tanh_ffn[:, 0], axis=0)
    grad_ffn_low = (
        unit_back(cot * (tanh_ffn * gain_ffn_out), unit_out, inv_out)
        .astype(BF16)
        .reshape(tokens, width)
    )
    grad_ffn_all = xs.gather(grad_ffn_low)
    grad_gate = []
    grad_up = []
    for g, u, d in zip(gate_part, up_part, grad_ffn_all):
        grad_hidden = mxu(d, w_down, ((1,), (1,)))
        sig = jax.nn.sigmoid(g)
        grad_gate.append((grad_hidden * u * (sig * (1.0 + g * (1.0 - sig)))).astype(BF16))
        grad_up.append((grad_hidden * (g * sig)).astype(BF16))

    def ffn_in_part(s):
        return mxu(grad_gate[s], w_gate_up[0], ((1,), (1,))) + mxu(
            grad_up[s], w_gate_up[1], ((1,), (1,))
        )

    def reduce_rows(term):
        return lax.psum_scatter(term, "dp", scatter_dimension=0, tiled=True).astype(F32)

    ffn_rest = [xs.swap(ffn_in_part(s).astype(BF16), s) for s in range(1, fsdp)]
    ffn_grads = ffn_weights(ffn_all, grad_ffn_all, grad_gate, grad_up, hidden)
    ffn_grads, grad_ffn_in, *ffn_rest = beside(ffn_grads, ffn_in_part(0), *ffn_rest)
    for v in ffn_rest:
        grad_ffn_in = grad_ffn_in + v.astype(F32)
    grad_ffn_in = frame_view(grad_ffn_in)
    inner = w_down.shape[0]
    ffn_sums = reduce_rows(ffn_grads)
    grad_unit = frame_sum(grad_ffn_in * unit_ffn)
    grad_scale_ffn = grad_unit * gain_ffn_in
    grad_gain_ffn_in = jnp.sum(grad_unit * (1.0 + scale_ffn[:, 0]), axis=0)
    grad_after = cot + unit_back(
        grad_ffn_in * (gain_ffn_in * (1.0 + scale_ffn)), unit_ffn, inv_ffn
    )
    after_unit = frame_sum(grad_after * unit_mix)
    grad_gate_attn = after_unit * gain_attn_out * (1.0 - tanh_attn[:, 0] ** 2)
    grad_gain_attn_out = jnp.sum(after_unit * tanh_attn[:, 0], axis=0)
    grad_mix_low = (
        unit_back(grad_after * (tanh_attn * gain_attn_out), unit_mix, inv_mix)
        .astype(BF16)
        .reshape(tokens, width)
    )
    grad_mix_all = held(jnp.stack(xs.gather(grad_mix_low)), normed_group, text_every)

    send_grad, keep_grad = out_back(core_info, grad_mix_all, w_out, groups)
    grad_group = group_exchange(keep_grad, send_grad)
    out_grad = mxu(
        grad_mix_all.reshape(fsdp * tokens, width),
        mixed_low.reshape(fsdp * tokens, own_width),
        ((0,), (0,)),
    ).astype(BF16)
    out_grad, *grad_group = beside(out_grad, *grad_group)
    dquery, dkv, dgate = attn_bwd(tables, kv, query, grad_group, kept, gate_row)
    for b in range(1, rank_bits):
        count = len(dkv) // 2
        dkv = [
            (dkv[i].astype(F32) + ds.swap(dkv[count + i], 1 << b).astype(F32)).astype(BF16)
            for i in range(count)
        ]

    w_tri = jnp.concatenate(
        [
            lax.dynamic_slice_in_dim(
                w_cols, p * own_width + group_me * GROUP_WIDTH, GROUP_WIDTH, 1
            )
            for p in range(2)
        ],
        axis=1,
    )
    tri_gain = jnp.concatenate([jnp.tile(gain_query, GROUP_HEADS), jnp.tile(gain_key, GROUP_HEADS)])
    tri_gain = jnp.pad(tri_gain[None, :], ((0, 7), (0, 0)))
    proj_pieces, qkv_grad, gain_qk = proj_back(
        group_info,
        normed_group,
        w_tri,
        dquery,
        dkv,
        far_cos,
        far_sin,
        tri_gain,
    )
    per = width // (fsdp * ranks)
    part = qkv_grad.reshape(fsdp, ranks, per, 3 * GROUP_WIDTH)
    parts = []
    for b in range(rank_bits):
        part = part.reshape(fsdp, part.shape[1] // 2, 2, per, 3 * GROUP_WIDTH)
        mine = (rank_me >> b) & 1
        got = ds.swap(pick(part, 1 - mine, 2), 1 << b)
        part = (pick(part, mine, 2).astype(F32) + got.astype(F32)).astype(BF16)
        parts.append(part)
    proj_own = [held(piece, parts[0]) for piece in group_swap(proj_pieces)]
    proj_other = ds.swap(jnp.stack([piece[1] for piece in proj_own]), 1)
    part = part[:, 0]
    part_own = pick(part, xs.me)
    part_sent = [pick(part, xs.me ^ s) for s in range(1, fsdp)]
    proj_other = held(proj_other, part_own, *part_sent)
    in_first, in_rest, grad_text, gain_text = in_back(
        both_info, proj_own, proj_other, w_cols, text_raw, gains, tokens
    )
    part_got = [held(xs.swap(v, s + 1), in_first) for s, v in enumerate(part_sent)]
    part = jnp.stack([part_own] + part_got)
    part = jnp.stack([pick(part, xs.me ^ k) for k in range(fsdp)])
    blocks = jnp.transpose(part.reshape(fsdp, per, 3, GROUP_WIDTH), (2, 0, 1, 3))
    blocks = blocks.reshape(3 * fsdp, per, GROUP_WIDTH)
    in_got = [xs.swap(in_rest[s - 1], s) for s in range(1, fsdp)]
    if groups > 1:
        window = 3 * heads // GROUP_HEADS // groups
        slots = -(-window // groups)
        first_of = lambda target, source: (window * target - source + groups - 1) // groups
        sent = []
        for s in range(groups):
            first = first_of(group_me ^ s, group_me)
            sent.append(
                jnp.stack(
                    [pick(blocks, jnp.clip(first + t, 0, 3 * fsdp - 1)) for t in range(slots)]
                )
            )
        in_got = [held(v, *sent) for v in in_got]
    for v in in_got:
        in_first = in_first + held(v, ffn_sums).astype(F32)
    grad_normed = frame_view(in_first)
    in_unit = frame_sum(grad_normed * unit_in)
    grad_scale_attn = in_unit * gain_attn_in
    grad_gain_attn_in = jnp.sum(in_unit * (1.0 + scale_attn[:, 0]), axis=0)
    grad_input = grad_after + unit_back(
        grad_normed * (gain_attn_in * (1.0 + scale_attn)), unit_in, inv_in
    )
    if groups > 1:
        got = held(jnp.stack(group_swap(sent)), grad_gain_attn_in, grad_scale_attn)
        got = got.reshape(groups * slots, per, GROUP_WIDTH)
        ordered = []
        for k in range(window):
            block = window * group_me + k
            source = block % groups
            slot = block // groups - first_of(group_me, source)
            ordered.append(pick(got, (source ^ group_me) * slots + slot))
        blocks = jnp.stack(ordered)
    columns = jnp.swapaxes(blocks, 0, 1).reshape(per, ranks, 3 * width // dps)
    columns = jnp.swapaxes(columns, 0, 1)
    if ranks <= 4:
        got = jnp.stack(
            [pick(columns, rank_me)]
            + [ds.swap(pick(columns, rank_me ^ m), m) for m in range(1, ranks)]
        )
        got = jnp.stack([pick(got, rank_me ^ r) for r in range(ranks)])
    else:
        got = lax.all_to_all(columns, "dp", 0, 0, tiled=True)
    grad_w_qkv = got.reshape(rows, 3 * width // dps).astype(F32)

    grad_w_gate_up = jnp.stack([ffn_sums[:, :inner], ffn_sums[:, inner : 2 * inner]])
    grad_w_down = jnp.transpose(ffn_sums[:, 2 * inner :])

    out_grad, ffn_sums = beside(out_grad, ffn_sums)
    grad_w_out = jnp.transpose(reduce_rows(out_grad))
    def gather_columns(values, parts):
        wide = values.shape[2] // parts
        cut = values.reshape(fsdp, values.shape[1], parts, wide)[..., :own_width]
        got = [cut]
        for s in range(1, fsdp):
            other = xs.swap(cut, s)
            got.append(jnp.stack([other[s ^ k] for k in range(fsdp)]))
        got = jnp.stack(got)
        whole = jnp.stack([pick(got, xs.me ^ k) for k in range(fsdp)], axis=3)
        return whole.reshape(fsdp * values.shape[1], parts * fsdp * own_width)

    grad_text_all = gather_columns(grad_text, 2)
    text_cols = grad_text_all.shape[1] // dps
    grad_text_cols = jnp.swapaxes(grad_text_all.reshape(fsdp * text_own, dps, text_cols), 0, 1)
    grad_text_cols = lax.all_to_all(grad_text_cols, "dp", 0, 0, tiled=True)
    grad_w_text_kv = mxu(text_every, grad_text_cols.reshape(-1, text_cols), ((0,), (0,)))

    frame_grads = jnp.concatenate(
        [grad_scale_attn, grad_gate_attn, grad_scale_ffn, grad_gate_ffn], axis=1
    )
    clip_grads = jnp.dot(jnp.transpose(onehot), frame_grads, precision=HIGHEST)
    mod_cols = clip_grads.shape[1] // dps
    clip_grads = jnp.swapaxes(clip_grads.reshape(clips, dps, mod_cols), 0, 1)
    clip_grads = jnp.sum(lax.all_to_all(clip_grads, "dp", 0, 0, tiled=True), axis=0)
    clip_rel = jnp.concatenate(xs.gather(clip_grads))
    grad_w_modulate = jnp.dot(jnp.transpose(cond_own.astype(F32)), clip_rel, precision=HIGHEST)
    head_term = jnp.sum(dgate.reshape(GROUP_HEADS, HD), axis=1)
    gate_term = lax.dynamic_update_slice_in_dim(jnp.zeros((heads,), F32), head_term, first_head, 0)
    gate_term = gate_term * (1.0 - tanh_gate * tanh_gate)
    qk_sums = jnp.sum(gain_qk[0].reshape(2, GROUP_HEADS, HD), axis=1)
    small = [
        grad_gain_attn_in,
        grad_gain_attn_out,
        grad_gain_ffn_in,
        grad_gain_ffn_out,
        qk_sums[0],
        qk_sums[1],
        gain_text[0, :HD] + gain_text[0, HD:],
        gate_term,
    ]
    sizes = [v.shape[0] for v in small]
    packed = jnp.concatenate(small)
    packed = jnp.pad(packed, (0, -packed.shape[0] % 1024)).reshape(-1, 128)
    for moves in (ds, xs):
        for b in range(moves.size.bit_length() - 1):
            packed = packed + moves.swap(packed, 1 << b)
    packed = packed.reshape(-1)
    sums = []
    at = 0
    for size in sizes:
        sums.append(packed[at : at + size])
        at += size
    return (
        output.reshape(1, tokens, width),
        grad_input.reshape(1, tokens, width),
        grad_w_modulate,
        grad_w_qkv,
        grad_w_text_kv,
        grad_w_out,
        grad_w_gate_up,
        grad_w_down,
        *sums,
    )


def solution(mesh):
    rows = P("fsdp", "dp", None)
    first = P("fsdp", None)
    split = P("fsdp", "dp")
    return jax.shard_map(
        functools.partial(per_device, mesh.shape["fsdp"], mesh.shape["dp"]),
        mesh=mesh,
        in_specs=(
            rows,
            rows,
            first,
            split,
            P("fsdp", None, None),
            rows,
            first,
            first,
            first,
            first,
            P(None, None, "fsdp"),
            first,
        )
        + (P(),) * 8,
        out_specs=(
            rows,
            rows,
            split,
            split,
            split,
            split,
            P(None, "dp", "fsdp"),
            split,
        )
        + (P(),) * 8,
        check_vma=False,
    )
```

time: 1050 us -> 850 us (0.81)
  waiting for transfers between devices: 504 us -> 348 us
  matrix products: 111 us -> 56.6 us
  Pallas kernels: 128 us -> 177 us
  local copies, waits for them, and re-layouts: 119 us -> 83.4 us
  starting transfers between devices: 72.3 us -> 90.9 us
  other arithmetic: 88.8 us -> 70.2 us
    ppermute x46 -> x66, waiting for transfers between devices: 459 us -> 320 us  [swap(): lax.ppermute(value, self.axis, [(i, i ^ mask) for i in range(self.size)])]
    dot_general x18 -> x16, matrix products: 108 us -> 53.6 us  [mxu(): return lax.dot_general(a, b, (dims, ((), ())), preferred_element_type=F32)]
    pallas_call x6 -> x8, Pallas kernels: 128 us -> 177 us  [call(): pl.pallas_call(kernel, grid_spec=pltpu.PrefetchScalarGridSpec(num_scalar_...]
    ppermute x46 -> x66, starting transfers between devices: 64.4 us -> 83.1 us  [swap(): lax.ppermute(value, self.axis, [(i, i ^ mask) for i in range(self.size)])]
    another operation x3 -> x1, other arithmetic: 18.3 us -> 0.02 us  [gather_columns(): got = jnp.stack(got)]
    dynamic_slice x13 -> x19, local copies, waits for them, and re-layouts: 26.1 us -> 11.7 us  [the longest x14 7.69 us: pick(): return lax.dynamic_index_in_dim(values, index, axis, keepdims=False)]
    reshape x4 -> x2, local copies, waits for them, and re-layouts: 14.2 us -> 1.01 us  [the longest x1 0.69 us: gather_columns(): cut = values.reshape(fsdp, values.shape[1], parts, wide)[..., :own_width]]
    all_to_all x1, waiting for transfers between devices: 13 us -> 0.01 us  [per_device(): grad_text_cols = lax.all_to_all(grad_text_cols, 'dp', 0, 0, tiled=True)]
  transfers between devices with their start and end apart: 54 -> 72, of which waited for: 26 -> 34; matrix products, arithmetic and copies ran while one was open for 21% -> 20% of each run, Pallas kernels for 8% -> 15%
where the time goes in v2:
time: 850 us; the launch traced here: 842 us
  waiting for transfers between devices  348 us (41%)
  Pallas kernels  177 us (21%)
  starting transfers between devices  90.9 us (11%)
  local copies, waits for them, and re-layouts  83.4 us (10%)
  other arithmetic  70.2 us (8%)
  matrix products  56.6 us (7%)
  between operations  16.1 us (2%)
    ppermute x66, waiting for transfers between devices, swap(): lax.ppermute(value, self.axis, [(i, i ^ mask) for i in range(self.size)])  320 us
    pallas_call x8, Pallas kernels, call(): pl.pallas_call(kernel, grid_spec=pltpu.PrefetchScalarGridSpec(num_scalar_...  177 us
    ppermute x66, starting transfers between devices, swap(): lax.ppermute(value, self.axis, [(i, i ^ mask) for i in range(self.size)])  83.1 us
    dot_general x16, matrix products, mxu(): return lax.dot_general(a, b, (dims, ((), ())), preferred_element_type=F32)  53.6 us
    unnamed x282, local copies, waits for them, and re-layouts  36.3 us
    reduce_scatter x2, waiting for transfers between devices, reduce_rows(): lax.psum_scatter(term, 'dp', scatter_dimension=0, tiled=True).astype(F32)  27.2 us
  transfers between devices with their start and end apart: 72, of which 34 were waited for; matrix products, arithmetic and copies ran while one was open for 20% of the time, Pallas kernels for 15%

profile of v2, /device:TPU:0, one launch (start us, length us, event | category | flops | bytes accessed | tf_op | source)
XLA Modules:
  0.0 842.3 jit_solution(17581544777784016500)
XLA Ops:
  21.7 5.2 fusion.86
  55.8 13.9 %collective-permute-done.9 = bf16[2,32,2,768]{3,2,1,0:T(2,128)(2,1)S(1)} collective-permute-done((bf16[2,32,2,768]{3,2,1,0:T(2,128)(2,1)S(1)}, bf16[2,32,2,768]{3,2,1,0:T(2,128)(2,1)S(1)}, u32[]{:S(2)}, u32[]{:S(2)}) %collective-permute-start.9) | collective-permute-done | bytes 196640 | tf_op jit(solution)/shard_map/ppermute | solution.py:41
  78.6 11.3 %make_heads.1 = (bf16[1,4,128,384]{3,2,1,0:T(8,128)(2,1)S(1)}, bf16[1,4,288,384]{3,2,1,0:T(8,128)(2,1)S(1)}, bf16[1,4,128,384]{3,2,1,0:T(8,128)(2,1)S(1)}, bf16[1,4,288,384]{3,2,1,0:T(8,128)(2,1)S(1)}) custom-call(s32[1]{0:T(128)} %bitcast.5.core_ref, bf16[2,256,1536]{2,1,0:T(8,128)(2,1)S(1)} %pad_maximum_fusion.x_ref, ...), custom_call_target="tpu_custom_call" | custom-call | flops 36238784 | bytes 110100 | tf_op jit(solution)/shard_map/make_heads/pallas_call | solution.py:117
  99.1 8.5 %collective-permute-done.13.refs_8_ = bf16[2,1,288,384]{3,2,1,0:T(8,128)(2,1)S(1)} collective-permute-done((bf16[2,1,288,384]{3,2,1,0:T(8,128)(2,1)S(1)}, bf16[2,1,288,384]{3,2,1,0:T(8,128)(2,1)S(1)}, u32[]{:S(2)}, u32[]{:S(2)}) %collective-permute-start.13) | collective-permute-done | bytes 442400 | tf_op jit(solution)/shard_map/ppermute | solution.py:41
  107.6 26.7 %collective-permute-done.12.refs_7_ = bf16[2,1,288,384]{3,2,1,0:T(8,128)(2,1)S(1)} collective-permute-done((bf16[2,1,288,384]{3,2,1,0:T(8,128)(2,1)S(1)}, bf16[2,1,288,384]{3,2,1,0:T(8,128)(2,1)S(1)}, u32[]{:S(2)}, u32[]{:S(2)}) %collective-permute-start.12) | collective-permute-done | bytes 442400 | tf_op jit(solution)/shard_map/ppermute | solution.py:41
  143.8 6.0 collective-permute-start.19
  154.3 5.2 collective-permute-done.16.refs_11_
  159.5 7.4 collective-permute-done.15.refs_10_
  166.9 43.4 %attention.1 = (bf16[2,1,128,384]{3,2,1,0:T(8,128)(2,1)S(1)}, bf16[2,1,128,384]{3,2,1,0:T(8,128)(2,1)S(1)}, bf16[2,1,128,384]{3,2,1,0:T(8,128)(2,1)S(1)}, bf16[2...) custom-call(s32[1,32]{1,0:T(1,128)S(1)} %bitcast.392, ...), custom_call_target="tpu_custom_call" | custom-call | flops 217432720 | bytes 48000 | tf_op jit(solution)/shard_map/attention/pallas_call | solution.py:117
  219.6 5.5 collective-permute-done.23.refs_2_
  257.7 7.0 sine_multiply_fusion
  269.5 5.5 fusion.14
  275.0 12.5 %collective-permute-done.31.refs_1_ = bf16[256,1536]{1,0:T(8,128)(2,1)S(1)} collective-permute-done((bf16[256,1536]{1,0:T(8,128)(2,1)S(1)}, bf16[256,1536]{1,0:T(8,128)(2,1)S(1)}, u32[]{:S(2)}, u32[]{:S(2)}) %collective-permute-start.31) | collective-permute-done | bytes 786464 | tf_op jit(solution)/shard_map/ppermute | solution.py:41
  299.5 13.3 %collective-permute-done.32 = bf16[256,1536]{1,0:T(8,128)(2,1)S(1)} collective-permute-done((bf16[256,1536]{1,0:T(8,128)(2,1)S(1)}, bf16[256,1536]{1,0:T(8,128)(2,1)S(1)}, u32[]{:S(2)}, u32[]{:S(2)}) %collective-permute-start.32) | collective-permute-done | bytes 786464 | tf_op jit(solution)/shard_map/ppermute | solution.py:41
  325.1 10.8 %collective-permute-done.33.refs_3_ = bf16[256,1536]{1,0:T(8,128)(2,1)S(1)} collective-permute-done((bf16[256,1536]{1,0:T(8,128)(2,1)S(1)}, bf16[256,1536]{1,0:T(8,128)(2,1)S(1)}, u32[]{:S(2)}, u32[]{:S(2)}) %collective-permute-start.33) | collective-permute-done | bytes 786464 | tf_op jit(solution)/shard_map/ppermute | solution.py:41
  351.7 19.2 %ffn_weights.1 = bf16[1536,6144]{1,0:T(8,128)(2,1)} custom-call(bf16[256,1536]{1,0:T(8,128)(2,1)} %copy-done.60, bf16[256,1536]{1,0:T(8,128)(2,1)} %copy-done.70, bf16[256,1536]{1,0:T(8,128)(2,1)} %copy-done.61, bf16[256,1536]{1,0:T(8,128)(2,1)} %copy-done.71, bf16[256,2048]{1,0:T(8,128)(2,1)} %copy-done.67, bf16[256,2048]{1,0:T(8,128)(2,1)} %copy-done.69, ...), custom_call_target="tpu_custom_call" | custom-call | flops 96636768 | bytes 267386 | tf_op jit(solution)/shard_map/ffn_weights/pallas_call | solution.py:117
  383.3 15.1 %collective-permute-done.36 = bf16[256,1536]{1,0:T(8,128)(2,1)S(1)} collective-permute-done((bf16[256,1536]{1,0:T(8,128)(2,1)S(1)}, bf16[256,1536]{1,0:T(8,128)(2,1)S(1)}, u32[]{:S(2)}, u32[]{:S(2)}) %collective-permute-start.36) | collective-permute-done | bytes 786464 | tf_op jit(solution)/shard_map/ppermute | solution.py:41
  420.2 10.7 %collective-permute-done.39.refs_19_ = bf16[2,1,128,384]{3,2,1,0:T(8,128)(2,1)} collective-permute-done((bf16[2,1,128,384]{3,2,1,0:T(8,128)(2,1)}, bf16[2,1,128,384]{3,2,1,0:T(8,128)(2,1)}, u32[]{:S(2)}, u32[]{:S(2)}) %collective-permute-start.39) | collective-permute-done | bytes 196640 | tf_op jit(solution)/shard_map/ppermute | solution.py:41
  441.5 63.3 %attention_back.1 = (bf16[1,16,128,192]{3,2,1,0:T(8,128)(2,1)S(1)}, bf16[2,1,288,384]{3,2,1,0:T(8,128)(2,1)S(1)}, bf16[2,1,288,384]{3,2,1,0:T(8,128)(2,1)S(1)}, ...) custom-call(s32[1,32]{1,0:T(1,128)S(1)} %bitcast.393, ...), custom_call_target="tpu_custom_call" | custom-call | flops 543581824 | bytes 80000 | tf_op jit(solution)/shard_map/attention_back/pallas_call | solution.py:117
  513.5 12.7 %collective-permute-done.44 = bf16[2,1,288,384]{3,2,1,0:T(8,128)(2,1)S(1)} collective-permute-done((bf16[2,1,288,384]{3,2,1,0:T(8,128)(2,1)S(1)}, bf16[2,1,288,384]{3,2,1,0:T(8,128)(2,1)S(1)}, u32[]{:S(2)}, u32[]{:S(2)}) %collective-permute-start.44) | collective-permute-done | bytes 442400 | tf_op jit(solution)/shard_map/ppermute | solution.py:41
  526.3 12.9 %collective-permute-done.43 = bf16[2,1,288,384]{3,2,1,0:T(8,128)(2,1)S(1)} collective-permute-done((bf16[2,1,288,384]{3,2,1,0:T(8,128)(2,1)S(1)}, bf16[2,1,288,384]{3,2,1,0:T(8,128)(2,1)S(1)}, u32[]{:S(2)}, u32[]{:S(2)}) %collective-permute-start.43) | collective-permute-done | bytes 442400 | tf_op jit(solution)/shard_map/ppermute | solution.py:41
  539.3 18.5 %collective-permute-done.42 = bf16[2,1,288,384]{3,2,1,0:T(8,128)(2,1)S(1)} collective-permute-done((bf16[2,1,288,384]{3,2,1,0:T(8,128)(2,1)S(1)}, bf16[2,1,288,384]{3,2,1,0:T(8,128)(2,1)S(1)}, u32[]{:S(2)}, u32[]{:S(2)}) %collective-permute-start.42) | collective-permute-done | bytes 442400 | tf_op jit(solution)/shard_map/ppermute | solution.py:41
  557.9 12.7 %collective-permute-done.41 = bf16[2,1,288,384]{3,2,1,0:T(8,128)(2,1)S(1)} collective-permute-done((bf16[2,1,288,384]{3,2,1,0:T(8,128)(2,1)S(1)}, bf16[2,1,288,384]{3,2,1,0:T(8,128)(2,1)S(1)}, u32[]{:S(2)}, u32[]{:S(2)}) %collective-permute-start.41) | collective-permute-done | bytes 442400 | tf_op jit(solution)/shard_map/ppermute | solution.py:41
  570.8 21.6 %proj_back.1 = (bf16[2,1,144,1152]{3,2,1,0:T(8,128)(2,1)S(1)}, bf16[2,1,144,1152]{3,2,1,0:T(8,128)(2,1)}, bf16[2,1,144,1152]{3,2,1,0:T(8,128)(2,1)}, bf16[2,1,14...) custom-call(s32[1]{0:T(128)} %bitcast.6.refs_0_, bf16[4,2,1,256,1536]{4,3,2,1,0:T(8,128)(2,1)} %bitcast.403, ...), custom_call_target="tpu_custom_call" | custom-call | flops 60397976 | bytes 137625 | tf_op jit(solution)/shard_map/proj_back/pallas_call | solution.py:117
  603.0 26.9 %collective-permute-done.48.refs_3_ = bf16[2,1,144,1152]{3,2,1,0:T(8,128)(2,1)S(1)} collective-permute-done((bf16[2,1,144,1152]{3,2,1,0:T(8,128)(2,1)}, bf16[2,1,144,1152]{3,2,1,0:T(8,128)(2,1)S(1)}, u32[]{:S(2)}, u32[]{:S(2)}) %collective-permute-start.48) | collective-permute-done | bytes 663584 | tf_op jit(solution)/shard_map/ppermute | solution.py:41
  629.9 44.2 %collective-permute-done.47.refs_2_ = bf16[2,1,144,1152]{3,2,1,0:T(8,128)(2,1)S(1)} collective-permute-done((bf16[2,1,144,1152]{3,2,1,0:T(8,128)(2,1)}, bf16[2,1,144,1152]{3,2,1,0:T(8,128)(2,1)S(1)}, u32[]{:S(2)}, u32[]{:S(2)}) %collective-permute-start.47) | collective-permute-done | bytes 663584 | tf_op jit(solution)/shard_map/ppermute | solution.py:41
  680.8 10.6 %collective-permute-done.50 = bf16[2,1,192,576]{3,2,1,0:T(8,128)(2,1)} collective-permute-done((bf16[2,1,192,576]{3,2,1,0:T(8,128)(2,1)}, bf16[2,1,192,576]{3,2,1,0:T(8,128)(2,1)}, u32[]{:S(2)}, u32[]{:S(2)}) %collective-permute-start.50) | collective-permute-done | bytes 442400 | tf_op jit(solution)/shard_map/ppermute | solution.py:41
  697.6 11.2 %in_back.1 = (f32[256,1536]{1,0:T(8,128)}, bf16[1,256,1536]{2,1,0:T(8,128)(2,1)S(1)}, bf16[2,32,1536]{2,1,0:T(8,128)(2,1)S(1)}, f32[8,128]{1,0:T(8,128)S(1)}) custom-call(s32[2]{0:T(128)S(1)} %pad_add_fusion.info_ref, bf16[2,1,144,1152]{3,2,1,0:T(8,128)(2,1)S(1)} %get-tuple-element.131.refs_0_, ...), custom_call_target="tpu_custom_call" | custom-call | flops 36238784 | bytes 117964 | tf_op jit(solution)/shard_map/in_back/pallas_call | solution.py:117
  730.5 13.2 %collective-permute-done.56 = bf16[2,192,192]{2,1,0:T(8,128)(2,1)S(1)} collective-permute-done((bf16[2,192,192]{2,1,0:T(8,128)(2,1)S(1)}, bf16[2,192,192]{2,1,0:T(8,128)(2,1)S(1)}, u32[]{:S(2)}, u32[]{:S(2)}) %collective-permute-start.56) | collective-permute-done | bytes 147488 | tf_op jit(solution)/shard_map/ppermute | solution.py:41
  743.7 13.9 %collective-permute-done.55 = bf16[2,192,192]{2,1,0:T(8,128)(2,1)S(1)} collective-permute-done((bf16[2,192,192]{2,1,0:T(8,128)(2,1)S(1)}, bf16[2,192,192]{2,1,0:T(8,128)(2,1)S(1)}, u32[]{:S(2)}, u32[]{:S(2)}) %collective-permute-start.55) | collective-permute-done | bytes 147488 | tf_op jit(solution)/shard_map/ppermute | solution.py:41
  767.3 5.1 multiply_reduce_fusion.2
  806.8 27.2 %reduce-scatter.5.cloned.1.call-done = bf16[96,768]{1,0:T(8,128)(2,1)} async-done(((bf16[1536,768]{1,0:T(8,128)(2,1)}), bf16[96,768]{1,0:T(8,128)(2,1)}) %reduce-scatter.5.cloned.1.call-update) | async-done | bytes 147472 | tf_op jit(solution)/shard_map/reduce_scatter | solution.py:1281
  (639 shorter events, 304.9 us)
Async XLA Ops:
  7.2 392.6 %all-gather.4.cloned.1.call-start = ((), (), s32[]{:S(2)}) async-start(), calls=%async_computation.4 | async-start | bytes 4456448 | tf_op jit(solution)/shard_map/all_gather | solution.py:1222
  13.7 26.2 %collective-permute-start.8 = (bf16[32,2048]{1,0:T(8,128)(2,1)S(1)}, bf16[32,2048]{1,0:T(8,128)(2,1)S(1)}, u32[]{:S(2)}, u32[]{:S(2)}) collective-permute-start(bf16[32,2048]{1,0:T(8,128)(2,1)S(1)} %get-tuple-element.319), channel_id=1, source_target_pairs={{0,1},{1,0},{2,3},{3,2},{4,5},{5,4},{6,7},{7,6},{8,9},{9,8},{10,11... | collective-permute-start | bytes 393224 | tf_op jit(solution)/shard_map/ppermute | solution.py:41
  27.1 23.7 %collective-permute-start.4 = (bf16[192,2304]{1,0:T(8,128)(2,1)}, bf16[192,2304]{1,0:T(8,128)(2,1)}, u32[]{:S(2)}, u32[]{:S(2)}) collective-permute-start(bf16[192,2304]{1,0:T(8,128)(2,1)} %pad_maximum_fusion.6), channel_id=1, source_target_pairs={{0,1},{1,0},{2,3},{3,2},{4,5},{5,4},{6,7},{7,6},{8,9},{9,8},{10,11... | collective-permute-start | bytes 2654216 | tf_op jit(solution)/shard_map/ppermute | solution.py:41
  33.0 37.4 %collective-permute-start.3 = (bf16[256,1536]{1,0:T(8,128)(2,1)S(1)}, bf16[256,1536]{1,0:T(8,128)(2,1)}, u32[]{:S(2)}, u32[]{:S(2)}) collective-permute-start(bf16[256,1536]{1,0:T(8,128)(2,1)S(1)} %fusion.52), channel_id=1, source_target_pairs={{0,1},{1,0},{2,3},{3,2},{4,5},{5,4},{6,7},{7,6},{8,9},{9,8},{10,11... | collective-permute-start | bytes 2359304 | tf_op jit(solution)/shard_map/ppermute | solution.py:41
  50.8 20.9 %collective-permute-start.5 = (bf16[192,2304]{1,0:T(8,128)(2,1)}, bf16[192,2304]{1,0:T(8,128)(2,1)}, u32[]{:S(2)}, u32[]{:S(2)}) collective-permute-start(bf16[192,2304]{1,0:T(8,128)(2,1)} %collective-permute-done.4), channel_id=1, source_target_pairs={{0,4},{2,6},{4,0},{6,2},{8,12},{10,14},{12,8},{14,10},{16,20},{18,... | collective-permute-start | bytes 2654216 | tf_op jit(solution)/shard_map/ppermute | solution.py:41
  96.3 38.0 %collective-permute-start.12 = (bf16[2,1,288,384]{3,2,1,0:T(8,128)(2,1)S(1)}, bf16[2,1,288,384]{3,2,1,0:T(8,128)(2,1)S(1)}, u32[]{:S(2)}, u32[]{:S(2)}) collective-permute-start(bf16[2,1,288,384]{3,2,1,0:T(8,128)(2,1)S(1)} %pad_maximum_fusion.13), channel_id=1, source_target_pairs={{0,16},{2,18},{4,20},{6,22},{8,24},{10,26},{12,28},{14,30},{16,0},... | collective-permute-start | bytes 1327112 | tf_op jit(solution)/shard_map/ppermute | solution.py:41
  96.5 37.9 %collective-permute-start.11 = (bf16[2,1,288,384]{3,2,1,0:T(8,128)(2,1)S(1)}, bf16[2,1,288,384]{3,2,1,0:T(8,128)(2,1)S(1)}, u32[]{:S(2)}, u32[]{:S(2)}) collective-permute-start(bf16[2,1,288,384]{3,2,1,0:T(8,128)(2,1)S(1)} %pad_maximum_fusion.12), channel_id=1, source_target_pairs={{0,8},{2,10},{4,12},{6,14},{8,0},{10,2},{12,4},{14,6},{16,24},{18,... | collective-permute-start | bytes 1327112 | tf_op jit(solution)/shard_map/ppermute | solution.py:41
  97.4 43.1 %collective-permute-start.14 = (bf16[2,1,288,384]{3,2,1,0:T(8,128)(2,1)S(1)}, bf16[2,1,288,384]{3,2,1,0:T(8,128)(2,1)S(1)}, u32[]{:S(2)}, u32[]{:S(2)}) collective-permute-start(bf16[2,1,288,384]{3,2,1,0:T(8,128)(2,1)S(1)} %pad_maximum_fusion.11.refs_5_), channel_id=1, source_target_pairs={{0,4},{2,6},{4,0},{6,2},{8,12},{10,14},{12,8},{14,10},{16,20},{18,... | collective-permute-start | bytes 1327112 | tf_op jit(solution)/shard_map/ppermute | solution.py:41
  138.4 21.1 %collective-permute-start.16 = (bf16[2,1,288,384]{3,2,1,0:T(8,128)(2,1)S(1)}, bf16[2,1,288,384]{3,2,1,0:T(8,128)(2,1)S(1)}, u32[]{:S(2)}, u32[]{:S(2)}) collective-permute-start(bf16[2,1,288,384]{3,2,1,0:T(8,128)(2,1)S(1)} %collective-permute-done.12.refs_7_), channel_id=1, source_target_pairs={{0,4},{2,6},{4,0},{6,2},{8,12},{10,14},{12,8},{14,10},{16,20},{18,... | collective-permute-start | bytes 1327112 | tf_op jit(solution)/shard_map/ppermute | solution.py:41
  139.0 28.0 %collective-permute-start.15 = (bf16[2,1,288,384]{3,2,1,0:T(8,128)(2,1)S(1)}, bf16[2,1,288,384]{3,2,1,0:T(8,128)(2,1)S(1)}, u32[]{:S(2)}, u32[]{:S(2)}) collective-permute-start(bf16[2,1,288,384]{3,2,1,0:T(8,128)(2,1)S(1)} %collective-permute-done.11.refs_6_), channel_id=1, source_target_pairs={{0,4},{2,6},{4,0},{6,2},{8,12},{10,14},{12,8},{14,10},{16,20},{18,... | collective-permute-start | bytes 1327112 | tf_op jit(solution)/shard_map/ppermute | solution.py:41
  225.1 174.7 %all-gather.6.cloned.1.call-start = ((), (), s32[]{:S(2)}) async-start(), calls=%async_computation.7 | async-start | bytes 7864320 | tf_op jit(solution)/shard_map/all_gather | solution.py:1225
  230.6 533.4 %reduce-scatter.3.cloned.1.call-start = ((), (), s32[]{:S(2)}) async-start(), calls=%async_computation.5 | async-start | bytes 20054016 | tf_op jit(solution)/shard_map/reduce_scatter | solution.py:1281
  242.0 22.6 %collective-permute-start.26 = (bf16[256,1536]{1,0:T(8,128)(2,1)}, bf16[256,1536]{1,0:T(8,128)(2,1)}, u32[]{:S(2)}, u32[]{:S(2)}) collective-permute-start(bf16[256,1536]{1,0:T(8,128)(2,1)} %bitcast.46), channel_id=1, source_target_pairs={{0,1},{1,0},{2,3},{3,2},{4,5},{5,4},{6,7},{7,6},{8,9},{9,8},{10,11... | collective-permute-start | bytes 2359304 | tf_op jit(solution)/shard_map/ppermute | solution.py:41
  268.7 18.9 %collective-permute-start.31 = (bf16[256,1536]{1,0:T(8,128)(2,1)S(1)}, bf16[256,1536]{1,0:T(8,128)(2,1)S(1)}, u32[]{:S(2)}, u32[]{:S(2)}) collective-permute-start(bf16[256,1536]{1,0:T(8,128)(2,1)S(1)} %fusion.50.refs_0_), channel_id=1, source_target_pairs={{0,1},{1,0},{2,3},{3,2},{4,5},{5,4},{6,7},{7,6},{8,9},{9,8},{10,11... | collective-permute-start | bytes 2359304 | tf_op jit(solution)/shard_map/ppermute | solution.py:41
  345.4 25.5 %collective-permute-start.34 = (bf16[256,1536]{1,0:T(8,128)(2,1)}, bf16[256,1536]{1,0:T(8,128)(2,1)}, u32[]{:S(2)}, u32[]{:S(2)}) collective-permute-start(bf16[256,1536]{1,0:T(8,128)(2,1)} %fusion.30), channel_id=1, source_target_pairs={{0,1},{1,0},{2,3},{3,2},{4,5},{5,4},{6,7},{7,6},{8,9},{9,8},{10,11... | collective-permute-start | bytes 2359304 | tf_op jit(solution)/shard_map/ppermute | solution.py:41
  410.6 20.3 %collective-permute-start.39 = (bf16[2,1,128,384]{3,2,1,0:T(8,128)(2,1)}, bf16[2,1,128,384]{3,2,1,0:T(8,128)(2,1)}, u32[]{:S(2)}, u32[]{:S(2)}) collective-permute-start(bf16[2,1,128,384]{3,2,1,0:T(8,128)(2,1)} %pad_maximum_fusion.25), channel_id=1, source_target_pairs={{0,16},{2,18},{4,20},{6,22},{8,24},{10,26},{12,28},{14,30},{16,0},... | collective-permute-start | bytes 589832 | tf_op jit(solution)/shard_map/ppermute | solution.py:41
  504.8 21.4 %collective-permute-start.44 = (bf16[2,1,288,384]{3,2,1,0:T(8,128)(2,1)S(1)}, bf16[2,1,288,384]{3,2,1,0:T(8,128)(2,1)S(1)}, u32[]{:S(2)}, u32[]{:S(2)}) collective-permute-start(bf16[2,1,288,384]{3,2,1,0:T(8,128)(2,1)S(1)} %get-tuple-element.128), channel_id=1, source_target_pairs={{0,4},{2,6},{4,0},{6,2},{8,12},{10,14},{12,8},{14,10},{16,20},{18,... | collective-permute-start | bytes 1327112 | tf_op jit(solution)/shard_map/ppermute | solution.py:41
  509.8 29.3 %collective-permute-start.43 = (bf16[2,1,288,384]{3,2,1,0:T(8,128)(2,1)S(1)}, bf16[2,1,288,384]{3,2,1,0:T(8,128)(2,1)S(1)}, u32[]{:S(2)}, u32[]{:S(2)}) collective-permute-start(bf16[2,1,288,384]{3,2,1,0:T(8,128)(2,1)S(1)} %get-tuple-element.126), channel_id=1, source_target_pairs={{0,4},{2,6},{4,0},{6,2},{8,12},{10,14},{12,8},{14,10},{16,20},{18,... | collective-permute-start | bytes 1327112 | tf_op jit(solution)/shard_map/ppermute | solution.py:41
  511.4 46.4 %collective-permute-start.42 = (bf16[2,1,288,384]{3,2,1,0:T(8,128)(2,1)S(1)}, bf16[2,1,288,384]{3,2,1,0:T(8,128)(2,1)S(1)}, u32[]{:S(2)}, u32[]{:S(2)}) collective-permute-start(bf16[2,1,288,384]{3,2,1,0:T(8,128)(2,1)S(1)} %get-tuple-element.124), channel_id=1, source_target_pairs={{0,4},{2,6},{4,0},{6,2},{8,12},{10,14},{12,8},{14,10},{16,20},{18,... | collective-permute-start | bytes 1327112 | tf_op jit(solution)/shard_map/ppermute | solution.py:41
  513.4 57.2 %collective-permute-start.41 = (bf16[2,1,288,384]{3,2,1,0:T(8,128)(2,1)S(1)}, bf16[2,1,288,384]{3,2,1,0:T(8,128)(2,1)S(1)}, u32[]{:S(2)}, u32[]{:S(2)}) collective-permute-start(bf16[2,1,288,384]{3,2,1,0:T(8,128)(2,1)S(1)} %get-tuple-element.122), channel_id=1, source_target_pairs={{0,4},{2,6},{4,0},{6,2},{8,12},{10,14},{12,8},{14,10},{16,20},{18,... | collective-permute-start | bytes 1327112 | tf_op jit(solution)/shard_map/ppermute | solution.py:41
  595.9 34.0 %collective-permute-start.48 = (bf16[2,1,144,1152]{3,2,1,0:T(8,128)(2,1)}, bf16[2,1,144,1152]{3,2,1,0:T(8,128)(2,1)S(1)}, u32[]{:S(2)}, u32[]{:S(2)}) collective-permute-start(bf16[2,1,144,1152]{3,2,1,0:T(8,128)(2,1)} %get-tuple-element.136), channel_id=1, source_target_pairs={{0,24},{2,26},{4,28},{6,30},{8,16},{10,18},{12,20},{14,22},{16,8},... | collective-permute-start | bytes 1990664 | tf_op jit(solution)/shard_map/ppermute | solution.py:41
  596.3 77.8 %collective-permute-start.47 = (bf16[2,1,144,1152]{3,2,1,0:T(8,128)(2,1)}, bf16[2,1,144,1152]{3,2,1,0:T(8,128)(2,1)S(1)}, u32[]{:S(2)}, u32[]{:S(2)}) collective-permute-start(bf16[2,1,144,1152]{3,2,1,0:T(8,128)(2,1)} %get-tuple-element.134), channel_id=1, source_target_pairs={{0,16},{2,18},{4,20},{6,22},{8,24},{10,26},{12,28},{14,30},{16,0},... | collective-permute-start | bytes 1990664 | tf_op jit(solution)/shard_map/ppermute | solution.py:41
  596.3 77.9 %collective-permute-start.46 = (bf16[2,1,144,1152]{3,2,1,0:T(8,128)(2,1)}, bf16[2,1,144,1152]{3,2,1,0:T(8,128)(2,1)S(1)}, u32[]{:S(2)}, u32[]{:S(2)}) collective-permute-start(bf16[2,1,144,1152]{3,2,1,0:T(8,128)(2,1)} %get-tuple-element.132), channel_id=1, source_target_pairs={{0,8},{2,10},{4,12},{6,14},{8,0},{10,2},{12,4},{14,6},{16,24},{18,... | collective-permute-start | bytes 1990664 | tf_op jit(solution)/shard_map/ppermute | solution.py:41
  675.5 22.0 %collective-permute-start.49 = (bf16[4,1,144,1152]{3,2,1,0:T(8,128)(2,1)}, bf16[4,1,144,1152]{3,2,1,0:T(8,128)(2,1)}, u32[]{:S(2)}, u32[]{:S(2)}) collective-permute-start(bf16[4,1,144,1152]{3,2,1,0:T(8,128)(2,1)} %pad_maximum_fusion.4), channel_id=1, source_target_pairs={{0,2},{2,0},{4,6},{6,4},{8,10},{10,8},{12,14},{14,12},{16,18},{18,... | collective-permute-start | bytes 3981320 | tf_op jit(solution)/shard_map/ppermute | solution.py:41
  712.8 45.9 %collective-permute-start.51 = (bf16[256,1536]{1,0:T(8,128)(2,1)S(1)}, bf16[256,1536]{1,0:T(8,128)(2,1)S(1)}, u32[]{:S(2)}, u32[]{:S(2)}) collective-permute-start(bf16[256,1536]{1,0:T(8,128)(2,1)S(1)} %bitcast.394), channel_id=1, source_target_pairs={{0,1},{1,0},{2,3},{3,2},{4,5},{5,4},{6,7},{7,6},{8,9},{9,8},{10,11... | collective-permute-start | bytes 2359304 | tf_op jit(solution)/shard_map/ppermute | solution.py:41
  721.6 37.1 %all-to-all-start.1 = ((bf16[16,64,192]{2,1,0:T(8,128)(2,1)}), bf16[16,64,192]{2,1,0:T(8,128)(2,1)S(1)}, u32[]{:S(2)}, u32[]{:S(2)}) async-start(bf16[16,64,192]{2,1,0:T(8,128)(2,1)} %copy.145), calls=%async_computation.2 | async-start | bytes 1048576 | tf_op jit(solution)/shard_map/all_to_all | solution.py:1431
  725.4 108.6 %reduce-scatter.5.cloned.1.call-start = ((), (), s32[]{:S(2)}) async-start(), calls=%async_computation.6 | async-start | bytes 2506752 | tf_op jit(solution)/shard_map/reduce_scatter | solution.py:1281
  729.5 28.1 %collective-permute-start.55 = (bf16[2,192,192]{2,1,0:T(8,128)(2,1)S(1)}, bf16[2,192,192]{2,1,0:T(8,128)(2,1)S(1)}, u32[]{:S(2)}, u32[]{:S(2)}) collective-permute-start(bf16[2,192,192]{2,1,0:T(8,128)(2,1)S(1)} %pad_maximum_fusion.29), channel_id=1, source_target_pairs={{0,16},{2,18},{4,20},{6,22},{8,24},{10,26},{12,28},{14,30},{16,0},... | collective-permute-start | bytes 442376 | tf_op jit(solution)/shard_map/ppermute | solution.py:41
  729.6 27.9 %collective-permute-start.54 = (bf16[2,192,192]{2,1,0:T(8,128)(2,1)S(1)}, bf16[2,192,192]{2,1,0:T(8,128)(2,1)S(1)}, u32[]{:S(2)}, u32[]{:S(2)}) collective-permute-start(bf16[2,192,192]{2,1,0:T(8,128)(2,1)S(1)} %pad_maximum_fusion.28), channel_id=1, source_target_pairs={{0,8},{2,10},{4,12},{6,14},{8,0},{10,2},{12,4},{14,6},{16,24},{18,... | collective-permute-start | bytes 442376 | tf_op jit(solution)/shard_map/ppermute | solution.py:41
  775.1 24.5 %collective-permute-start.57 = (bf16[192,288]{1,0:T(8,128)(2,1)}, bf16[192,288]{1,0:T(8,128)(2,1)}, u32[]{:S(2)}, u32[]{:S(2)}) collective-permute-start(bf16[192,288]{1,0:T(8,128)(2,1)} %bitcast.110), channel_id=1, source_target_pairs={{0,2},{2,0},{4,6},{6,4},{8,10},{10,8},{12,14},{14,12},{16,18},{18,... | collective-permute-start | bytes 331784 | tf_op jit(solution)/shard_map/ppermute | solution.py:41
  775.9 23.7 %collective-permute-start.58 = (bf16[192,288]{1,0:T(8,128)(2,1)}, bf16[192,288]{1,0:T(8,128)(2,1)}, u32[]{:S(2)}, u32[]{:S(2)}) collective-permute-start(bf16[192,288]{1,0:T(8,128)(2,1)} %bitcast.112), channel_id=1, source_target_pairs={{0,4},{2,6},{4,0},{6,2},{8,12},{10,14},{12,8},{14,10},{16,20},{18,... | collective-permute-start | bytes 331784 | tf_op jit(solution)/shard_map/ppermute | solution.py:41
  778.1 21.5 %collective-permute-start.59 = (bf16[192,288]{1,0:T(8,128)(2,1)}, bf16[192,288]{1,0:T(8,128)(2,1)}, u32[]{:S(2)}, u32[]{:S(2)}) collective-permute-start(bf16[192,288]{1,0:T(8,128)(2,1)} %bitcast.114), channel_id=1, source_target_pairs={{0,6},{2,4},{4,2},{6,0},{8,14},{10,12},{12,10},{14,8},{16,22},{18,... | collective-permute-start | bytes 331784 | tf_op jit(solution)/shard_map/ppermute | solution.py:41
  (172 other events, 1843.9 us)
Sparse Core Ops, SparseCore 0:
  225.2 54.9 all-gather.3
  282.3 113.8 all-gather.5
  400.3 256.7 reduce-scatter.2
  772.8 61.1 reduce-scatter.4

commit v3 on v2

--- a/solution.py
+++ b/solution.py
@@ -75,10 +75,9 @@
 
 
 def head_means(values, ones):
-    total = lax.dot_general(
-        values, ones, (((1,), (0,)), ((), ())), precision=HIGHEST, preferred_element_type=F32
-    )
-    return total * (1.0 / HD)
+    upper = values.astype(BF16)
+    lower = (values - upper.astype(F32)).astype(BF16)
+    return mxu(jnp.concatenate([upper, lower], axis=1), ones) * (1.0 / HD)
 
 
 def joined(pieces, axis):
@@ -102,7 +101,8 @@
 
 def head_ones():
     lane = np.arange(128) // HD
-    return jnp.asarray((lane[:, None] == lane[None, :]).astype(np.float32))
+    ones = (lane[:, None] == lane[None, :]).astype(np.float32)
+    return jnp.asarray(np.concatenate([ones, ones]), BF16)
 
 
 def group_cut(values, g):
@@ -222,7 +222,7 @@
             pl.BlockSpec((1, tokens, 128), by_stream),
             pl.BlockSpec((1, tokens, 128), by_stream),
             whole_spec((8, 128)),
-            whole_spec((128, 128)),
+            whole_spec((256, 128)),
         ],
         [
             pl.BlockSpec(q_block, first),
@@ -244,21 +244,30 @@
 
 
 BIG = 4
+CLIP = 16
 
 
 def over_tiles(start, count, body):
-    big = count // BIG
+    whole = count // CLIP
+    rest = count - whole * CLIP
+    big = rest // BIG
+    at = lambda frame: pl.multiple_of(frame * FRAME_TOK, FRAME_TOK)
+
+    def whole_step(t, carry):
+        body(at(start + t * CLIP), BIG * FRAME_TOK, CLIP // BIG)
+        return carry
 
     def big_step(t, carry):
-        body(pl.multiple_of((start + t * BIG) * FRAME_TOK, FRAME_TOK), BIG * FRAME_TOK)
+        body(at(start + whole * CLIP + t * BIG), BIG * FRAME_TOK, 1)
         return carry
 
     def small_step(t, carry):
-        body(pl.multiple_of((start + big * BIG + t) * FRAME_TOK, FRAME_TOK), FRAME_TOK)
+        body(at(start + whole * CLIP + big * BIG + t), FRAME_TOK, 1)
         return carry
 
+    lax.fori_loop(0, whole, whole_step, 0)
     lax.fori_loop(0, big, big_step, 0)
-    lax.fori_loop(0, count - big * BIG, small_step, 0)
+    lax.fori_loop(0, rest - big * BIG, small_step, 0)
 
 
 def stacked(values, mask):
@@ -347,10 +356,15 @@
 
     query = stacked(queries[j], mask_ref[...])
 
-    def tile(base, size):
-        scores = mxu(keys[pl.ds(base, size), :], query, ((1,), (1,)))
-        weights = jnp.exp2(scores * EXP2_SCALE).astype(BF16)
-        acc[...] += mxu(values[:, pl.ds(base, size)], weights)
+    def tile(base, size, times):
+        total = None
+        for t in range(times):
+            rows = pl.ds(pl.multiple_of(base + t * size, FRAME_TOK), size)
+            scores = mxu(keys[rows, :], query, ((1,), (1,)))
+            weights = jnp.exp2(scores * EXP2_SCALE).astype(BF16)
+            part = mxu(values[:, rows], weights)
+            total = part if total is None else total + part
+        acc[...] += total
 
     def finish(row):
         total = acc[GROUP_WIDTH : GROUP_WIDTH + 1, :]
@@ -361,7 +375,7 @@
     over_tiles(start_ref[s, j], count_ref[s, j], tile)
     self_out = finish(0)
     acc[...] = jnp.zeros_like(acc)
-    tile(pl.multiple_of(self_rows + clip_ref[s, j] * CTX, 128), CTX)
+    tile(pl.multiple_of(self_rows + clip_ref[s, j] * CTX, 128), CTX, 1)
     text_out = finish(1)
     self_ref[0, 0] = self_out
     text_ref[0, 0] = text_out
@@ -431,21 +445,25 @@
         grad_stack = stacked(grad, mask)
         delta = head_row(grad.astype(F32) * out)
 
-        def tile(base, size):
-            rows = pl.ds(base, size)
-            scores = mxu(keys[rows, :], query, ((1,), (1,)))
-            weights = jnp.exp2(scores * EXP2_SCALE - lse)
-            dweights = mxu(values[rows, :], grad_stack, ((1,), (1,)))
-            dscores = (weights * (dweights - delta)).astype(BF16)
-            dvalues[rows, :] += mxu(weights.astype(BF16), grad_stack)
-            dkeys[rows, :] += mxu(dscores, query)
-            dquery[...] += mxu(keys_flip[:, rows], dscores)
+        def tile(base, size, times):
+            total = None
+            for t in range(times):
+                rows = pl.ds(pl.multiple_of(base + t * size, FRAME_TOK), size)
+                scores = mxu(keys[rows, :], query, ((1,), (1,)))
+                weights = jnp.exp2(scores * EXP2_SCALE - lse)
+                dweights = mxu(values[rows, :], grad_stack, ((1,), (1,)))
+                dscores = (weights * (dweights - delta)).astype(BF16)
+                dvalues[rows, :] += mxu(weights.astype(BF16), grad_stack)
+                dkeys[rows, :] += mxu(dscores, query)
+                part = mxu(keys_flip[:, rows], dscores)
+                total = part if total is None else total + part
+            dquery[...] += total
 
         return tile
 
     over_tiles(start_ref[s, j], count_ref[s, j], over(grad_low, self_ref[0, 0], lse_ref[0, 0, 0:1, :]))
     over(grad_text, text_out, lse_ref[0, 0, 1:2, :])(
-        pl.multiple_of(self_rows + clip_ref[s, j] * CTX, 128), CTX
+        pl.multiple_of(self_rows + clip_ref[s, j] * CTX, 128), CTX, 1
     )
     dq_ref[0, 0] = (diagonal(dquery[...]) * SCALE).astype(BF16)
 
@@ -772,7 +790,7 @@
             pl.BlockSpec((1, 1, 2 * tokens, 128), lambda i, g: (i // half, i % half, 0, 0)),
             pl.BlockSpec((1, 1, 2 * tokens, 128), lambda i, g: (i // half, i % half, 0, 0)),
             whole_spec(gains.shape),
-            whole_spec((128, 128)),
+            whole_spec((256, 128)),
         ],
         [
             pl.BlockSpec(
@@ -888,7 +906,7 @@
             whole_spec(w_cols.shape),
             pl.BlockSpec((1, chunk_text, text_lanes), lambda k, _: (k, 0, 0)),
             whole_spec((8, 128)),
-            whole_spec((128, 128)),
+            whole_spec((256, 128)),
         ],
         [
             whole_spec((tokens, width)),
@@ -1355,7 +1373,7 @@
     part = part[:, 0]
     part_own = pick(part, xs.me)
     part_sent = [pick(part, xs.me ^ s) for s in range(1, fsdp)]
-    proj_other = held(proj_other, part_own, *part_sent)
+    proj_other = held(proj_other, part_own, ffn_sums, *part_sent)
     in_first, in_rest, grad_text, gain_text = in_back(
         both_info, proj_own, proj_other, w_cols, text_raw, gains, tokens
     )
@@ -1379,7 +1397,7 @@
             )
         in_got = [held(v, *sent) for v in in_got]
     for v in in_got:
-        in_first = in_first + held(v, ffn_sums).astype(F32)
+        in_first = in_first + v.astype(F32)
     grad_normed = frame_view(in_first)
     in_unit = frame_sum(grad_normed * unit_in)
     grad_scale_attn = in_unit * gain_attn_in

time: 850 us -> 792 us (0.932)
  waiting for transfers between devices: 348 us -> 309 us
  Pallas kernels: 177 us -> 160 us
    reduce_scatter x2, waiting for transfers between devices: 27.2 us -> 0.01 us  [reduce_rows(): lax.psum_scatter(term, 'dp', scatter_dimension=0, tiled=True).astype(F32)]
    pallas_call x8, Pallas kernels: 177 us -> 160 us  [call(): pl.pallas_call(kernel, grid_spec=pltpu.PrefetchScalarGridSpec(num_scalar_...]
    ppermute x66, waiting for transfers between devices: 320 us -> 306 us  [swap(): lax.ppermute(value, self.axis, [(i, i ^ mask) for i in range(self.size)])]
    unnamed x282 -> x278, local copies, waits for them, and re-layouts: 36.3 us -> 30.5 us
  transfers between devices with their start and end apart: 72 -> 72, of which waited for: 34 -> 34; matrix products, arithmetic and copies ran while one was open for 20% -> 23% of each run, Pallas kernels for 15% -> 14%
where the time goes in v3:
time: 792 us; the launch traced here: 785 us
  waiting for transfers between devices  309 us (39%)
  Pallas kernels  160 us (20%)
  starting transfers between devices  87.5 us (11%)
  local copies, waits for them, and re-layouts  79.2 us (10%)
  other arithmetic  75.6 us (10%)
  matrix products  57.3 us (7%)
  between operations  16.4 us (2%)
    ppermute x66, waiting for transfers between devices, swap(): lax.ppermute(value, self.axis, [(i, i ^ mask) for i in range(self.size)])  306 us
    pallas_call x8, Pallas kernels, call(): pl.pallas_call(kernel, grid_spec=pltpu.PrefetchScalarGridSpec(num_scalar_...  160 us
    ppermute x66, starting transfers between devices, swap(): lax.ppermute(value, self.axis, [(i, i ^ mask) for i in range(self.size)])  80.2 us
    dot_general x16, matrix products, mxu(): return lax.dot_general(a, b, (dims, ((), ())), preferred_element_type=F32)  54.4 us
    unnamed x278, local copies, waits for them, and re-layouts  30.5 us
  transfers between devices with their start and end apart: 72, of which 34 were waited for; matrix products, arithmetic and copies ran while one was open for 23% of the time, Pallas kernels for 14%

profile of v3, /device:TPU:0, one launch (start us, length us, event | category | flops | bytes accessed | tf_op | source)
XLA Modules:
  0.0 785.3 jit_solution(2507821696019146584)
XLA Ops:
  23.5 5.2 fusion.86
  57.8 13.6 %collective-permute-done.9 = bf16[2,32,2,768]{3,2,1,0:T(2,128)(2,1)S(1)} collective-permute-done((bf16[2,32,2,768]{3,2,1,0:T(2,128)(2,1)S(1)}, bf16[2,32,2,768]{3,2,1,0:T(2,128)(2,1)S(1)}, u32[]{:S(2)}, u32[]{:S(2)}) %collective-permute-start.9) | collective-permute-done | bytes 196640 | tf_op jit(solution)/shard_map/ppermute | solution.py:41
  80.3 8.8 %make_heads.1 = (bf16[1,4,128,384]{3,2,1,0:T(8,128)(2,1)S(1)}, bf16[1,4,288,384]{3,2,1,0:T(8,128)(2,1)S(1)}, bf16[1,4,128,384]{3,2,1,0:T(8,128)(2,1)S(1)}, bf16[1,4,288,384]{3,2,1,0:T(8,128)(2,1)S(1)}) custom-call(s32[1]{0:T(128)} %bitcast.5.core_ref, bf16[2,256,1536]{2,1,0:T(8,128)(2,1)S(1)} %pad_maximum_fusion.x_ref, ...), custom_call_target="tpu_custom_call" | custom-call | flops 36238784 | bytes 110100 | tf_op jit(solution)/shard_map/make_heads/pallas_call | solution.py:117
  98.2 8.5 %collective-permute-done.13.refs_8_ = bf16[2,1,288,384]{3,2,1,0:T(8,128)(2,1)S(1)} collective-permute-done((bf16[2,1,288,384]{3,2,1,0:T(8,128)(2,1)S(1)}, bf16[2,1,288,384]{3,2,1,0:T(8,128)(2,1)S(1)}, u32[]{:S(2)}, u32[]{:S(2)}) %collective-permute-start.13) | collective-permute-done | bytes 442400 | tf_op jit(solution)/shard_map/ppermute | solution.py:41
  106.8 26.7 %collective-permute-done.12.refs_7_ = bf16[2,1,288,384]{3,2,1,0:T(8,128)(2,1)S(1)} collective-permute-done((bf16[2,1,288,384]{3,2,1,0:T(8,128)(2,1)S(1)}, bf16[2,1,288,384]{3,2,1,0:T(8,128)(2,1)S(1)}, u32[]{:S(2)}, u32[]{:S(2)}) %collective-permute-start.12) | collective-permute-done | bytes 442400 | tf_op jit(solution)/shard_map/ppermute | solution.py:41
  142.9 6.0 collective-permute-start.19
  153.5 5.2 collective-permute-done.16.refs_11_
  158.7 7.4 collective-permute-done.15.refs_10_
  166.1 38.1 %attention.1 = (bf16[2,1,128,384]{3,2,1,0:T(8,128)(2,1)S(1)}, bf16[2,1,128,384]{3,2,1,0:T(8,128)(2,1)S(1)}, bf16[2,1,128,384]{3,2,1,0:T(8,128)(2,1)S(1)}, bf16[2...) custom-call(s32[1,32]{1,0:T(1,128)S(1)} %bitcast.392, ...), custom_call_target="tpu_custom_call" | custom-call | flops 217432720 | bytes 48000 | tf_op jit(solution)/shard_map/attention/pallas_call | solution.py:117
  215.8 7.7 collective-permute-done.23.refs_2_
  253.6 6.9 sine_multiply_fusion
  265.7 5.4 fusion.14
  271.1 12.3 %collective-permute-done.31.refs_1_ = bf16[256,1536]{1,0:T(8,128)(2,1)S(1)} collective-permute-done((bf16[256,1536]{1,0:T(8,128)(2,1)S(1)}, bf16[256,1536]{1,0:T(8,128)(2,1)S(1)}, u32[]{:S(2)}, u32[]{:S(2)}) %collective-permute-start.31) | collective-permute-done | bytes 786464 | tf_op jit(solution)/shard_map/ppermute | solution.py:41
  295.4 13.2 %collective-permute-done.32 = bf16[256,1536]{1,0:T(8,128)(2,1)S(1)} collective-permute-done((bf16[256,1536]{1,0:T(8,128)(2,1)S(1)}, bf16[256,1536]{1,0:T(8,128)(2,1)S(1)}, u32[]{:S(2)}, u32[]{:S(2)}) %collective-permute-start.32) | collective-permute-done | bytes 786464 | tf_op jit(solution)/shard_map/ppermute | solution.py:41
  315.7 5.0 multiply_convert_fusion.1
  320.8 10.8 %collective-permute-done.33.refs_3_ = bf16[256,1536]{1,0:T(8,128)(2,1)S(1)} collective-permute-done((bf16[256,1536]{1,0:T(8,128)(2,1)S(1)}, bf16[256,1536]{1,0:T(8,128)(2,1)S(1)}, u32[]{:S(2)}, u32[]{:S(2)}) %collective-permute-start.33) | collective-permute-done | bytes 786464 | tf_op jit(solution)/shard_map/ppermute | solution.py:41
  331.5 4.9 multiply_convert_fusion
  347.1 19.0 %ffn_weights.1 = bf16[1536,6144]{1,0:T(8,128)(2,1)} custom-call(bf16[256,1536]{1,0:T(8,128)(2,1)} %copy-done.59, bf16[256,1536]{1,0:T(8,128)(2,1)} %copy-done.72, bf16[256,1536]{1,0:T(8,128)(2,1)} %copy-done.60, bf16[256,1536]{1,0:T(8,128)(2,1)} %copy-done.73, bf16[256,2048]{1,0:T(8,128)(2,1)} %copy-done.69, bf16[256,2048]{1,0:T(8,128)(2,1)} %copy-done.71, ...), custom_call_target="tpu_custom_call" | custom-call | flops 96636768 | bytes 267386 | tf_op jit(solution)/shard_map/ffn_weights/pallas_call | solution.py:117
  378.9 14.6 %collective-permute-done.36 = bf16[256,1536]{1,0:T(8,128)(2,1)S(1)} collective-permute-done((bf16[256,1536]{1,0:T(8,128)(2,1)S(1)}, bf16[256,1536]{1,0:T(8,128)(2,1)S(1)}, u32[]{:S(2)}, u32[]{:S(2)}) %collective-permute-start.36) | collective-permute-done | bytes 786464 | tf_op jit(solution)/shard_map/ppermute | solution.py:41
  415.1 11.0 %collective-permute-done.39.refs_19_ = bf16[2,1,128,384]{3,2,1,0:T(8,128)(2,1)} collective-permute-done((bf16[2,1,128,384]{3,2,1,0:T(8,128)(2,1)}, bf16[2,1,128,384]{3,2,1,0:T(8,128)(2,1)}, u32[]{:S(2)}, u32[]{:S(2)}) %collective-permute-start.39) | collective-permute-done | bytes 196640 | tf_op jit(solution)/shard_map/ppermute | solution.py:41
  436.7 59.9 %attention_back.1 = (bf16[1,16,128,192]{3,2,1,0:T(8,128)(2,1)S(1)}, bf16[2,1,288,384]{3,2,1,0:T(8,128)(2,1)S(1)}, bf16[2,1,288,384]{3,2,1,0:T(8,128)(2,1)S(1)}, ...) custom-call(s32[1,32]{1,0:T(1,128)S(1)} %bitcast.393, ...), custom_call_target="tpu_custom_call" | custom-call | flops 543581824 | bytes 80000 | tf_op jit(solution)/shard_map/attention_back/pallas_call | solution.py:117
  504.7 5.3 collective-permute-done.44
  510.1 18.8 %collective-permute-done.43 = bf16[2,1,288,384]{3,2,1,0:T(8,128)(2,1)S(1)} collective-permute-done((bf16[2,1,288,384]{3,2,1,0:T(8,128)(2,1)S(1)}, bf16[2,1,288,384]{3,2,1,0:T(8,128)(2,1)S(1)}, u32[]{:S(2)}, u32[]{:S(2)}) %collective-permute-start.43) | collective-permute-done | bytes 442400 | tf_op jit(solution)/shard_map/ppermute | solution.py:41
  529.0 13.9 %collective-permute-done.42 = bf16[2,1,288,384]{3,2,1,0:T(8,128)(2,1)S(1)} collective-permute-done((bf16[2,1,288,384]{3,2,1,0:T(8,128)(2,1)S(1)}, bf16[2,1,288,384]{3,2,1,0:T(8,128)(2,1)S(1)}, u32[]{:S(2)}, u32[]{:S(2)}) %collective-permute-start.42) | collective-permute-done | bytes 442400 | tf_op jit(solution)/shard_map/ppermute | solution.py:41
  543.0 18.1 %collective-permute-done.41 = bf16[2,1,288,384]{3,2,1,0:T(8,128)(2,1)S(1)} collective-permute-done((bf16[2,1,288,384]{3,2,1,0:T(8,128)(2,1)S(1)}, bf16[2,1,288,384]{3,2,1,0:T(8,128)(2,1)S(1)}, u32[]{:S(2)}, u32[]{:S(2)}) %collective-permute-start.41) | collective-permute-done | bytes 442400 | tf_op jit(solution)/shard_map/ppermute | solution.py:41
  561.2 16.1 %proj_back.1 = (bf16[2,1,144,1152]{3,2,1,0:T(8,128)(2,1)S(1)}, bf16[2,1,144,1152]{3,2,1,0:T(8,128)(2,1)}, bf16[2,1,144,1152]{3,2,1,0:T(8,128)(2,1)}, bf16[2,1,14...) custom-call(s32[1]{0:T(128)} %bitcast.6.refs_0_, bf16[4,2,1,256,1536]{4,3,2,1,0:T(8,128)(2,1)} %bitcast.403, ...), custom_call_target="tpu_custom_call" | custom-call | flops 60397976 | bytes 137625 | tf_op jit(solution)/shard_map/proj_back/pallas_call | solution.py:117
  591.0 24.6 %collective-permute-done.48.refs_3_ = bf16[2,1,144,1152]{3,2,1,0:T(8,128)(2,1)S(1)} collective-permute-done((bf16[2,1,144,1152]{3,2,1,0:T(8,128)(2,1)}, bf16[2,1,144,1152]{3,2,1,0:T(8,128)(2,1)S(1)}, u32[]{:S(2)}, u32[]{:S(2)}) %collective-permute-start.48) | collective-permute-done | bytes 663584 | tf_op jit(solution)/shard_map/ppermute | solution.py:41
  615.6 51.6 %collective-permute-done.47.refs_2_ = bf16[2,1,144,1152]{3,2,1,0:T(8,128)(2,1)S(1)} collective-permute-done((bf16[2,1,144,1152]{3,2,1,0:T(8,128)(2,1)}, bf16[2,1,144,1152]{3,2,1,0:T(8,128)(2,1)S(1)}, u32[]{:S(2)}, u32[]{:S(2)}) %collective-permute-start.47) | collective-permute-done | bytes 663584 | tf_op jit(solution)/shard_map/ppermute | solution.py:41
  680.0 10.9 %in_back.1 = (f32[256,1536]{1,0:T(8,128)}, bf16[1,256,1536]{2,1,0:T(8,128)(2,1)S(1)}, bf16[2,32,1536]{2,1,0:T(8,128)(2,1)S(1)}, f32[8,128]{1,0:T(8,128)S(1)}) custom-call(s32[2]{0:T(128)S(1)} %pad_add_fusion.info_ref, bf16[2,1,144,1152]{3,2,1,0:T(8,128)(2,1)S(1)} %get-tuple-element.130.refs_0_, ...), custom_call_target="tpu_custom_call" | custom-call | flops 36238784 | bytes 117964 | tf_op jit(solution)/shard_map/in_back/pallas_call | solution.py:117
  707.0 7.9 %collective-permute-done.55 = bf16[2,192,192]{2,1,0:T(8,128)(2,1)} collective-permute-done((bf16[2,192,192]{2,1,0:T(8,128)(2,1)}, bf16[2,192,192]{2,1,0:T(8,128)(2,1)}, u32[]{:S(2)}, u32[]{:S(2)}) %collective-permute-start.55) | collective-permute-done | bytes 147488 | tf_op jit(solution)/shard_map/ppermute | solution.py:41
  722.6 6.1 multiply_reduce_fusion.2
  757.9 8.7 %collective-permute-done.64 = f32[56,128]{1,0:T(8,128)S(1)} collective-permute-done((f32[56,128]{1,0:T(8,128)S(1)}, f32[56,128]{1,0:T(8,128)S(1)}, u32[]{:S(2)}, u32[]{:S(2)}) %collective-permute-start.64) | collective-permute-done | bytes 28704 | tf_op jit(solution)/shard_map/ppermute | solution.py:41
  (635 shorter events, 296.5 us)
Async XLA Ops:
  7.2 387.6 %all-gather.4.cloned.1.call-start = ((), (), s32[]{:S(2)}) async-start(), calls=%async_computation.4 | async-start | bytes 4456448 | tf_op jit(solution)/shard_map/all_gather | solution.py:1240
  14.3 28.9 %collective-permute-start.8 = (bf16[32,2048]{1,0:T(8,128)(2,1)}, bf16[32,2048]{1,0:T(8,128)(2,1)}, u32[]{:S(2)}, u32[]{:S(2)}) collective-permute-start(bf16[32,2048]{1,0:T(8,128)(2,1)} %get-tuple-element.317), channel_id=1, source_target_pairs={{0,1},{1,0},{2,3},{3,2},{4,5},{5,4},{6,7},{7,6},{8,9},{9,8},{10,11... | collective-permute-start | bytes 393224 | tf_op jit(solution)/shard_map/ppermute | solution.py:41
  28.8 23.7 %collective-permute-start.4 = (bf16[192,2304]{1,0:T(8,128)(2,1)}, bf16[192,2304]{1,0:T(8,128)(2,1)}, u32[]{:S(2)}, u32[]{:S(2)}) collective-permute-start(bf16[192,2304]{1,0:T(8,128)(2,1)} %pad_maximum_fusion.6), channel_id=1, source_target_pairs={{0,1},{1,0},{2,3},{3,2},{4,5},{5,4},{6,7},{7,6},{8,9},{9,8},{10,11... | collective-permute-start | bytes 2654216 | tf_op jit(solution)/shard_map/ppermute | solution.py:41
  34.7 37.3 %collective-permute-start.3 = (bf16[256,1536]{1,0:T(8,128)(2,1)S(1)}, bf16[256,1536]{1,0:T(8,128)(2,1)}, u32[]{:S(2)}, u32[]{:S(2)}) collective-permute-start(bf16[256,1536]{1,0:T(8,128)(2,1)S(1)} %fusion.52), channel_id=1, source_target_pairs={{0,1},{1,0},{2,3},{3,2},{4,5},{5,4},{6,7},{7,6},{8,9},{9,8},{10,11... | collective-permute-start | bytes 2359304 | tf_op jit(solution)/shard_map/ppermute | solution.py:41
  52.5 20.9 %collective-permute-start.5 = (bf16[192,2304]{1,0:T(8,128)(2,1)}, bf16[192,2304]{1,0:T(8,128)(2,1)}, u32[]{:S(2)}, u32[]{:S(2)}) collective-permute-start(bf16[192,2304]{1,0:T(8,128)(2,1)} %collective-permute-done.4), channel_id=1, source_target_pairs={{0,4},{2,6},{4,0},{6,2},{8,12},{10,14},{12,8},{14,10},{16,20},{18,... | collective-permute-start | bytes 2654216 | tf_op jit(solution)/shard_map/ppermute | solution.py:41
  95.5 38.0 %collective-permute-start.12 = (bf16[2,1,288,384]{3,2,1,0:T(8,128)(2,1)S(1)}, bf16[2,1,288,384]{3,2,1,0:T(8,128)(2,1)S(1)}, u32[]{:S(2)}, u32[]{:S(2)}) collective-permute-start(bf16[2,1,288,384]{3,2,1,0:T(8,128)(2,1)S(1)} %pad_maximum_fusion.13), channel_id=1, source_target_pairs={{0,16},{2,18},{4,20},{6,22},{8,24},{10,26},{12,28},{14,30},{16,0},... | collective-permute-start | bytes 1327112 | tf_op jit(solution)/shard_map/ppermute | solution.py:41
  95.6 37.9 %collective-permute-start.11 = (bf16[2,1,288,384]{3,2,1,0:T(8,128)(2,1)S(1)}, bf16[2,1,288,384]{3,2,1,0:T(8,128)(2,1)S(1)}, u32[]{:S(2)}, u32[]{:S(2)}) collective-permute-start(bf16[2,1,288,384]{3,2,1,0:T(8,128)(2,1)S(1)} %pad_maximum_fusion.12), channel_id=1, source_target_pairs={{0,8},{2,10},{4,12},{6,14},{8,0},{10,2},{12,4},{14,6},{16,24},{18,... | collective-permute-start | bytes 1327112 | tf_op jit(solution)/shard_map/ppermute | solution.py:41
  96.6 43.1 %collective-permute-start.14 = (bf16[2,1,288,384]{3,2,1,0:T(8,128)(2,1)S(1)}, bf16[2,1,288,384]{3,2,1,0:T(8,128)(2,1)S(1)}, u32[]{:S(2)}, u32[]{:S(2)}) collective-permute-start(bf16[2,1,288,384]{3,2,1,0:T(8,128)(2,1)S(1)} %pad_maximum_fusion.11.refs_5_), channel_id=1, source_target_pairs={{0,4},{2,6},{4,0},{6,2},{8,12},{10,14},{12,8},{14,10},{16,20},{18,... | collective-permute-start | bytes 1327112 | tf_op jit(solution)/shard_map/ppermute | solution.py:41
  137.6 21.1 %collective-permute-start.16 = (bf16[2,1,288,384]{3,2,1,0:T(8,128)(2,1)S(1)}, bf16[2,1,288,384]{3,2,1,0:T(8,128)(2,1)S(1)}, u32[]{:S(2)}, u32[]{:S(2)}) collective-permute-start(bf16[2,1,288,384]{3,2,1,0:T(8,128)(2,1)S(1)} %collective-permute-done.12.refs_7_), channel_id=1, source_target_pairs={{0,4},{2,6},{4,0},{6,2},{8,12},{10,14},{12,8},{14,10},{16,20},{18,... | collective-permute-start | bytes 1327112 | tf_op jit(solution)/shard_map/ppermute | solution.py:41
  138.1 28.0 %collective-permute-start.15 = (bf16[2,1,288,384]{3,2,1,0:T(8,128)(2,1)S(1)}, bf16[2,1,288,384]{3,2,1,0:T(8,128)(2,1)S(1)}, u32[]{:S(2)}, u32[]{:S(2)}) collective-permute-start(bf16[2,1,288,384]{3,2,1,0:T(8,128)(2,1)S(1)} %collective-permute-done.11.refs_6_), channel_id=1, source_target_pairs={{0,4},{2,6},{4,0},{6,2},{8,12},{10,14},{12,8},{14,10},{16,20},{18,... | collective-permute-start | bytes 1327112 | tf_op jit(solution)/shard_map/ppermute | solution.py:41
  223.6 171.2 %all-gather.6.cloned.1.call-start = ((), (), s32[]{:S(2)}) async-start(), calls=%async_computation.7 | async-start | bytes 7864320 | tf_op jit(solution)/shard_map/all_gather | solution.py:1243
  229.1 448.0 %reduce-scatter.3.cloned.1.call-start = ((), (), s32[]{:S(2)}) async-start(), calls=%async_computation.5 | async-start | bytes 20054016 | tf_op jit(solution)/shard_map/reduce_scatter | solution.py:1299
  240.5 20.0 %collective-permute-start.26 = (bf16[256,1536]{1,0:T(8,128)(2,1)}, bf16[256,1536]{1,0:T(8,128)(2,1)}, u32[]{:S(2)}, u32[]{:S(2)}) collective-permute-start(bf16[256,1536]{1,0:T(8,128)(2,1)} %bitcast.46), channel_id=1, source_target_pairs={{0,1},{1,0},{2,3},{3,2},{4,5},{5,4},{6,7},{7,6},{8,9},{9,8},{10,11... | collective-permute-start | bytes 2359304 | tf_op jit(solution)/shard_map/ppermute | solution.py:41
  264.6 18.8 %collective-permute-start.31 = (bf16[256,1536]{1,0:T(8,128)(2,1)S(1)}, bf16[256,1536]{1,0:T(8,128)(2,1)S(1)}, u32[]{:S(2)}, u32[]{:S(2)}) collective-permute-start(bf16[256,1536]{1,0:T(8,128)(2,1)S(1)} %fusion.50.refs_0_), channel_id=1, source_target_pairs={{0,1},{1,0},{2,3},{3,2},{4,5},{5,4},{6,7},{7,6},{8,9},{9,8},{10,11... | collective-permute-start | bytes 2359304 | tf_op jit(solution)/shard_map/ppermute | solution.py:41
  290.7 17.9 %collective-permute-start.32 = (bf16[256,1536]{1,0:T(8,128)(2,1)S(1)}, bf16[256,1536]{1,0:T(8,128)(2,1)S(1)}, u32[]{:S(2)}, u32[]{:S(2)}) collective-permute-start(bf16[256,1536]{1,0:T(8,128)(2,1)S(1)} %convolution_convert_fusion), channel_id=1, source_target_pairs={{0,1},{1,0},{2,3},{3,2},{4,5},{5,4},{6,7},{7,6},{8,9},{9,8},{10,11... | collective-permute-start | bytes 2359304 | tf_op jit(solution)/shard_map/ppermute | solution.py:41
  341.1 25.0 %collective-permute-start.34 = (bf16[256,1536]{1,0:T(8,128)(2,1)}, bf16[256,1536]{1,0:T(8,128)(2,1)}, u32[]{:S(2)}, u32[]{:S(2)}) collective-permute-start(bf16[256,1536]{1,0:T(8,128)(2,1)} %fusion.30), channel_id=1, source_target_pairs={{0,1},{1,0},{2,3},{3,2},{4,5},{5,4},{6,7},{7,6},{8,9},{9,8},{10,11... | collective-permute-start | bytes 2359304 | tf_op jit(solution)/shard_map/ppermute | solution.py:41
  366.2 410.5 %reduce-scatter.5.cloned.1.call-start = ((), (), s32[]{:S(2)}) async-start(), calls=%async_computation.6 | async-start | bytes 2506752 | tf_op jit(solution)/shard_map/reduce_scatter | solution.py:1299
  405.0 21.1 %collective-permute-start.39 = (bf16[2,1,128,384]{3,2,1,0:T(8,128)(2,1)}, bf16[2,1,128,384]{3,2,1,0:T(8,128)(2,1)}, u32[]{:S(2)}, u32[]{:S(2)}) collective-permute-start(bf16[2,1,128,384]{3,2,1,0:T(8,128)(2,1)} %pad_maximum_fusion.25), channel_id=1, source_target_pairs={{0,16},{2,18},{4,20},{6,22},{8,24},{10,26},{12,28},{14,30},{16,0},... | collective-permute-start | bytes 589832 | tf_op jit(solution)/shard_map/ppermute | solution.py:41
  499.8 29.1 %collective-permute-start.43 = (bf16[2,1,288,384]{3,2,1,0:T(8,128)(2,1)S(1)}, bf16[2,1,288,384]{3,2,1,0:T(8,128)(2,1)S(1)}, u32[]{:S(2)}, u32[]{:S(2)}) collective-permute-start(bf16[2,1,288,384]{3,2,1,0:T(8,128)(2,1)S(1)} %get-tuple-element.125), channel_id=1, source_target_pairs={{0,4},{2,6},{4,0},{6,2},{8,12},{10,14},{12,8},{14,10},{16,20},{18,... | collective-permute-start | bytes 1327112 | tf_op jit(solution)/shard_map/ppermute | solution.py:41
  502.6 40.3 %collective-permute-start.42 = (bf16[2,1,288,384]{3,2,1,0:T(8,128)(2,1)S(1)}, bf16[2,1,288,384]{3,2,1,0:T(8,128)(2,1)S(1)}, u32[]{:S(2)}, u32[]{:S(2)}) collective-permute-start(bf16[2,1,288,384]{3,2,1,0:T(8,128)(2,1)S(1)} %get-tuple-element.123), channel_id=1, source_target_pairs={{0,4},{2,6},{4,0},{6,2},{8,12},{10,14},{12,8},{14,10},{16,20},{18,... | collective-permute-start | bytes 1327112 | tf_op jit(solution)/shard_map/ppermute | solution.py:41
  503.4 57.8 %collective-permute-start.41 = (bf16[2,1,288,384]{3,2,1,0:T(8,128)(2,1)S(1)}, bf16[2,1,288,384]{3,2,1,0:T(8,128)(2,1)S(1)}, u32[]{:S(2)}, u32[]{:S(2)}) collective-permute-start(bf16[2,1,288,384]{3,2,1,0:T(8,128)(2,1)S(1)} %get-tuple-element.121), channel_id=1, source_target_pairs={{0,4},{2,6},{4,0},{6,2},{8,12},{10,14},{12,8},{14,10},{16,20},{18,... | collective-permute-start | bytes 1327112 | tf_op jit(solution)/shard_map/ppermute | solution.py:41
  581.6 34.0 %collective-permute-start.48 = (bf16[2,1,144,1152]{3,2,1,0:T(8,128)(2,1)}, bf16[2,1,144,1152]{3,2,1,0:T(8,128)(2,1)S(1)}, u32[]{:S(2)}, u32[]{:S(2)}) collective-permute-start(bf16[2,1,144,1152]{3,2,1,0:T(8,128)(2,1)} %get-tuple-element.135), channel_id=1, source_target_pairs={{0,24},{2,26},{4,28},{6,30},{8,16},{10,18},{12,20},{14,22},{16,8},... | collective-permute-start | bytes 1990664 | tf_op jit(solution)/shard_map/ppermute | solution.py:41
  581.9 85.4 %collective-permute-start.47 = (bf16[2,1,144,1152]{3,2,1,0:T(8,128)(2,1)}, bf16[2,1,144,1152]{3,2,1,0:T(8,128)(2,1)S(1)}, u32[]{:S(2)}, u32[]{:S(2)}) collective-permute-start(bf16[2,1,144,1152]{3,2,1,0:T(8,128)(2,1)} %get-tuple-element.133), channel_id=1, source_target_pairs={{0,16},{2,18},{4,20},{6,22},{8,24},{10,26},{12,28},{14,30},{16,0},... | collective-permute-start | bytes 1990664 | tf_op jit(solution)/shard_map/ppermute | solution.py:41
  581.9 85.4 %collective-permute-start.46 = (bf16[2,1,144,1152]{3,2,1,0:T(8,128)(2,1)}, bf16[2,1,144,1152]{3,2,1,0:T(8,128)(2,1)S(1)}, u32[]{:S(2)}, u32[]{:S(2)}) collective-permute-start(bf16[2,1,144,1152]{3,2,1,0:T(8,128)(2,1)} %get-tuple-element.131), channel_id=1, source_target_pairs={{0,8},{2,10},{4,12},{6,14},{8,0},{10,2},{12,4},{14,6},{16,24},{18,... | collective-permute-start | bytes 1990664 | tf_op jit(solution)/shard_map/ppermute | solution.py:41
  590.3 79.6 %collective-permute-start.50 = (bf16[2,1,192,576]{3,2,1,0:T(8,128)(2,1)}, bf16[2,1,192,576]{3,2,1,0:T(8,128)(2,1)}, u32[]{:S(2)}, u32[]{:S(2)}) collective-permute-start(bf16[2,1,192,576]{3,2,1,0:T(8,128)(2,1)} %constant_dynamic-slice_fusion.24), channel_id=1, source_target_pairs={{0,4},{2,6},{4,0},{6,2},{8,12},{10,14},{12,8},{14,10},{16,20},{18,... | collective-permute-start | bytes 1327112 | tf_op jit(solution)/shard_map/ppermute | solution.py:41
  673.8 18.1 %collective-permute-start.52 = (bf16[192,576]{0,1:T(8,128)(2,1)}, bf16[192,576]{0,1:T(8,128)(2,1)}, u32[]{:S(2)}, u32[]{:S(2)}) collective-permute-start(bf16[192,576]{0,1:T(8,128)(2,1)} %bitcast.419), channel_id=1, source_target_pairs={{0,1},{1,0},{2,3},{3,2},{4,5},{5,4},{6,7},{7,6},{8,9},{9,8},{10,11... | collective-permute-start | bytes 663560 | tf_op jit(solution)/shard_map/ppermute | solution.py:41
  693.6 29.0 %collective-permute-start.51 = (bf16[256,1536]{1,0:T(8,128)(2,1)S(1)}, bf16[256,1536]{1,0:T(8,128)(2,1)}, u32[]{:S(2)}, u32[]{:S(2)}) collective-permute-start(bf16[256,1536]{1,0:T(8,128)(2,1)S(1)} %bitcast.394), channel_id=1, source_target_pairs={{0,1},{1,0},{2,3},{3,2},{4,5},{5,4},{6,7},{7,6},{8,9},{9,8},{10,11... | collective-permute-start | bytes 2359304 | tf_op jit(solution)/shard_map/ppermute | solution.py:41
  694.9 22.7 %collective-permute-start.60 = (bf16[2,32,2,768]{3,1,2,0:T(8,128)(2,1)}, bf16[2,32,2,768]{3,1,2,0:T(8,128)(2,1)}, u32[]{:S(2)}, u32[]{:S(2)}) collective-permute-start(bf16[2,32,2,768]{3,1,2,0:T(8,128)(2,1)} %bitcast.381), channel_id=1, source_target_pairs={{0,1},{1,0},{2,3},{3,2},{4,5},{5,4},{6,7},{7,6},{8,9},{9,8},{10,11... | collective-permute-start | bytes 589832 | tf_op jit(solution)/shard_map/ppermute | solution.py:41
  730.1 27.4 %collective-permute-start.57 = (bf16[192,288]{1,0:T(8,128)(2,1)S(1)}, bf16[192,288]{1,0:T(8,128)(2,1)S(1)}, u32[]{:S(2)}, u32[]{:S(2)}) collective-permute-start(bf16[192,288]{1,0:T(8,128)(2,1)S(1)} %bitcast.424), channel_id=1, source_target_pairs={{0,2},{2,0},{4,6},{6,4},{8,10},{10,8},{12,14},{14,12},{16,18},{18,... | collective-permute-start | bytes 331784 | tf_op jit(solution)/shard_map/ppermute | solution.py:41
  730.8 26.8 %collective-permute-start.58 = (bf16[192,288]{1,0:T(8,128)(2,1)S(1)}, bf16[192,288]{1,0:T(8,128)(2,1)S(1)}, u32[]{:S(2)}, u32[]{:S(2)}) collective-permute-start(bf16[192,288]{1,0:T(8,128)(2,1)S(1)} %bitcast.425), channel_id=1, source_target_pairs={{0,4},{2,6},{4,0},{6,2},{8,12},{10,14},{12,8},{14,10},{16,20},{18,... | collective-permute-start | bytes 331784 | tf_op jit(solution)/shard_map/ppermute | solution.py:41
  732.4 25.1 %collective-permute-start.59 = (bf16[192,288]{1,0:T(8,128)(2,1)S(1)}, bf16[192,288]{1,0:T(8,128)(2,1)S(1)}, u32[]{:S(2)}, u32[]{:S(2)}) collective-permute-start(bf16[192,288]{1,0:T(8,128)(2,1)S(1)} %bitcast.426), channel_id=1, source_target_pairs={{0,6},{2,4},{4,2},{6,0},{8,14},{10,12},{12,10},{14,8},{16,22},{18,... | collective-permute-start | bytes 331784 | tf_op jit(solution)/shard_map/ppermute | solution.py:41
  745.1 27.1 %all-to-all-start.1 = ((bf16[16,64,192]{2,1,0:T(8,128)(2,1)}), bf16[16,64,192]{2,1,0:T(8,128)(2,1)S(1)}, u32[]{:S(2)}, u32[]{:S(2)}) async-start(bf16[16,64,192]{2,1,0:T(8,128)(2,1)} %copy.145), calls=%async_computation.2 | async-start | bytes 1048576 | tf_op jit(solution)/shard_map/all_to_all | solution.py:1449
  (170 other events, 2032.6 us)
Sparse Core Ops, SparseCore 0:
  223.7 51.0 all-gather.3
  276.3 113.8 all-gather.5
  394.3 259.7 reduce-scatter.2
  694.3 64.7 reduce-scatter.4

commit v4 on v3

--- a/solution.py
+++ b/solution.py
@@ -566,7 +566,7 @@
             pltpu.VMEM((grid[1], FRAME_TOK, GROUP_WIDTH), BF16),
             pltpu.VMEM((grid[1], FRAME_TOK, GROUP_WIDTH), BF16),
         ],
-        min(62 * MIB, total * 5800 + 16 * MIB),
+        60 * MIB,
         grid[0] * grid[1] * STACK * 2304 * GROUP_WIDTH * 20,
         grid[0] * grid[1] * 500000,
         (*tables, *kv, *query, *grad, *kept, gate, stack_mask()),

time: 792 us -> 786 us (level)
  local copies, waits for them, and re-layouts: 79.2 us -> 62.8 us
  waiting for transfers between devices: 309 us -> 324 us
    ppermute x66, waiting for transfers between devices: 306 us -> 321 us  [swap(): lax.ppermute(value, self.axis, [(i, i ^ mask) for i in range(self.size)])]
    unnamed x278 -> x286, local copies, waits for them, and re-layouts: 30.5 us -> 18.6 us
  transfers between devices with their start and end apart: 72 -> 72, of which waited for: 34 -> 38; matrix products, arithmetic and copies ran while one was open for 23% -> 21% of each run, Pallas kernels for 14% -> 15%
where the time goes in v4:
time: 786 us; the launch traced here: 779 us
  waiting for transfers between devices  324 us (41%)
  Pallas kernels  165 us (21%)
  starting transfers between devices  85.3 us (11%)
  other arithmetic  69.7 us (9%)
  local copies, waits for them, and re-layouts  62.8 us (8%)
  matrix products  54.8 us (7%)
  between operations  16.5 us (2%)
    ppermute x66, waiting for transfers between devices, swap(): lax.ppermute(value, self.axis, [(i, i ^ mask) for i in range(self.size)])  321 us
    pallas_call x8, Pallas kernels, call(): pl.pallas_call(kernel, grid_spec=pltpu.PrefetchScalarGridSpec(num_scalar_...  165 us
    ppermute x66, starting transfers between devices, swap(): lax.ppermute(value, self.axis, [(i, i ^ mask) for i in range(self.size)])  78 us
    dot_general x16, matrix products, mxu(): return lax.dot_general(a, b, (dims, ((), ())), preferred_element_type=F32)  51.9 us
    unnamed x286, local copies, waits for them, and re-layouts  18.6 us
  transfers between devices with their start and end apart: 72, of which 38 were waited for; matrix products, arithmetic and copies ran while one was open for 21% of the time, Pallas kernels for 15%

profile of v4, /device:TPU:0, one launch (start us, length us, event | category | flops | bytes accessed | tf_op | source)
XLA Modules:
  0.0 778.5 jit_solution(4621373199407399916)
XLA Ops:
  24.5 5.2 fusion.86
  48.0 5.5 collective-permute-done.4
  58.8 13.6 %collective-permute-done.9 = bf16[2,32,2,768]{3,2,1,0:T(2,128)(2,1)S(1)} collective-permute-done((bf16[2,32,2,768]{3,2,1,0:T(2,128)(2,1)S(1)}, bf16[2,32,2,768]{3,2,1,0:T(2,128)(2,1)S(1)}, u32[]{:S(2)}, u32[]{:S(2)}) %collective-permute-start.9) | collective-permute-done | bytes 196640 | tf_op jit(solution)/shard_map/ppermute | solution.py:41
  81.3 8.8 %make_heads.1 = (bf16[1,4,128,384]{3,2,1,0:T(8,128)(2,1)S(1)}, bf16[1,4,288,384]{3,2,1,0:T(8,128)(2,1)S(1)}, bf16[1,4,128,384]{3,2,1,0:T(8,128)(2,1)S(1)}, bf16[1,4,288,384]{3,2,1,0:T(8,128)(2,1)S(1)}) custom-call(s32[1]{0:T(128)} %bitcast.5.core_ref, bf16[2,256,1536]{2,1,0:T(8,128)(2,1)S(1)} %pad_maximum_fusion.x_ref, ...), custom_call_target="tpu_custom_call" | custom-call | flops 36238784 | bytes 110100 | tf_op jit(solution)/shard_map/make_heads/pallas_call | solution.py:117
  99.4 8.5 %collective-permute-done.13.refs_8_ = bf16[2,1,288,384]{3,2,1,0:T(8,128)(2,1)S(1)} collective-permute-done((bf16[2,1,288,384]{3,2,1,0:T(8,128)(2,1)S(1)}, bf16[2,1,288,384]{3,2,1,0:T(8,128)(2,1)S(1)}, u32[]{:S(2)}, u32[]{:S(2)}) %collective-permute-start.13) | collective-permute-done | bytes 442400 | tf_op jit(solution)/shard_map/ppermute | solution.py:41
  107.8 26.7 %collective-permute-done.12.refs_7_ = bf16[2,1,288,384]{3,2,1,0:T(8,128)(2,1)S(1)} collective-permute-done((bf16[2,1,288,384]{3,2,1,0:T(8,128)(2,1)S(1)}, bf16[2,1,288,384]{3,2,1,0:T(8,128)(2,1)S(1)}, u32[]{:S(2)}, u32[]{:S(2)}) %collective-permute-start.12) | collective-permute-done | bytes 442400 | tf_op jit(solution)/shard_map/ppermute | solution.py:41
  144.0 6.0 collective-permute-start.19
  154.6 5.2 collective-permute-done.16.refs_11_
  159.8 7.4 collective-permute-done.15.refs_10_
  167.3 38.1 %attention.1 = (bf16[2,1,128,384]{3,2,1,0:T(8,128)(2,1)S(1)}, bf16[2,1,128,384]{3,2,1,0:T(8,128)(2,1)S(1)}, bf16[2,1,128,384]{3,2,1,0:T(8,128)(2,1)S(1)}, bf16[2...) custom-call(s32[1,32]{1,0:T(1,128)S(1)} %bitcast.392, ...), custom_call_target="tpu_custom_call" | custom-call | flops 217432720 | bytes 48000 | tf_op jit(solution)/shard_map/attention/pallas_call | solution.py:117
  217.3 8.0 %collective-permute-done.23.refs_2_ = bf16[2,1,128,384]{3,2,1,0:T(8,128)(2,1)S(1)} collective-permute-done((bf16[2,1,128,384]{3,2,1,0:T(8,128)(2,1)S(1)}, bf16[2,1,128,384]{3,2,1,0:T(8,128)(2,1)S(1)}, u32[]{:S(2)}, u32[]{:S(2)}) %collective-permute-start.23) | collective-permute-done | bytes 196640 | tf_op jit(solution)/shard_map/ppermute | solution.py:41
  250.4 5.9 sine_multiply_fusion
  264.7 5.3 fusion.14
  270.0 12.2 %collective-permute-done.31.refs_1_ = bf16[256,1536]{1,0:T(8,128)(2,1)S(1)} collective-permute-done((bf16[256,1536]{1,0:T(8,128)(2,1)S(1)}, bf16[256,1536]{1,0:T(8,128)(2,1)S(1)}, u32[]{:S(2)}, u32[]{:S(2)}) %collective-permute-start.31) | collective-permute-done | bytes 786464 | tf_op jit(solution)/shard_map/ppermute | solution.py:41
  294.4 13.1 %collective-permute-done.32 = bf16[256,1536]{1,0:T(8,128)(2,1)S(1)} collective-permute-done((bf16[256,1536]{1,0:T(8,128)(2,1)S(1)}, bf16[256,1536]{1,0:T(8,128)(2,1)S(1)}, u32[]{:S(2)}, u32[]{:S(2)}) %collective-permute-start.32) | collective-permute-done | bytes 786464 | tf_op jit(solution)/shard_map/ppermute | solution.py:41
  314.6 5.0 multiply_convert_fusion.1
  319.7 10.8 %collective-permute-done.33.refs_3_ = bf16[256,1536]{1,0:T(8,128)(2,1)S(1)} collective-permute-done((bf16[256,1536]{1,0:T(8,128)(2,1)S(1)}, bf16[256,1536]{1,0:T(8,128)(2,1)S(1)}, u32[]{:S(2)}, u32[]{:S(2)}) %collective-permute-start.33) | collective-permute-done | bytes 786464 | tf_op jit(solution)/shard_map/ppermute | solution.py:41
  346.0 19.1 %ffn_weights.1 = bf16[1536,6144]{1,0:T(8,128)(2,1)} custom-call(bf16[256,1536]{1,0:T(8,128)(2,1)} %copy-done.53, bf16[256,1536]{1,0:T(8,128)(2,1)} %copy-done.66, bf16[256,1536]{1,0:T(8,128)(2,1)} %copy-done.54, bf16[256,1536]{1,0:T(8,128)(2,1)} %copy-done.67, bf16[256,2048]{1,0:T(8,128)(2,1)} %copy-done.63, bf16[256,2048]{1,0:T(8,128)(2,1)} %copy-done.65, ...), custom_call_target="tpu_custom_call" | custom-call | flops 96636768 | bytes 267386 | tf_op jit(solution)/shard_map/ffn_weights/pallas_call | solution.py:117
  377.7 14.7 %collective-permute-done.36 = bf16[256,1536]{1,0:T(8,128)(2,1)S(1)} collective-permute-done((bf16[256,1536]{1,0:T(8,128)(2,1)S(1)}, bf16[256,1536]{1,0:T(8,128)(2,1)S(1)}, u32[]{:S(2)}, u32[]{:S(2)}) %collective-permute-start.36) | collective-permute-done | bytes 786464 | tf_op jit(solution)/shard_map/ppermute | solution.py:41
  411.8 11.8 %collective-permute-done.39.refs_19_ = bf16[2,1,128,384]{3,2,1,0:T(8,128)(2,1)} collective-permute-done((bf16[2,1,128,384]{3,2,1,0:T(8,128)(2,1)S(1)}, bf16[2,1,128,384]{3,2,1,0:T(8,128)(2,1)}, u32[]{:S(2)}, u32[]{:S(2)}) %collective-permute-start.39) | collective-permute-done | bytes 196640 | tf_op jit(solution)/shard_map/ppermute | solution.py:41
  424.2 64.3 %attention_back.1 = (bf16[1,16,128,192]{3,2,1,0:T(8,128)(2,1)}, bf16[2,1,288,384]{3,2,1,0:T(8,128)(2,1)}, bf16[2,1,288,384]{3,2,1,0:T(8,128)(2,1)}, bf16[2,1,288...) custom-call(s32[1,32]{1,0:T(1,128)} %bitcast.393, ...), custom_call_target="tpu_custom_call" | custom-call | flops 543581824 | bytes 80000 | tf_op jit(solution)/shard_map/attention_back/pallas_call | solution.py:117
  496.7 5.1 collective-permute-done.44
  501.9 14.3 %collective-permute-done.43 = bf16[2,1,288,384]{3,2,1,0:T(8,128)(2,1)S(1)} collective-permute-done((bf16[2,1,288,384]{3,2,1,0:T(8,128)(2,1)S(1)}, bf16[2,1,288,384]{3,2,1,0:T(8,128)(2,1)S(1)}, u32[]{:S(2)}, u32[]{:S(2)}) %collective-permute-start.43) | collective-permute-done | bytes 442400 | tf_op jit(solution)/shard_map/ppermute | solution.py:41
  516.4 17.0 %collective-permute-done.42 = bf16[2,1,288,384]{3,2,1,0:T(8,128)(2,1)S(1)} collective-permute-done((bf16[2,1,288,384]{3,2,1,0:T(8,128)(2,1)S(1)}, bf16[2,1,288,384]{3,2,1,0:T(8,128)(2,1)S(1)}, u32[]{:S(2)}, u32[]{:S(2)}) %collective-permute-start.42) | collective-permute-done | bytes 442400 | tf_op jit(solution)/shard_map/ppermute | solution.py:41
  533.5 15.0 %collective-permute-done.41 = bf16[2,1,288,384]{3,2,1,0:T(8,128)(2,1)S(1)} collective-permute-done((bf16[2,1,288,384]{3,2,1,0:T(8,128)(2,1)S(1)}, bf16[2,1,288,384]{3,2,1,0:T(8,128)(2,1)S(1)}, u32[]{:S(2)}, u32[]{:S(2)}) %collective-permute-start.41) | collective-permute-done | bytes 442400 | tf_op jit(solution)/shard_map/ppermute | solution.py:41
  548.6 16.2 %proj_back.1 = (bf16[2,1,144,1152]{3,2,1,0:T(8,128)(2,1)S(1)}, bf16[2,1,144,1152]{3,2,1,0:T(8,128)(2,1)}, bf16[2,1,144,1152]{3,2,1,0:T(8,128)(2,1)}, bf16[2,1,14...) custom-call(s32[1]{0:T(128)} %bitcast.6.refs_0_, bf16[4,2,1,256,1536]{4,3,2,1,0:T(8,128)(2,1)} %bitcast.403, ...), custom_call_target="tpu_custom_call" | custom-call | flops 60397976 | bytes 137625 | tf_op jit(solution)/shard_map/proj_back/pallas_call | solution.py:117
  576.8 24.2 %collective-permute-done.48.refs_3_ = bf16[2,1,144,1152]{3,2,1,0:T(8,128)(2,1)S(1)} collective-permute-done((bf16[2,1,144,1152]{3,2,1,0:T(8,128)(2,1)}, bf16[2,1,144,1152]{3,2,1,0:T(8,128)(2,1)S(1)}, u32[]{:S(2)}, u32[]{:S(2)}) %collective-permute-start.48) | collective-permute-done | bytes 663584 | tf_op jit(solution)/shard_map/ppermute | solution.py:41
  601.0 60.5 %collective-permute-done.47.refs_2_ = bf16[2,1,144,1152]{3,2,1,0:T(8,128)(2,1)S(1)} collective-permute-done((bf16[2,1,144,1152]{3,2,1,0:T(8,128)(2,1)}, bf16[2,1,144,1152]{3,2,1,0:T(8,128)(2,1)S(1)}, u32[]{:S(2)}, u32[]{:S(2)}) %collective-permute-start.47) | collective-permute-done | bytes 663584 | tf_op jit(solution)/shard_map/ppermute | solution.py:41
  673.8 10.9 %in_back.1 = (f32[256,1536]{1,0:T(8,128)}, bf16[1,256,1536]{2,1,0:T(8,128)(2,1)S(1)}, bf16[2,32,1536]{2,1,0:T(8,128)(2,1)S(1)}, f32[8,128]{1,0:T(8,128)S(1)}) custom-call(s32[2]{0:T(128)S(1)} %pad_add_fusion.info_ref, bf16[2,1,144,1152]{3,2,1,0:T(8,128)(2,1)S(1)} %get-tuple-element.130.refs_0_, ...), custom_call_target="tpu_custom_call" | custom-call | flops 36238784 | bytes 117964 | tf_op jit(solution)/shard_map/in_back/pallas_call | solution.py:117
  700.0 7.6 collective-permute-done.55
  716.6 6.1 multiply_reduce_fusion.2
  751.8 8.1 %collective-permute-done.64 = f32[56,128]{1,0:T(8,128)S(1)} collective-permute-done((f32[56,128]{1,0:T(8,128)S(1)}, f32[56,128]{1,0:T(8,128)S(1)}, u32[]{:S(2)}, u32[]{:S(2)}) %collective-permute-start.64) | collective-permute-done | bytes 28704 | tf_op jit(solution)/shard_map/ppermute | solution.py:41
  (643 shorter events, 281.5 us)
Async XLA Ops:
  7.2 386.5 %all-gather.4.cloned.1.call-start = ((), (), s32[]{:S(2)}) async-start(), calls=%async_computation.4 | async-start | bytes 4456448 | tf_op jit(solution)/shard_map/all_gather | solution.py:1240
  14.3 29.7 %collective-permute-start.8 = (bf16[32,2048]{1,0:T(8,128)(2,1)}, bf16[32,2048]{1,0:T(8,128)(2,1)S(1)}, u32[]{:S(2)}, u32[]{:S(2)}) collective-permute-start(bf16[32,2048]{1,0:T(8,128)(2,1)} %get-tuple-element.317), channel_id=1, source_target_pairs={{0,1},{1,0},{2,3},{3,2},{4,5},{5,4},{6,7},{7,6},{8,9},{9,8},{10,11... | collective-permute-start | bytes 393224 | tf_op jit(solution)/shard_map/ppermute | solution.py:41
  29.8 23.7 %collective-permute-start.4 = (bf16[192,2304]{1,0:T(8,128)(2,1)}, bf16[192,2304]{1,0:T(8,128)(2,1)}, u32[]{:S(2)}, u32[]{:S(2)}) collective-permute-start(bf16[192,2304]{1,0:T(8,128)(2,1)} %pad_maximum_fusion.6), channel_id=1, source_target_pairs={{0,1},{1,0},{2,3},{3,2},{4,5},{5,4},{6,7},{7,6},{8,9},{9,8},{10,11... | collective-permute-start | bytes 2654216 | tf_op jit(solution)/shard_map/ppermute | solution.py:41
  35.7 37.4 %collective-permute-start.3 = (bf16[256,1536]{1,0:T(8,128)(2,1)S(1)}, bf16[256,1536]{1,0:T(8,128)(2,1)}, u32[]{:S(2)}, u32[]{:S(2)}) collective-permute-start(bf16[256,1536]{1,0:T(8,128)(2,1)S(1)} %fusion.52), channel_id=1, source_target_pairs={{0,1},{1,0},{2,3},{3,2},{4,5},{5,4},{6,7},{7,6},{8,9},{9,8},{10,11... | collective-permute-start | bytes 2359304 | tf_op jit(solution)/shard_map/ppermute | solution.py:41
  53.5 20.9 %collective-permute-start.5 = (bf16[192,2304]{1,0:T(8,128)(2,1)}, bf16[192,2304]{1,0:T(8,128)(2,1)}, u32[]{:S(2)}, u32[]{:S(2)}) collective-permute-start(bf16[192,2304]{1,0:T(8,128)(2,1)} %collective-permute-done.4), channel_id=1, source_target_pairs={{0,4},{2,6},{4,0},{6,2},{8,12},{10,14},{12,8},{14,10},{16,20},{18,... | collective-permute-start | bytes 2654216 | tf_op jit(solution)/shard_map/ppermute | solution.py:41
  96.6 38.0 %collective-permute-start.12 = (bf16[2,1,288,384]{3,2,1,0:T(8,128)(2,1)S(1)}, bf16[2,1,288,384]{3,2,1,0:T(8,128)(2,1)S(1)}, u32[]{:S(2)}, u32[]{:S(2)}) collective-permute-start(bf16[2,1,288,384]{3,2,1,0:T(8,128)(2,1)S(1)} %pad_maximum_fusion.13), channel_id=1, source_target_pairs={{0,16},{2,18},{4,20},{6,22},{8,24},{10,26},{12,28},{14,30},{16,0},... | collective-permute-start | bytes 1327112 | tf_op jit(solution)/shard_map/ppermute | solution.py:41
  96.7 37.9 %collective-permute-start.11 = (bf16[2,1,288,384]{3,2,1,0:T(8,128)(2,1)S(1)}, bf16[2,1,288,384]{3,2,1,0:T(8,128)(2,1)S(1)}, u32[]{:S(2)}, u32[]{:S(2)}) collective-permute-start(bf16[2,1,288,384]{3,2,1,0:T(8,128)(2,1)S(1)} %pad_maximum_fusion.12), channel_id=1, source_target_pairs={{0,8},{2,10},{4,12},{6,14},{8,0},{10,2},{12,4},{14,6},{16,24},{18,... | collective-permute-start | bytes 1327112 | tf_op jit(solution)/shard_map/ppermute | solution.py:41
  97.7 43.1 %collective-permute-start.14 = (bf16[2,1,288,384]{3,2,1,0:T(8,128)(2,1)S(1)}, bf16[2,1,288,384]{3,2,1,0:T(8,128)(2,1)S(1)}, u32[]{:S(2)}, u32[]{:S(2)}) collective-permute-start(bf16[2,1,288,384]{3,2,1,0:T(8,128)(2,1)S(1)} %pad_maximum_fusion.11.refs_5_), channel_id=1, source_target_pairs={{0,4},{2,6},{4,0},{6,2},{8,12},{10,14},{12,8},{14,10},{16,20},{18,... | collective-permute-start | bytes 1327112 | tf_op jit(solution)/shard_map/ppermute | solution.py:41
  138.7 21.1 %collective-permute-start.16 = (bf16[2,1,288,384]{3,2,1,0:T(8,128)(2,1)S(1)}, bf16[2,1,288,384]{3,2,1,0:T(8,128)(2,1)S(1)}, u32[]{:S(2)}, u32[]{:S(2)}) collective-permute-start(bf16[2,1,288,384]{3,2,1,0:T(8,128)(2,1)S(1)} %collective-permute-done.12.refs_7_), channel_id=1, source_target_pairs={{0,4},{2,6},{4,0},{6,2},{8,12},{10,14},{12,8},{14,10},{16,20},{18,... | collective-permute-start | bytes 1327112 | tf_op jit(solution)/shard_map/ppermute | solution.py:41
  139.2 28.0 %collective-permute-start.15 = (bf16[2,1,288,384]{3,2,1,0:T(8,128)(2,1)S(1)}, bf16[2,1,288,384]{3,2,1,0:T(8,128)(2,1)S(1)}, u32[]{:S(2)}, u32[]{:S(2)}) collective-permute-start(bf16[2,1,288,384]{3,2,1,0:T(8,128)(2,1)S(1)} %collective-permute-done.11.refs_6_), channel_id=1, source_target_pairs={{0,4},{2,6},{4,0},{6,2},{8,12},{10,14},{12,8},{14,10},{16,20},{18,... | collective-permute-start | bytes 1327112 | tf_op jit(solution)/shard_map/ppermute | solution.py:41
  225.3 168.4 %all-gather.6.cloned.1.call-start = ((), (), s32[]{:S(2)}) async-start(), calls=%async_computation.7 | async-start | bytes 7864320 | tf_op jit(solution)/shard_map/all_gather | solution.py:1243
  230.8 440.1 %reduce-scatter.3.cloned.1.call-start = ((), (), s32[]{:S(2)}) async-start(), calls=%async_computation.5 | async-start | bytes 20054016 | tf_op jit(solution)/shard_map/reduce_scatter | solution.py:1299
  239.6 19.9 %collective-permute-start.26 = (bf16[256,1536]{1,0:T(8,128)(2,1)}, bf16[256,1536]{1,0:T(8,128)(2,1)}, u32[]{:S(2)}, u32[]{:S(2)}) collective-permute-start(bf16[256,1536]{1,0:T(8,128)(2,1)} %bitcast.46), channel_id=1, source_target_pairs={{0,1},{1,0},{2,3},{3,2},{4,5},{5,4},{6,7},{7,6},{8,9},{9,8},{10,11... | collective-permute-start | bytes 2359304 | tf_op jit(solution)/shard_map/ppermute | solution.py:41
  263.4 18.8 %collective-permute-start.31 = (bf16[256,1536]{1,0:T(8,128)(2,1)S(1)}, bf16[256,1536]{1,0:T(8,128)(2,1)S(1)}, u32[]{:S(2)}, u32[]{:S(2)}) collective-permute-start(bf16[256,1536]{1,0:T(8,128)(2,1)S(1)} %fusion.50.refs_0_), channel_id=1, source_target_pairs={{0,1},{1,0},{2,3},{3,2},{4,5},{5,4},{6,7},{7,6},{8,9},{9,8},{10,11... | collective-permute-start | bytes 2359304 | tf_op jit(solution)/shard_map/ppermute | solution.py:41
  289.6 17.9 %collective-permute-start.32 = (bf16[256,1536]{1,0:T(8,128)(2,1)S(1)}, bf16[256,1536]{1,0:T(8,128)(2,1)S(1)}, u32[]{:S(2)}, u32[]{:S(2)}) collective-permute-start(bf16[256,1536]{1,0:T(8,128)(2,1)S(1)} %convolution_convert_fusion), channel_id=1, source_target_pairs={{0,1},{1,0},{2,3},{3,2},{4,5},{5,4},{6,7},{7,6},{8,9},{9,8},{10,11... | collective-permute-start | bytes 2359304 | tf_op jit(solution)/shard_map/ppermute | solution.py:41
  339.9 25.2 %collective-permute-start.34 = (bf16[256,1536]{1,0:T(8,128)(2,1)}, bf16[256,1536]{1,0:T(8,128)(2,1)}, u32[]{:S(2)}, u32[]{:S(2)}) collective-permute-start(bf16[256,1536]{1,0:T(8,128)(2,1)} %fusion.30), channel_id=1, source_target_pairs={{0,1},{1,0},{2,3},{3,2},{4,5},{5,4},{6,7},{7,6},{8,9},{9,8},{10,11... | collective-permute-start | bytes 2359304 | tf_op jit(solution)/shard_map/ppermute | solution.py:41
  365.1 404.8 %reduce-scatter.5.cloned.1.call-start = ((), (), s32[]{:S(2)}) async-start(), calls=%async_computation.6 | async-start | bytes 2506752 | tf_op jit(solution)/shard_map/reduce_scatter | solution.py:1299
  403.5 20.1 %collective-permute-start.39 = (bf16[2,1,128,384]{3,2,1,0:T(8,128)(2,1)S(1)}, bf16[2,1,128,384]{3,2,1,0:T(8,128)(2,1)}, u32[]{:S(2)}, u32[]{:S(2)}) collective-permute-start(bf16[2,1,128,384]{3,2,1,0:T(8,128)(2,1)S(1)} %pad_maximum_fusion.25), channel_id=1, source_target_pairs={{0,16},{2,18},{4,20},{6,22},{8,24},{10,26},{12,28},{14,30},{16,0},... | collective-permute-start | bytes 589832 | tf_op jit(solution)/shard_map/ppermute | solution.py:41
  491.5 24.7 %collective-permute-start.43 = (bf16[2,1,288,384]{3,2,1,0:T(8,128)(2,1)S(1)}, bf16[2,1,288,384]{3,2,1,0:T(8,128)(2,1)S(1)}, u32[]{:S(2)}, u32[]{:S(2)}) collective-permute-start(bf16[2,1,288,384]{3,2,1,0:T(8,128)(2,1)S(1)} %copy-done.116), channel_id=1, source_target_pairs={{0,4},{2,6},{4,0},{6,2},{8,12},{10,14},{12,8},{14,10},{16,20},{18,... | collective-permute-start | bytes 1327112 | tf_op jit(solution)/shard_map/ppermute | solution.py:41
  494.7 38.8 %collective-permute-start.42 = (bf16[2,1,288,384]{3,2,1,0:T(8,128)(2,1)S(1)}, bf16[2,1,288,384]{3,2,1,0:T(8,128)(2,1)S(1)}, u32[]{:S(2)}, u32[]{:S(2)}) collective-permute-start(bf16[2,1,288,384]{3,2,1,0:T(8,128)(2,1)S(1)} %copy-done.115), channel_id=1, source_target_pairs={{0,4},{2,6},{4,0},{6,2},{8,12},{10,14},{12,8},{14,10},{16,20},{18,... | collective-permute-start | bytes 1327112 | tf_op jit(solution)/shard_map/ppermute | solution.py:41
  495.2 53.4 %collective-permute-start.41 = (bf16[2,1,288,384]{3,2,1,0:T(8,128)(2,1)S(1)}, bf16[2,1,288,384]{3,2,1,0:T(8,128)(2,1)S(1)}, u32[]{:S(2)}, u32[]{:S(2)}) collective-permute-start(bf16[2,1,288,384]{3,2,1,0:T(8,128)(2,1)S(1)} %copy-done.114), channel_id=1, source_target_pairs={{0,4},{2,6},{4,0},{6,2},{8,12},{10,14},{12,8},{14,10},{16,20},{18,... | collective-permute-start | bytes 1327112 | tf_op jit(solution)/shard_map/ppermute | solution.py:41
  567.1 33.9 %collective-permute-start.48 = (bf16[2,1,144,1152]{3,2,1,0:T(8,128)(2,1)}, bf16[2,1,144,1152]{3,2,1,0:T(8,128)(2,1)S(1)}, u32[]{:S(2)}, u32[]{:S(2)}) collective-permute-start(bf16[2,1,144,1152]{3,2,1,0:T(8,128)(2,1)} %get-tuple-element.135), channel_id=1, source_target_pairs={{0,24},{2,26},{4,28},{6,30},{8,16},{10,18},{12,20},{14,22},{16,8},... | collective-permute-start | bytes 1990664 | tf_op jit(solution)/shard_map/ppermute | solution.py:41
  569.1 92.4 %collective-permute-start.47 = (bf16[2,1,144,1152]{3,2,1,0:T(8,128)(2,1)}, bf16[2,1,144,1152]{3,2,1,0:T(8,128)(2,1)S(1)}, u32[]{:S(2)}, u32[]{:S(2)}) collective-permute-start(bf16[2,1,144,1152]{3,2,1,0:T(8,128)(2,1)} %get-tuple-element.133), channel_id=1, source_target_pairs={{0,16},{2,18},{4,20},{6,22},{8,24},{10,26},{12,28},{14,30},{16,0},... | collective-permute-start | bytes 1990664 | tf_op jit(solution)/shard_map/ppermute | solution.py:41
  569.1 92.5 %collective-permute-start.46 = (bf16[2,1,144,1152]{3,2,1,0:T(8,128)(2,1)}, bf16[2,1,144,1152]{3,2,1,0:T(8,128)(2,1)S(1)}, u32[]{:S(2)}, u32[]{:S(2)}) collective-permute-start(bf16[2,1,144,1152]{3,2,1,0:T(8,128)(2,1)} %get-tuple-element.131), channel_id=1, source_target_pairs={{0,8},{2,10},{4,12},{6,14},{8,0},{10,2},{12,4},{14,6},{16,24},{18,... | collective-permute-start | bytes 1990664 | tf_op jit(solution)/shard_map/ppermute | solution.py:41
  575.8 88.4 %collective-permute-start.50 = (bf16[2,1,192,576]{3,2,1,0:T(8,128)(2,1)}, bf16[2,1,192,576]{3,2,1,0:T(8,128)(2,1)}, u32[]{:S(2)}, u32[]{:S(2)}) collective-permute-start(bf16[2,1,192,576]{3,2,1,0:T(8,128)(2,1)} %constant_dynamic-slice_fusion.24), channel_id=1, source_target_pairs={{0,4},{2,6},{4,0},{6,2},{8,12},{10,14},{12,8},{14,10},{16,20},{18,... | collective-permute-start | bytes 1327112 | tf_op jit(solution)/shard_map/ppermute | solution.py:41
  668.1 17.5 %collective-permute-start.52 = (bf16[192,576]{0,1:T(8,128)(2,1)}, bf16[192,576]{0,1:T(8,128)(2,1)}, u32[]{:S(2)}, u32[]{:S(2)}) collective-permute-start(bf16[192,576]{0,1:T(8,128)(2,1)} %bitcast.419), channel_id=1, source_target_pairs={{0,1},{1,0},{2,3},{3,2},{4,5},{5,4},{6,7},{7,6},{8,9},{9,8},{10,11... | collective-permute-start | bytes 663560 | tf_op jit(solution)/shard_map/ppermute | solution.py:41
  687.4 29.1 %collective-permute-start.51 = (bf16[256,1536]{1,0:T(8,128)(2,1)S(1)}, bf16[256,1536]{1,0:T(8,128)(2,1)}, u32[]{:S(2)}, u32[]{:S(2)}) collective-permute-start(bf16[256,1536]{1,0:T(8,128)(2,1)S(1)} %bitcast.394), channel_id=1, source_target_pairs={{0,1},{1,0},{2,3},{3,2},{4,5},{5,4},{6,7},{7,6},{8,9},{9,8},{10,11... | collective-permute-start | bytes 2359304 | tf_op jit(solution)/shard_map/ppermute | solution.py:41
  689.3 22.2 %collective-permute-start.60 = (bf16[2,32,2,768]{3,1,2,0:T(8,128)(2,1)}, bf16[2,32,2,768]{3,1,2,0:T(8,128)(2,1)}, u32[]{:S(2)}, u32[]{:S(2)}) collective-permute-start(bf16[2,32,2,768]{3,1,2,0:T(8,128)(2,1)} %bitcast.381), channel_id=1, source_target_pairs={{0,1},{1,0},{2,3},{3,2},{4,5},{5,4},{6,7},{7,6},{8,9},{9,8},{10,11... | collective-permute-start | bytes 589832 | tf_op jit(solution)/shard_map/ppermute | solution.py:41
  724.0 27.4 %collective-permute-start.57 = (bf16[192,288]{1,0:T(8,128)(2,1)S(1)}, bf16[192,288]{1,0:T(8,128)(2,1)S(1)}, u32[]{:S(2)}, u32[]{:S(2)}) collective-permute-start(bf16[192,288]{1,0:T(8,128)(2,1)S(1)} %bitcast.426), channel_id=1, source_target_pairs={{0,2},{2,0},{4,6},{6,4},{8,10},{10,8},{12,14},{14,12},{16,18},{18,... | collective-permute-start | bytes 331784 | tf_op jit(solution)/shard_map/ppermute | solution.py:41
  724.7 26.7 %collective-permute-start.58 = (bf16[192,288]{1,0:T(8,128)(2,1)S(1)}, bf16[192,288]{1,0:T(8,128)(2,1)S(1)}, u32[]{:S(2)}, u32[]{:S(2)}) collective-permute-start(bf16[192,288]{1,0:T(8,128)(2,1)S(1)} %bitcast.427), channel_id=1, source_target_pairs={{0,4},{2,6},{4,0},{6,2},{8,12},{10,14},{12,8},{14,10},{16,20},{18,... | collective-permute-start | bytes 331784 | tf_op jit(solution)/shard_map/ppermute | solution.py:41
  725.6 25.7 %collective-permute-start.59 = (bf16[192,288]{1,0:T(8,128)(2,1)S(1)}, bf16[192,288]{1,0:T(8,128)(2,1)S(1)}, u32[]{:S(2)}, u32[]{:S(2)}) collective-permute-start(bf16[192,288]{1,0:T(8,128)(2,1)S(1)} %bitcast.428), channel_id=1, source_target_pairs={{0,6},{2,4},{4,2},{6,0},{8,14},{10,12},{12,10},{14,8},{16,22},{18,... | collective-permute-start | bytes 331784 | tf_op jit(solution)/shard_map/ppermute | solution.py:41
  738.4 27.1 %all-to-all-start.1 = ((bf16[16,64,192]{2,1,0:T(8,128)(2,1)}), bf16[16,64,192]{2,1,0:T(8,128)(2,1)S(1)}, u32[]{:S(2)}, u32[]{:S(2)}) async-start(bf16[16,64,192]{2,1,0:T(8,128)(2,1)} %copy.145), calls=%async_computation.2 | async-start | bytes 1048576 | tf_op jit(solution)/shard_map/all_to_all | solution.py:1449
  (174 other events, 3013.5 us)
Sparse Core Ops, SparseCore 0:
  225.4 51.1 all-gather.3
  278.2 113.8 all-gather.5
  396.2 256.8 reduce-scatter.2
  688.7 63.8 reduce-scatter.4

commit v5 on v4

--- a/solution.py
+++ b/solution.py
@@ -1243,12 +1243,8 @@
         normed_group = lax.all_gather(late_normed, "dp", axis_index_groups=members)
     else:
         normed_group = late_normed[None]
-    far_cos, far_sin = rope_lanes(jnp.repeat(far_ids.reshape(-1), FRAME_TOK))
-    far_shape = (groups, half, 2 * tokens, 128)
-    far_cos = far_cos.reshape(far_shape)
-    far_sin = far_sin.reshape(far_shape)
     mix_got = [xs.swap(mix_rest[s - 1], s) for s in range(1, fsdp)]
-    mix_got = [held(v, far_cos, far_sin) for v in mix_got]
+    mix_got = [held(v, far_ids) for v in mix_got]
     for v in mix_got:
         mix_first = mix_first + v.astype(F32)
     mixed_out = frame_view(mix_first)
@@ -1261,9 +1257,15 @@
     gate_part = [mxu(x, w_gate_up[0]) for x in ffn_all]
     up_part = [mxu(x, w_gate_up[1]) for x in ffn_all]
     hidden = [(jax.nn.silu(g) * u).astype(BF16) for g, u in zip(gate_part, up_part)]
-    ffn_out = swapped_sum(
-        mxu(hidden[0], w_down), [mxu(h, w_down).astype(BF16) for h in hidden[1:]]
-    )
+    far_ids = held(far_ids, hidden[-1])
+    far_cos, far_sin = rope_lanes(jnp.repeat(far_ids.reshape(-1), FRAME_TOK))
+    far_shape = (groups, half, 2 * tokens, 128)
+    far_cos = far_cos.reshape(far_shape)
+    far_sin = far_sin.reshape(far_shape)
+    ffn_got = [xs.swap(mxu(h, w_down).astype(BF16), s + 1) for s, h in enumerate(hidden[1:])]
+    ffn_out = mxu(hidden[0], w_down)
+    for v in ffn_got:
+        ffn_out = ffn_out + held(v, far_cos, far_sin).astype(F32)
     ffn_out = frame_view(ffn_out)
     unit_out, inv_out = unit_rms(ffn_out)
     tanh_ffn = jnp.tanh(gate_ffn)

time: 786 us -> 782 us (level)
  waiting for transfers between devices: 324 us -> 316 us
    unnamed x286 -> x320, local copies, waits for them, and re-layouts: 18.6 us -> 17.9 us
  transfers between devices with their start and end apart: 72 -> 72, of which waited for: 38 -> 37; matrix products, arithmetic and copies ran while one was open for 21% -> 22% of each run, Pallas kernels for 15% -> 15%
where the time goes in v5:
time: 782 us; the launch traced here: 776 us
  waiting for transfers between devices  316 us (40%)
  Pallas kernels  163 us (21%)
  starting transfers between devices  92.5 us (12%)
  other arithmetic  69.3 us (9%)
  local copies, waits for them, and re-layouts  61.3 us (8%)
  matrix products  57 us (7%)
  between operations  16.5 us (2%)
    ppermute x66, waiting for transfers between devices, swap(): lax.ppermute(value, self.axis, [(i, i ^ mask) for i in range(self.size)])  313 us
    pallas_call x8, Pallas kernels, call(): pl.pallas_call(kernel, grid_spec=pltpu.PrefetchScalarGridSpec(num_scalar_...  163 us
    ppermute x66, starting transfers between devices, swap(): lax.ppermute(value, self.axis, [(i, i ^ mask) for i in range(self.size)])  84.9 us
    dot_general x16, matrix products, mxu(): return lax.dot_general(a, b, (dims, ((), ())), preferred_element_type=F32)  54.1 us
    unnamed x320, local copies, waits for them, and re-layouts  17.9 us
  transfers between devices with their start and end apart: 72, of which 37 were waited for; matrix products, arithmetic and copies ran while one was open for 22% of the time, Pallas kernels for 15%

profile of v5, /device:TPU:0, one launch (start us, length us, event | category | flops | bytes accessed | tf_op | source)
XLA Modules:
  0.0 776.1 jit_solution(17079785203750581113)
XLA Ops:
  45.5 5.3 collective-permute-done.4
  55.8 13.9 %collective-permute-done.9 = bf16[2,32,2,768]{3,2,1,0:T(2,128)(2,1)S(1)} collective-permute-done((bf16[2,32,2,768]{3,2,1,0:T(2,128)(2,1)S(1)}, bf16[2,32,2,768]{3,2,1,0:T(2,128)(2,1)S(1)}, u32[]{:S(2)}, u32[]{:S(2)}) %collective-permute-start.9) | collective-permute-done | bytes 196640 | tf_op jit(solution)/shard_map/ppermute | solution.py:41
  78.5 8.6 %make_heads.1 = (bf16[1,4,128,384]{3,2,1,0:T(8,128)(2,1)S(1)}, bf16[1,4,288,384]{3,2,1,0:T(8,128)(2,1)S(1)}, bf16[1,4,128,384]{3,2,1,0:T(8,128)(2,1)S(1)}, bf16[1,4,288,384]{3,2,1,0:T(8,128)(2,1)S(1)}) custom-call(s32[1]{0:T(128)} %bitcast.5.core_ref, bf16[2,256,1536]{2,1,0:T(8,128)(2,1)S(1)} %pad_maximum_fusion.x_ref, ...), custom_call_target="tpu_custom_call" | custom-call | flops 36238784 | bytes 110100 | tf_op jit(solution)/shard_map/make_heads/pallas_call | solution.py:117
  96.3 8.5 %collective-permute-done.13.refs_8_ = bf16[2,1,288,384]{3,2,1,0:T(8,128)(2,1)S(1)} collective-permute-done((bf16[2,1,288,384]{3,2,1,0:T(8,128)(2,1)S(1)}, bf16[2,1,288,384]{3,2,1,0:T(8,128)(2,1)S(1)}, u32[]{:S(2)}, u32[]{:S(2)}) %collective-permute-start.13) | collective-permute-done | bytes 442400 | tf_op jit(solution)/shard_map/ppermute | solution.py:41
  104.8 26.7 %collective-permute-done.12.refs_7_ = bf16[2,1,288,384]{3,2,1,0:T(8,128)(2,1)S(1)} collective-permute-done((bf16[2,1,288,384]{3,2,1,0:T(8,128)(2,1)S(1)}, bf16[2,1,288,384]{3,2,1,0:T(8,128)(2,1)S(1)}, u32[]{:S(2)}, u32[]{:S(2)}) %collective-permute-start.12) | collective-permute-done | bytes 442400 | tf_op jit(solution)/shard_map/ppermute | solution.py:41
  141.0 6.0 collective-permute-start.19
  156.7 7.4 collective-permute-done.15.refs_10_
  164.2 36.9 %attention.1 = (bf16[2,1,128,384]{3,2,1,0:T(8,128)(2,1)S(1)}, bf16[2,1,128,384]{3,2,1,0:T(8,128)(2,1)S(1)}, bf16[2,1,128,384]{3,2,1,0:T(8,128)(2,1)S(1)}, bf16[2...) custom-call(s32[1,32]{1,0:T(1,128)S(1)} %bitcast.398, ...), custom_call_target="tpu_custom_call" | custom-call | flops 217432720 | bytes 48000 | tf_op jit(solution)/shard_map/attention/pallas_call | solution.py:117
  214.9 7.4 collective-permute-done.23.refs_2_
  245.8 7.5 collective-permute-done.26
  258.4 5.4 fusion.14
  267.2 9.3 %collective-permute-done.31.refs_1_ = bf16[256,1536]{1,0:T(8,128)(2,1)S(1)} collective-permute-done((bf16[256,1536]{1,0:T(8,128)(2,1)S(1)}, bf16[256,1536]{1,0:T(8,128)(2,1)S(1)}, u32[]{:S(2)}, u32[]{:S(2)}) %collective-permute-start.31) | collective-permute-done | bytes 786464 | tf_op jit(solution)/shard_map/ppermute | solution.py:41
  288.3 5.9 sine_multiply_fusion
  294.2 8.3 %collective-permute-done.32 = bf16[256,1536]{1,0:T(8,128)(2,1)} collective-permute-done((bf16[256,1536]{1,0:T(8,128)(2,1)}, bf16[256,1536]{1,0:T(8,128)(2,1)}, u32[]{:S(2)}, u32[]{:S(2)}) %collective-permute-start.32) | collective-permute-done | bytes 786464 | tf_op jit(solution)/shard_map/ppermute | solution.py:41
  308.9 5.7 multiply_convert_fusion.1
  314.6 10.4 %collective-permute-done.33.refs_3_ = bf16[256,1536]{1,0:T(8,128)(2,1)S(1)} collective-permute-done((bf16[256,1536]{1,0:T(8,128)(2,1)S(1)}, bf16[256,1536]{1,0:T(8,128)(2,1)S(1)}, u32[]{:S(2)}, u32[]{:S(2)}) %collective-permute-start.33) | collective-permute-done | bytes 786464 | tf_op jit(solution)/shard_map/ppermute | solution.py:41
  340.3 19.5 %ffn_weights.1 = bf16[1536,6144]{1,0:T(8,128)(2,1)} custom-call(bf16[256,1536]{1,0:T(8,128)(2,1)} %copy-done.51, bf16[256,1536]{1,0:T(8,128)(2,1)} %copy-done.65, bf16[256,1536]{1,0:T(8,128)(2,1)} %copy-done.52, bf16[256,1536]{1,0:T(8,128)(2,1)} %copy-done.66, bf16[256,2048]{1,0:T(8,128)(2,1)} %copy-done.62, bf16[256,2048]{1,0:T(8,128)(2,1)} %copy-done.64, ...), custom_call_target="tpu_custom_call" | custom-call | flops 96636768 | bytes 267386 | tf_op jit(solution)/shard_map/ffn_weights/pallas_call | solution.py:117
  373.6 14.1 %collective-permute-done.36 = bf16[256,1536]{1,0:T(8,128)(2,1)S(1)} collective-permute-done((bf16[256,1536]{1,0:T(8,128)(2,1)S(1)}, bf16[256,1536]{1,0:T(8,128)(2,1)S(1)}, u32[]{:S(2)}, u32[]{:S(2)}) %collective-permute-start.36) | collective-permute-done | bytes 786464 | tf_op jit(solution)/shard_map/ppermute | solution.py:41
  398.5 5.4 collective-permute-start.39
  408.2 10.4 %collective-permute-done.39.refs_19_ = bf16[2,1,128,384]{3,2,1,0:T(8,128)(2,1)} collective-permute-done((bf16[2,1,128,384]{3,2,1,0:T(8,128)(2,1)S(1)}, bf16[2,1,128,384]{3,2,1,0:T(8,128)(2,1)}, u32[]{:S(2)}, u32[]{:S(2)}) %collective-permute-start.39) | collective-permute-done | bytes 196640 | tf_op jit(solution)/shard_map/ppermute | solution.py:41
  419.2 64.6 %attention_back.1 = (bf16[1,16,128,192]{3,2,1,0:T(8,128)(2,1)}, bf16[2,1,288,384]{3,2,1,0:T(8,128)(2,1)}, bf16[2,1,288,384]{3,2,1,0:T(8,128)(2,1)}, bf16[2,1,288...) custom-call(s32[1,32]{1,0:T(1,128)} %bitcast.399, ...), custom_call_target="tpu_custom_call" | custom-call | flops 543581824 | bytes 80000 | tf_op jit(solution)/shard_map/attention_back/pallas_call | solution.py:117
  495.4 11.7 %collective-permute-done.43 = bf16[2,1,288,384]{3,2,1,0:T(8,128)(2,1)S(1)} collective-permute-done((bf16[2,1,288,384]{3,2,1,0:T(8,128)(2,1)S(1)}, bf16[2,1,288,384]{3,2,1,0:T(8,128)(2,1)S(1)}, u32[]{:S(2)}, u32[]{:S(2)}) %collective-permute-start.43) | collective-permute-done | bytes 442400 | tf_op jit(solution)/shard_map/ppermute | solution.py:41
  507.3 18.8 %collective-permute-done.42 = bf16[2,1,288,384]{3,2,1,0:T(8,128)(2,1)S(1)} collective-permute-done((bf16[2,1,288,384]{3,2,1,0:T(8,128)(2,1)S(1)}, bf16[2,1,288,384]{3,2,1,0:T(8,128)(2,1)S(1)}, u32[]{:S(2)}, u32[]{:S(2)}) %collective-permute-start.42) | collective-permute-done | bytes 442400 | tf_op jit(solution)/shard_map/ppermute | solution.py:41
  526.2 13.9 %collective-permute-done.41 = bf16[2,1,288,384]{3,2,1,0:T(8,128)(2,1)S(1)} collective-permute-done((bf16[2,1,288,384]{3,2,1,0:T(8,128)(2,1)S(1)}, bf16[2,1,288,384]{3,2,1,0:T(8,128)(2,1)S(1)}, u32[]{:S(2)}, u32[]{:S(2)}) %collective-permute-start.41) | collective-permute-done | bytes 442400 | tf_op jit(solution)/shard_map/ppermute | solution.py:41
  540.3 16.0 %proj_back.1 = (bf16[2,1,144,1152]{3,2,1,0:T(8,128)(2,1)S(1)}, bf16[2,1,144,1152]{3,2,1,0:T(8,128)(2,1)}, bf16[2,1,144,1152]{3,2,1,0:T(8,128)(2,1)}, bf16[2,1,14...) custom-call(s32[1]{0:T(128)} %bitcast.6.refs_0_, bf16[4,2,1,256,1536]{4,3,2,1,0:T(8,128)(2,1)} %bitcast.409, ...), custom_call_target="tpu_custom_call" | custom-call | flops 60397976 | bytes 137625 | tf_op jit(solution)/shard_map/proj_back/pallas_call | solution.py:117
  558.5 5.8 collective-permute-start.45
  573.5 24.9 %collective-permute-done.48.refs_3_ = bf16[2,1,144,1152]{3,2,1,0:T(8,128)(2,1)S(1)} collective-permute-done((bf16[2,1,144,1152]{3,2,1,0:T(8,128)(2,1)}, bf16[2,1,144,1152]{3,2,1,0:T(8,128)(2,1)S(1)}, u32[]{:S(2)}, u32[]{:S(2)}) %collective-permute-start.48) | collective-permute-done | bytes 663584 | tf_op jit(solution)/shard_map/ppermute | solution.py:41
  598.3 58.9 %collective-permute-done.47.refs_2_ = bf16[2,1,144,1152]{3,2,1,0:T(8,128)(2,1)S(1)} collective-permute-done((bf16[2,1,144,1152]{3,2,1,0:T(8,128)(2,1)}, bf16[2,1,144,1152]{3,2,1,0:T(8,128)(2,1)S(1)}, u32[]{:S(2)}, u32[]{:S(2)}) %collective-permute-start.47) | collective-permute-done | bytes 663584 | tf_op jit(solution)/shard_map/ppermute | solution.py:41
  670.0 10.9 %in_back.1 = (f32[256,1536]{1,0:T(8,128)}, bf16[1,256,1536]{2,1,0:T(8,128)(2,1)S(1)}, bf16[2,32,1536]{2,1,0:T(8,128)(2,1)S(1)}, f32[8,128]{1,0:T(8,128)S(1)}) custom-call(s32[2]{0:T(128)S(1)} %pad_add_fusion.info_ref, bf16[2,1,144,1152]{3,2,1,0:T(8,128)(2,1)S(1)} %get-tuple-element.134.refs_0_, ...), custom_call_target="tpu_custom_call" | custom-call | flops 36238784 | bytes 117964 | tf_op jit(solution)/shard_map/in_back/pallas_call | solution.py:117
  696.2 7.7 collective-permute-done.55
  714.4 5.4 multiply_reduce_fusion.2
  749.7 7.9 %collective-permute-done.64 = f32[56,128]{1,0:T(8,128)S(1)} collective-permute-done((f32[56,128]{1,0:T(8,128)S(1)}, f32[56,128]{1,0:T(8,128)S(1)}, u32[]{:S(2)}, u32[]{:S(2)}) %collective-permute-start.64) | collective-permute-done | bytes 28704 | tf_op jit(solution)/shard_map/ppermute | solution.py:41
  (678 shorter events, 290.4 us)
Async XLA Ops:
  7.2 381.7 %all-gather.4.cloned.1.call-start = ((), (), s32[]{:S(2)}) async-start(), calls=%async_computation.4 | async-start | bytes 4456448 | tf_op jit(solution)/shard_map/all_gather | solution.py:1240
  13.7 28.2 %collective-permute-start.8 = (bf16[32,2048]{1,0:T(8,128)(2,1)S(1)}, bf16[32,2048]{1,0:T(8,128)(2,1)S(1)}, u32[]{:S(2)}, u32[]{:S(2)}) collective-permute-start(bf16[32,2048]{1,0:T(8,128)(2,1)S(1)} %get-tuple-element.321), channel_id=1, source_target_pairs={{0,1},{1,0},{2,3},{3,2},{4,5},{5,4},{6,7},{7,6},{8,9},{9,8},{10,11... | collective-permute-start | bytes 393224 | tf_op jit(solution)/shard_map/ppermute | solution.py:41
  27.1 23.7 %collective-permute-start.4 = (bf16[192,2304]{1,0:T(8,128)(2,1)}, bf16[192,2304]{1,0:T(8,128)(2,1)}, u32[]{:S(2)}, u32[]{:S(2)}) collective-permute-start(bf16[192,2304]{1,0:T(8,128)(2,1)} %pad_maximum_fusion.6), channel_id=1, source_target_pairs={{0,1},{1,0},{2,3},{3,2},{4,5},{5,4},{6,7},{7,6},{8,9},{9,8},{10,11... | collective-permute-start | bytes 2654216 | tf_op jit(solution)/shard_map/ppermute | solution.py:41
  33.0 37.4 %collective-permute-start.3 = (bf16[256,1536]{1,0:T(8,128)(2,1)S(1)}, bf16[256,1536]{1,0:T(8,128)(2,1)}, u32[]{:S(2)}, u32[]{:S(2)}) collective-permute-start(bf16[256,1536]{1,0:T(8,128)(2,1)S(1)} %fusion.52), channel_id=1, source_target_pairs={{0,1},{1,0},{2,3},{3,2},{4,5},{5,4},{6,7},{7,6},{8,9},{9,8},{10,11... | collective-permute-start | bytes 2359304 | tf_op jit(solution)/shard_map/ppermute | solution.py:41
  50.8 20.9 %collective-permute-start.5 = (bf16[192,2304]{1,0:T(8,128)(2,1)}, bf16[192,2304]{1,0:T(8,128)(2,1)}, u32[]{:S(2)}, u32[]{:S(2)}) collective-permute-start(bf16[192,2304]{1,0:T(8,128)(2,1)} %collective-permute-done.4), channel_id=1, source_target_pairs={{0,4},{2,6},{4,0},{6,2},{8,12},{10,14},{12,8},{14,10},{16,20},{18,... | collective-permute-start | bytes 2654216 | tf_op jit(solution)/shard_map/ppermute | solution.py:41
  93.5 38.0 %collective-permute-start.12 = (bf16[2,1,288,384]{3,2,1,0:T(8,128)(2,1)S(1)}, bf16[2,1,288,384]{3,2,1,0:T(8,128)(2,1)S(1)}, u32[]{:S(2)}, u32[]{:S(2)}) collective-permute-start(bf16[2,1,288,384]{3,2,1,0:T(8,128)(2,1)S(1)} %pad_maximum_fusion.13), channel_id=1, source_target_pairs={{0,16},{2,18},{4,20},{6,22},{8,24},{10,26},{12,28},{14,30},{16,0},... | collective-permute-start | bytes 1327112 | tf_op jit(solution)/shard_map/ppermute | solution.py:41
  93.6 37.9 %collective-permute-start.11 = (bf16[2,1,288,384]{3,2,1,0:T(8,128)(2,1)S(1)}, bf16[2,1,288,384]{3,2,1,0:T(8,128)(2,1)S(1)}, u32[]{:S(2)}, u32[]{:S(2)}) collective-permute-start(bf16[2,1,288,384]{3,2,1,0:T(8,128)(2,1)S(1)} %pad_maximum_fusion.12), channel_id=1, source_target_pairs={{0,8},{2,10},{4,12},{6,14},{8,0},{10,2},{12,4},{14,6},{16,24},{18,... | collective-permute-start | bytes 1327112 | tf_op jit(solution)/shard_map/ppermute | solution.py:41
  94.6 43.1 %collective-permute-start.14 = (bf16[2,1,288,384]{3,2,1,0:T(8,128)(2,1)S(1)}, bf16[2,1,288,384]{3,2,1,0:T(8,128)(2,1)S(1)}, u32[]{:S(2)}, u32[]{:S(2)}) collective-permute-start(bf16[2,1,288,384]{3,2,1,0:T(8,128)(2,1)S(1)} %pad_maximum_fusion.11.refs_5_), channel_id=1, source_target_pairs={{0,4},{2,6},{4,0},{6,2},{8,12},{10,14},{12,8},{14,10},{16,20},{18,... | collective-permute-start | bytes 1327112 | tf_op jit(solution)/shard_map/ppermute | solution.py:41
  135.6 21.1 %collective-permute-start.16 = (bf16[2,1,288,384]{3,2,1,0:T(8,128)(2,1)S(1)}, bf16[2,1,288,384]{3,2,1,0:T(8,128)(2,1)S(1)}, u32[]{:S(2)}, u32[]{:S(2)}) collective-permute-start(bf16[2,1,288,384]{3,2,1,0:T(8,128)(2,1)S(1)} %collective-permute-done.12.refs_7_), channel_id=1, source_target_pairs={{0,4},{2,6},{4,0},{6,2},{8,12},{10,14},{12,8},{14,10},{16,20},{18,... | collective-permute-start | bytes 1327112 | tf_op jit(solution)/shard_map/ppermute | solution.py:41
  136.1 28.0 %collective-permute-start.15 = (bf16[2,1,288,384]{3,2,1,0:T(8,128)(2,1)S(1)}, bf16[2,1,288,384]{3,2,1,0:T(8,128)(2,1)S(1)}, u32[]{:S(2)}, u32[]{:S(2)}) collective-permute-start(bf16[2,1,288,384]{3,2,1,0:T(8,128)(2,1)S(1)} %collective-permute-done.11.refs_6_), channel_id=1, source_target_pairs={{0,4},{2,6},{4,0},{6,2},{8,12},{10,14},{12,8},{14,10},{16,20},{18,... | collective-permute-start | bytes 1327112 | tf_op jit(solution)/shard_map/ppermute | solution.py:41
  222.4 166.5 %all-gather.6.cloned.1.call-start = ((), (), s32[]{:S(2)}) async-start(), calls=%async_computation.7 | async-start | bytes 7864320 | tf_op jit(solution)/shard_map/all_gather | solution.py:1243
  233.3 19.9 %collective-permute-start.26 = (bf16[256,1536]{1,0:T(8,128)(2,1)}, bf16[256,1536]{1,0:T(8,128)(2,1)}, u32[]{:S(2)}, u32[]{:S(2)}) collective-permute-start(bf16[256,1536]{1,0:T(8,128)(2,1)} %bitcast.46), channel_id=1, source_target_pairs={{0,1},{1,0},{2,3},{3,2},{4,5},{5,4},{6,7},{7,6},{8,9},{9,8},{10,11... | collective-permute-start | bytes 2359304 | tf_op jit(solution)/shard_map/ppermute | solution.py:41
  235.4 431.7 %reduce-scatter.3.cloned.1.call-start = ((), (), s32[]{:S(2)}) async-start(), calls=%async_computation.5 | async-start | bytes 20054016 | tf_op jit(solution)/shard_map/reduce_scatter | solution.py:1301
  257.7 18.8 %collective-permute-start.31 = (bf16[256,1536]{1,0:T(8,128)(2,1)S(1)}, bf16[256,1536]{1,0:T(8,128)(2,1)S(1)}, u32[]{:S(2)}, u32[]{:S(2)}) collective-permute-start(bf16[256,1536]{1,0:T(8,128)(2,1)S(1)} %fusion.50.refs_0_), channel_id=1, source_target_pairs={{0,1},{1,0},{2,3},{3,2},{4,5},{5,4},{6,7},{7,6},{8,9},{9,8},{10,11... | collective-permute-start | bytes 2359304 | tf_op jit(solution)/shard_map/ppermute | solution.py:41
  284.3 18.1 %collective-permute-start.32 = (bf16[256,1536]{1,0:T(8,128)(2,1)}, bf16[256,1536]{1,0:T(8,128)(2,1)}, u32[]{:S(2)}, u32[]{:S(2)}) collective-permute-start(bf16[256,1536]{1,0:T(8,128)(2,1)} %convolution_convert_fusion), channel_id=1, source_target_pairs={{0,1},{1,0},{2,3},{3,2},{4,5},{5,4},{6,7},{7,6},{8,9},{9,8},{10,11... | collective-permute-start | bytes 2359304 | tf_op jit(solution)/shard_map/ppermute | solution.py:41
  334.7 25.1 %collective-permute-start.34 = (bf16[256,1536]{1,0:T(8,128)(2,1)}, bf16[256,1536]{1,0:T(8,128)(2,1)}, u32[]{:S(2)}, u32[]{:S(2)}) collective-permute-start(bf16[256,1536]{1,0:T(8,128)(2,1)} %fusion.30), channel_id=1, source_target_pairs={{0,1},{1,0},{2,3},{3,2},{4,5},{5,4},{6,7},{7,6},{8,9},{9,8},{10,11... | collective-permute-start | bytes 2359304 | tf_op jit(solution)/shard_map/ppermute | solution.py:41
  359.8 407.8 %reduce-scatter.5.cloned.1.call-start = ((), (), s32[]{:S(2)}) async-start(), calls=%async_computation.6 | async-start | bytes 2506752 | tf_op jit(solution)/shard_map/reduce_scatter | solution.py:1301
  398.5 20.1 %collective-permute-start.39 = (bf16[2,1,128,384]{3,2,1,0:T(8,128)(2,1)S(1)}, bf16[2,1,128,384]{3,2,1,0:T(8,128)(2,1)}, u32[]{:S(2)}, u32[]{:S(2)}) collective-permute-start(bf16[2,1,128,384]{3,2,1,0:T(8,128)(2,1)S(1)} %pad_maximum_fusion.25), channel_id=1, source_target_pairs={{0,16},{2,18},{4,20},{6,22},{8,24},{10,26},{12,28},{14,30},{16,0},... | collective-permute-start | bytes 589832 | tf_op jit(solution)/shard_map/ppermute | solution.py:41
  486.5 20.7 %collective-permute-start.43 = (bf16[2,1,288,384]{3,2,1,0:T(8,128)(2,1)S(1)}, bf16[2,1,288,384]{3,2,1,0:T(8,128)(2,1)S(1)}, u32[]{:S(2)}, u32[]{:S(2)}) collective-permute-start(bf16[2,1,288,384]{3,2,1,0:T(8,128)(2,1)S(1)} %copy-done.126), channel_id=1, source_target_pairs={{0,4},{2,6},{4,0},{6,2},{8,12},{10,14},{12,8},{14,10},{16,20},{18,... | collective-permute-start | bytes 1327112 | tf_op jit(solution)/shard_map/ppermute | solution.py:41
  490.0 36.1 %collective-permute-start.42 = (bf16[2,1,288,384]{3,2,1,0:T(8,128)(2,1)S(1)}, bf16[2,1,288,384]{3,2,1,0:T(8,128)(2,1)S(1)}, u32[]{:S(2)}, u32[]{:S(2)}) collective-permute-start(bf16[2,1,288,384]{3,2,1,0:T(8,128)(2,1)S(1)} %copy-done.125), channel_id=1, source_target_pairs={{0,4},{2,6},{4,0},{6,2},{8,12},{10,14},{12,8},{14,10},{16,20},{18,... | collective-permute-start | bytes 1327112 | tf_op jit(solution)/shard_map/ppermute | solution.py:41
  490.1 50.0 %collective-permute-start.41 = (bf16[2,1,288,384]{3,2,1,0:T(8,128)(2,1)S(1)}, bf16[2,1,288,384]{3,2,1,0:T(8,128)(2,1)S(1)}, u32[]{:S(2)}, u32[]{:S(2)}) collective-permute-start(bf16[2,1,288,384]{3,2,1,0:T(8,128)(2,1)S(1)} %copy-done.124), channel_id=1, source_target_pairs={{0,4},{2,6},{4,0},{6,2},{8,12},{10,14},{12,8},{14,10},{16,20},{18,... | collective-permute-start | bytes 1327112 | tf_op jit(solution)/shard_map/ppermute | solution.py:41
  564.3 34.0 %collective-permute-start.48 = (bf16[2,1,144,1152]{3,2,1,0:T(8,128)(2,1)}, bf16[2,1,144,1152]{3,2,1,0:T(8,128)(2,1)S(1)}, u32[]{:S(2)}, u32[]{:S(2)}) collective-permute-start(bf16[2,1,144,1152]{3,2,1,0:T(8,128)(2,1)} %get-tuple-element.139), channel_id=1, source_target_pairs={{0,24},{2,26},{4,28},{6,30},{8,16},{10,18},{12,20},{14,22},{16,8},... | collective-permute-start | bytes 1990664 | tf_op jit(solution)/shard_map/ppermute | solution.py:41
  566.5 90.8 %collective-permute-start.47 = (bf16[2,1,144,1152]{3,2,1,0:T(8,128)(2,1)}, bf16[2,1,144,1152]{3,2,1,0:T(8,128)(2,1)S(1)}, u32[]{:S(2)}, u32[]{:S(2)}) collective-permute-start(bf16[2,1,144,1152]{3,2,1,0:T(8,128)(2,1)} %get-tuple-element.137), channel_id=1, source_target_pairs={{0,16},{2,18},{4,20},{6,22},{8,24},{10,26},{12,28},{14,30},{16,0},... | collective-permute-start | bytes 1990664 | tf_op jit(solution)/shard_map/ppermute | solution.py:41
  566.5 90.8 %collective-permute-start.46 = (bf16[2,1,144,1152]{3,2,1,0:T(8,128)(2,1)}, bf16[2,1,144,1152]{3,2,1,0:T(8,128)(2,1)S(1)}, u32[]{:S(2)}, u32[]{:S(2)}) collective-permute-start(bf16[2,1,144,1152]{3,2,1,0:T(8,128)(2,1)} %get-tuple-element.135), channel_id=1, source_target_pairs={{0,8},{2,10},{4,12},{6,14},{8,0},{10,2},{12,4},{14,6},{16,24},{18,... | collective-permute-start | bytes 1990664 | tf_op jit(solution)/shard_map/ppermute | solution.py:41
  573.0 86.8 %collective-permute-start.50 = (bf16[2,1,192,576]{3,2,1,0:T(8,128)(2,1)}, bf16[2,1,192,576]{3,2,1,0:T(8,128)(2,1)}, u32[]{:S(2)}, u32[]{:S(2)}) collective-permute-start(bf16[2,1,192,576]{3,2,1,0:T(8,128)(2,1)} %constant_dynamic-slice_fusion.24), channel_id=1, source_target_pairs={{0,4},{2,6},{4,0},{6,2},{8,12},{10,14},{12,8},{14,10},{16,20},{18,... | collective-permute-start | bytes 1327112 | tf_op jit(solution)/shard_map/ppermute | solution.py:41
  663.8 18.0 %collective-permute-start.52 = (bf16[192,576]{0,1:T(8,128)(2,1)}, bf16[192,576]{0,1:T(8,128)(2,1)}, u32[]{:S(2)}, u32[]{:S(2)}) collective-permute-start(bf16[192,576]{0,1:T(8,128)(2,1)} %bitcast.425), channel_id=1, source_target_pairs={{0,1},{1,0},{2,3},{3,2},{4,5},{5,4},{6,7},{7,6},{8,9},{9,8},{10,11... | collective-permute-start | bytes 663560 | tf_op jit(solution)/shard_map/ppermute | solution.py:41
  683.5 30.7 %collective-permute-start.51 = (bf16[256,1536]{1,0:T(8,128)(2,1)S(1)}, bf16[256,1536]{1,0:T(8,128)(2,1)}, u32[]{:S(2)}, u32[]{:S(2)}) collective-permute-start(bf16[256,1536]{1,0:T(8,128)(2,1)S(1)} %bitcast.400), channel_id=1, source_target_pairs={{0,1},{1,0},{2,3},{3,2},{4,5},{5,4},{6,7},{7,6},{8,9},{9,8},{10,11... | collective-permute-start | bytes 2359304 | tf_op jit(solution)/shard_map/ppermute | solution.py:41
  684.9 22.7 %collective-permute-start.60 = (bf16[2,32,2,768]{3,1,2,0:T(8,128)(2,1)}, bf16[2,32,2,768]{3,1,2,0:T(8,128)(2,1)}, u32[]{:S(2)}, u32[]{:S(2)}) collective-permute-start(bf16[2,32,2,768]{3,1,2,0:T(8,128)(2,1)} %bitcast.387), channel_id=1, source_target_pairs={{0,1},{1,0},{2,3},{3,2},{4,5},{5,4},{6,7},{7,6},{8,9},{9,8},{10,11... | collective-permute-start | bytes 589832 | tf_op jit(solution)/shard_map/ppermute | solution.py:41
  721.7 27.6 %collective-permute-start.57 = (bf16[192,288]{1,0:T(8,128)(2,1)S(1)}, bf16[192,288]{1,0:T(8,128)(2,1)S(1)}, u32[]{:S(2)}, u32[]{:S(2)}) collective-permute-start(bf16[192,288]{1,0:T(8,128)(2,1)S(1)} %bitcast.432), channel_id=1, source_target_pairs={{0,2},{2,0},{4,6},{6,4},{8,10},{10,8},{12,14},{14,12},{16,18},{18,... | collective-permute-start | bytes 331784 | tf_op jit(solution)/shard_map/ppermute | solution.py:41
  722.4 26.9 %collective-permute-start.58 = (bf16[192,288]{1,0:T(8,128)(2,1)S(1)}, bf16[192,288]{1,0:T(8,128)(2,1)S(1)}, u32[]{:S(2)}, u32[]{:S(2)}) collective-permute-start(bf16[192,288]{1,0:T(8,128)(2,1)S(1)} %bitcast.433), channel_id=1, source_target_pairs={{0,4},{2,6},{4,0},{6,2},{8,12},{10,14},{12,8},{14,10},{16,20},{18,... | collective-permute-start | bytes 331784 | tf_op jit(solution)/shard_map/ppermute | solution.py:41
  724.1 25.2 %collective-permute-start.59 = (bf16[192,288]{1,0:T(8,128)(2,1)S(1)}, bf16[192,288]{1,0:T(8,128)(2,1)S(1)}, u32[]{:S(2)}, u32[]{:S(2)}) collective-permute-start(bf16[192,288]{1,0:T(8,128)(2,1)S(1)} %bitcast.434), channel_id=1, source_target_pairs={{0,6},{2,4},{4,2},{6,0},{8,14},{10,12},{12,10},{14,8},{16,22},{18,... | collective-permute-start | bytes 331784 | tf_op jit(solution)/shard_map/ppermute | solution.py:41
  736.8 26.5 %all-to-all-start.1 = ((bf16[16,64,192]{2,1,0:T(8,128)(2,1)}), bf16[16,64,192]{2,1,0:T(8,128)(2,1)S(1)}, u32[]{:S(2)}, u32[]{:S(2)}) async-start(bf16[16,64,192]{2,1,0:T(8,128)(2,1)} %copy.157), calls=%async_computation.2 | async-start | bytes 1048576 | tf_op jit(solution)/shard_map/all_to_all | solution.py:1451
  (191 other events, 2895.3 us)
Sparse Core Ops, SparseCore 0:
  222.5 50.2 all-gather.3
  274.3 113.8 all-gather.5
  392.4 255.6 reduce-scatter.2
  684.3 65.2 reduce-scatter.4
